TPU v7x, 768 devices: a whole 4x8x12 slice. The times are simulated.
768 devices in a mesh: replica: 96 (over x, y, z_lo), fsdp: 8 (over z_hi, core).
Axes of the slice: x: 4, y: 8, z: 12 (z_hi: 4, z_lo: 3; z = z_hi * 3 + z_lo), core: 2. Of those that a mesh axis runs over, the one named last changes fastest.
Arguments:
- weights: bfloat16 [96, 4096, 512], P('replica', 'fsdp'), may hold values from -6 to 6
- pseudo_grad: bfloat16 [96, 4096, 512], P('replica', 'fsdp'), may hold values from -6 to 6
- momentum: bfloat16 [96, 4096, 512], P('replica', 'fsdp'), may hold values from -6 to 6
- partner: int32 [96], replicated, may hold values from 0 to 95, as said below
- activations: bfloat16 [98304, 4096], P('replica', 'fsdp'), may hold values from -6 to 6
- key_cotangent: bfloat16 [98304, 512], P(('replica', 'fsdp')), may hold values from -0.1875 to 0.1875
Outputs:
- new_weights: bfloat16 [96, 4096, 512], P('replica', 'fsdp')
- new_momentum: bfloat16 [96, 4096, 512], P('replica', 'fsdp')
- weight_grad: bfloat16 [96, 4096, 512], P('replica', 'fsdp')
Inputs may be any that keep to these rules, and one draw needn't show every extreme that they name: partner is a matching: partner[partner[r]] = r and partner[r] != r for every replica r.
All inputs are finite; a program needn't handle non-finite values.
Results may differ from a plain program's by a relative error of at most 0.001.
Values may be sent and summed in bfloat16 or wider, within the bound.
No kernel may reach another device: no remote copies, remote signals or barrier semaphores. Data moves between devices by JAX's collectives and lax.ppermute only.
A program may use at most 32 MiB of HBM per device.

v0:
```python
import jax
import jax.numpy as jnp
from jax import lax
from jax.sharding import PartitionSpec as P

BLOCKS = 16


decay_old = 0.5
grad_rate = 0.7
pull_rate = 0.9


def on_device(weights, pseudo_grad, momentum, partner, activations, key_cotangent):
    peer_count = lax.axis_size("replica")
    row_count = weights.shape[1]
    col_count = weights.shape[2]
    block_count = BLOCKS
    per_block = row_count * col_count // block_count
    joint_len = 2 * per_block
    piece_len = (joint_len + peer_count * 128 - 1) // (peer_count * 128) * 128
    padded_len = piece_len * peer_count
    joined = jnp.concatenate(
        [
            weights[0].reshape(block_count, per_block),
            pseudo_grad[0].reshape(block_count, per_block),
        ],
        axis=1,
    )
    joined = jnp.pad(joined, ((0, 0), (0, padded_len - joint_len)))
    stacked = joined.reshape(block_count, peer_count, piece_len)

    def relay_step(state_val, block_data):
        holder_data = lax.all_to_all(block_data, "replica", split_axis=0, concat_axis=0, tiled=True)
        routed = jnp.take(holder_data, partner, axis=0)
        return (
            state_val,
            lax.all_to_all(routed, "replica", split_axis=0, concat_axis=0, tiled=True),
        )

    arrived = lax.scan(relay_step, jnp.int32(0), stacked)[1]
    arrived = arrived.reshape(block_count, padded_len)
    partner_weights = arrived[:, :per_block].reshape(row_count, col_count)
    partner_grad = arrived[:, per_block:joint_len].reshape(row_count, col_count)
    weights_f32 = weights[0].astype(jnp.float32)
    mean_weights = (weights_f32 + partner_weights.astype(jnp.float32)) * 0.5
    mean_grad = (pseudo_grad[0].astype(jnp.float32) + partner_grad.astype(jnp.float32)) * 0.5
    momentum_f = (
        decay_old * momentum[0].astype(jnp.float32)
        - grad_rate * mean_grad
        - pull_rate * (weights_f32 - mean_weights)
    )
    new_weights = (weights_f32 + decay_old * momentum_f - grad_rate * mean_grad).astype(
        jnp.bfloat16
    )
    new_momentum = momentum_f.astype(jnp.bfloat16)
    contract = (((0,), (0,)), ((), ()))
    gathered = lax.all_gather(key_cotangent, "fsdp", axis=0, tiled=True)
    grad_f32 = lax.dot_general(activations, gathered, contract, preferred_element_type=jnp.float32)
    weight_grad = grad_f32.astype(jnp.bfloat16)
    return (new_weights[None], new_momentum[None], weight_grad[None])


def solution(mesh):
    return jax.shard_map(
        on_device,
        mesh=mesh,
        in_specs=(
            P("replica", "fsdp", None),
            P("replica", "fsdp", None),
            P("replica", "fsdp", None),
            P(),
            P("replica", "fsdp"),
            P(("replica", "fsdp"), None),
        ),
        out_specs=(
            P("replica", "fsdp", None),
            P("replica", "fsdp", None),
            P("replica", "fsdp", None),
        ),
        check_vma=False,
    )
```

profile of v0, /device:TPU:192, one launch (start us, length us, event | category | flops | bytes accessed | tf_op | source)
XLA Modules:
  0.0 724.7 jit_solution(12733178745124629719)
XLA Ops:
  10.2 697.2 %while.10 = (s32[]{:T(128)}, bf16[16,96,384]{2,1,0:T(8,128)(2,1)}, s32[96]{0:T(128)S(1)}, bf16[16,96,384]{2,1,0:T(8,128)(2,1)S(1)}, s32[]{:T(128)}, /*index=5*/bf16[]{:T(256)}, bf16[]{:T(256)}) while((s32[]{:T(128)}, bf16[16,96,384]{2,1,0:T(8,128)(2,1)}, s32[96]{0:T(128)S(1)}, bf16[16,96,384]{2,1,0:T(8,128)(2,1)S(1)}, s32[]{:T(128)}, ...), condition=%wide.region_1.2_spmd, body=%wide.region_0.1_spmd.sunk | while | flops 38754 | bytes 2169065 | solution.py:41
  12.2 16.0 %all-to-all-start = ((bf16[96,2,192]{2,1,0:T(2,128)(2,1)}), bf16[96,2,192]{2,1,0:T(2,128)(2,1)S(1)}, u32[]{:S(2)}, u32[]{:S(2)}) async-start(bf16[96,2,192]{2,1,0:T(2,128)(2,1)} %reshape.113), calls=%async_computation | async-start | bytes 196608 | tf_op jit(solution)/shard_map/while/body/eval_jaxpr/all_to_all | solution.py:34
  28.2 12.6 %all-to-all-done = bf16[96,2,192]{2,1,0:T(2,128)(2,1)S(1)} async-done(((bf16[96,2,192]{2,1,0:T(2,128)(2,1)}), bf16[96,2,192]{2,1,0:T(2,128)(2,1)S(1)}, u32[]{:S(2)}, u32[]{:S(2)}) %all-to-all-start) | async-done | bytes 73760 | tf_op jit(solution)/shard_map/while/body/eval_jaxpr/all_to_all | solution.py:34
  49.8 12.6 %all-to-all-done.1 = bf16[96,2,192]{2,1,0:T(2,128)(2,1)S(1)} async-done(((bf16[96,2,192]{2,1,0:T(2,128)(2,1)}), bf16[96,2,192]{2,1,0:T(2,128)(2,1)S(1)}, u32[]{:S(2)}, u32[]{:S(2)}) %all-to-all-start.1) | async-done | bytes 73760 | tf_op jit(solution)/shard_map/while/body/eval_jaxpr/all_to_all | solution.py:38
  71.1 12.6 %all-to-all-done = bf16[96,2,192]{2,1,0:T(2,128)(2,1)S(1)} async-done(((bf16[96,2,192]{2,1,0:T(2,128)(2,1)}), bf16[96,2,192]{2,1,0:T(2,128)(2,1)S(1)}, u32[]{:S(2)}, u32[]{:S(2)}) %all-to-all-start) | async-done | bytes 73760 | tf_op jit(solution)/shard_map/while/body/eval_jaxpr/all_to_all | solution.py:34
  92.7 12.6 %all-to-all-done.1 = bf16[96,2,192]{2,1,0:T(2,128)(2,1)S(1)} async-done(((bf16[96,2,192]{2,1,0:T(2,128)(2,1)}), bf16[96,2,192]{2,1,0:T(2,128)(2,1)S(1)}, u32[]{:S(2)}, u32[]{:S(2)}) %all-to-all-start.1) | async-done | bytes 73760 | tf_op jit(solution)/shard_map/while/body/eval_jaxpr/all_to_all | solution.py:38
  135.6 12.6 %all-to-all-done.1 = bf16[96,2,192]{2,1,0:T(2,128)(2,1)S(1)} async-done(((bf16[96,2,192]{2,1,0:T(2,128)(2,1)}), bf16[96,2,192]{2,1,0:T(2,128)(2,1)S(1)}, u32[]{:S(2)}, u32[]{:S(2)}) %all-to-all-start.1) | async-done | bytes 73760 | tf_op jit(solution)/shard_map/while/body/eval_jaxpr/all_to_all | solution.py:38
  178.5 12.6 %all-to-all-done.1 = bf16[96,2,192]{2,1,0:T(2,128)(2,1)S(1)} async-done(((bf16[96,2,192]{2,1,0:T(2,128)(2,1)}), bf16[96,2,192]{2,1,0:T(2,128)(2,1)S(1)}, u32[]{:S(2)}, u32[]{:S(2)}) %all-to-all-start.1) | async-done | bytes 73760 | tf_op jit(solution)/shard_map/while/body/eval_jaxpr/all_to_all | solution.py:38
  221.4 12.6 %all-to-all-done.1 = bf16[96,2,192]{2,1,0:T(2,128)(2,1)S(1)} async-done(((bf16[96,2,192]{2,1,0:T(2,128)(2,1)}), bf16[96,2,192]{2,1,0:T(2,128)(2,1)S(1)}, u32[]{:S(2)}, u32[]{:S(2)}) %all-to-all-start.1) | async-done | bytes 73760 | tf_op jit(solution)/shard_map/while/body/eval_jaxpr/all_to_all | solution.py:38
  264.4 12.6 %all-to-all-done.1 = bf16[96,2,192]{2,1,0:T(2,128)(2,1)S(1)} async-done(((bf16[96,2,192]{2,1,0:T(2,128)(2,1)}), bf16[96,2,192]{2,1,0:T(2,128)(2,1)S(1)}, u32[]{:S(2)}, u32[]{:S(2)}) %all-to-all-start.1) | async-done | bytes 73760 | tf_op jit(solution)/shard_map/while/body/eval_jaxpr/all_to_all | solution.py:38
  307.3 12.6 %all-to-all-done.1 = bf16[96,2,192]{2,1,0:T(2,128)(2,1)S(1)} async-done(((bf16[96,2,192]{2,1,0:T(2,128)(2,1)}), bf16[96,2,192]{2,1,0:T(2,128)(2,1)S(1)}, u32[]{:S(2)}, u32[]{:S(2)}) %all-to-all-start.1) | async-done | bytes 73760 | tf_op jit(solution)/shard_map/while/body/eval_jaxpr/all_to_all | solution.py:38
  350.2 12.6 %all-to-all-done.1 = bf16[96,2,192]{2,1,0:T(2,128)(2,1)S(1)} async-done(((bf16[96,2,192]{2,1,0:T(2,128)(2,1)}), bf16[96,2,192]{2,1,0:T(2,128)(2,1)S(1)}, u32[]{:S(2)}, u32[]{:S(2)}) %all-to-all-start.1) | async-done | bytes 73760 | tf_op jit(solution)/shard_map/while/body/eval_jaxpr/all_to_all | solution.py:38
  393.1 13.1 %all-to-all-done.1 = bf16[96,2,192]{2,1,0:T(2,128)(2,1)S(1)} async-done(((bf16[96,2,192]{2,1,0:T(2,128)(2,1)}), bf16[96,2,192]{2,1,0:T(2,128)(2,1)S(1)}, u32[]{:S(2)}, u32[]{:S(2)}) %all-to-all-start.1) | async-done | bytes 73760 | tf_op jit(solution)/shard_map/while/body/eval_jaxpr/all_to_all | solution.py:38
  414.9 12.7 %all-to-all-done = bf16[96,2,192]{2,1,0:T(2,128)(2,1)S(1)} async-done(((bf16[96,2,192]{2,1,0:T(2,128)(2,1)}), bf16[96,2,192]{2,1,0:T(2,128)(2,1)S(1)}, u32[]{:S(2)}, u32[]{:S(2)}) %all-to-all-start) | async-done | bytes 73760 | tf_op jit(solution)/shard_map/while/body/eval_jaxpr/all_to_all | solution.py:34
  436.5 12.6 %all-to-all-done.1 = bf16[96,2,192]{2,1,0:T(2,128)(2,1)S(1)} async-done(((bf16[96,2,192]{2,1,0:T(2,128)(2,1)}), bf16[96,2,192]{2,1,0:T(2,128)(2,1)S(1)}, u32[]{:S(2)}, u32[]{:S(2)}) %all-to-all-start.1) | async-done | bytes 73760 | tf_op jit(solution)/shard_map/while/body/eval_jaxpr/all_to_all | solution.py:38
  479.4 12.6 %all-to-all-done.1 = bf16[96,2,192]{2,1,0:T(2,128)(2,1)S(1)} async-done(((bf16[96,2,192]{2,1,0:T(2,128)(2,1)}), bf16[96,2,192]{2,1,0:T(2,128)(2,1)S(1)}, u32[]{:S(2)}, u32[]{:S(2)}) %all-to-all-start.1) | async-done | bytes 73760 | tf_op jit(solution)/shard_map/while/body/eval_jaxpr/all_to_all | solution.py:38
  500.8 12.6 %all-to-all-done = bf16[96,2,192]{2,1,0:T(2,128)(2,1)S(1)} async-done(((bf16[96,2,192]{2,1,0:T(2,128)(2,1)}), bf16[96,2,192]{2,1,0:T(2,128)(2,1)S(1)}, u32[]{:S(2)}, u32[]{:S(2)}) %all-to-all-start) | async-done | bytes 73760 | tf_op jit(solution)/shard_map/while/body/eval_jaxpr/all_to_all | solution.py:34
  522.3 12.6 %all-to-all-done.1 = bf16[96,2,192]{2,1,0:T(2,128)(2,1)S(1)} async-done(((bf16[96,2,192]{2,1,0:T(2,128)(2,1)}), bf16[96,2,192]{2,1,0:T(2,128)(2,1)S(1)}, u32[]{:S(2)}, u32[]{:S(2)}) %all-to-all-start.1) | async-done | bytes 73760 | tf_op jit(solution)/shard_map/while/body/eval_jaxpr/all_to_all | solution.py:38
  543.7 12.6 %all-to-all-done = bf16[96,2,192]{2,1,0:T(2,128)(2,1)S(1)} async-done(((bf16[96,2,192]{2,1,0:T(2,128)(2,1)}), bf16[96,2,192]{2,1,0:T(2,128)(2,1)S(1)}, u32[]{:S(2)}, u32[]{:S(2)}) %all-to-all-start) | async-done | bytes 73760 | tf_op jit(solution)/shard_map/while/body/eval_jaxpr/all_to_all | solution.py:34
  565.3 12.6 %all-to-all-done.1 = bf16[96,2,192]{2,1,0:T(2,128)(2,1)S(1)} async-done(((bf16[96,2,192]{2,1,0:T(2,128)(2,1)}), bf16[96,2,192]{2,1,0:T(2,128)(2,1)S(1)}, u32[]{:S(2)}, u32[]{:S(2)}) %all-to-all-start.1) | async-done | bytes 73760 | tf_op jit(solution)/shard_map/while/body/eval_jaxpr/all_to_all | solution.py:38
  608.2 12.6 %all-to-all-done.1 = bf16[96,2,192]{2,1,0:T(2,128)(2,1)S(1)} async-done(((bf16[96,2,192]{2,1,0:T(2,128)(2,1)}), bf16[96,2,192]{2,1,0:T(2,128)(2,1)S(1)}, u32[]{:S(2)}, u32[]{:S(2)}) %all-to-all-start.1) | async-done | bytes 73760 | tf_op jit(solution)/shard_map/while/body/eval_jaxpr/all_to_all | solution.py:38
  629.5 12.6 %all-to-all-done = bf16[96,2,192]{2,1,0:T(2,128)(2,1)S(1)} async-done(((bf16[96,2,192]{2,1,0:T(2,128)(2,1)}), bf16[96,2,192]{2,1,0:T(2,128)(2,1)S(1)}, u32[]{:S(2)}, u32[]{:S(2)}) %all-to-all-start) | async-done | bytes 73760 | tf_op jit(solution)/shard_map/while/body/eval_jaxpr/all_to_all | solution.py:34
  651.1 12.6 %all-to-all-done.1 = bf16[96,2,192]{2,1,0:T(2,128)(2,1)S(1)} async-done(((bf16[96,2,192]{2,1,0:T(2,128)(2,1)}), bf16[96,2,192]{2,1,0:T(2,128)(2,1)S(1)}, u32[]{:S(2)}, u32[]{:S(2)}) %all-to-all-start.1) | async-done | bytes 73760 | tf_op jit(solution)/shard_map/while/body/eval_jaxpr/all_to_all | solution.py:38
  694.0 12.6 %all-to-all-done.1 = bf16[96,2,192]{2,1,0:T(2,128)(2,1)S(1)} async-done(((bf16[96,2,192]{2,1,0:T(2,128)(2,1)}), bf16[96,2,192]{2,1,0:T(2,128)(2,1)S(1)}, u32[]{:S(2)}, u32[]{:S(2)}) %all-to-all-start.1) | async-done | bytes 73760 | tf_op jit(solution)/shard_map/while/body/eval_jaxpr/all_to_all | solution.py:38
  (319 shorter events, 415.0 us)
Async XLA Ops:
  7.2 707.9 %all-gather.2.cloned.1.call-start = ((), (), s32[]{:S(2)}) async-start(), calls=%async_computation.2 | async-start | bytes 1179648 | tf_op jit(solution)/shard_map/all_gather | solution.py:58
  12.2 28.6 %all-to-all-start = ((bf16[96,2,192]{2,1,0:T(2,128)(2,1)}), bf16[96,2,192]{2,1,0:T(2,128)(2,1)S(1)}, u32[]{:S(2)}, u32[]{:S(2)}) async-start(bf16[96,2,192]{2,1,0:T(2,128)(2,1)} %reshape.113), calls=%async_computation | async-start | bytes 196608 | tf_op jit(solution)/shard_map/while/body/eval_jaxpr/all_to_all | solution.py:34
  43.8 18.6 %all-to-all-start.1 = ((bf16[96,2,192]{2,1,0:T(2,128)(2,1)}), bf16[96,2,192]{2,1,0:T(2,128)(2,1)S(1)}, u32[]{:S(2)}, u32[]{:S(2)}) async-start(bf16[96,2,192]{2,1,0:T(2,128)(2,1)} %reshape.115), calls=%async_computation.1 | async-start | bytes 196608 | tf_op jit(solution)/shard_map/while/body/eval_jaxpr/all_to_all | solution.py:38
  65.2 18.6 %all-to-all-start = ((bf16[96,2,192]{2,1,0:T(2,128)(2,1)}), bf16[96,2,192]{2,1,0:T(2,128)(2,1)S(1)}, u32[]{:S(2)}, u32[]{:S(2)}) async-start(bf16[96,2,192]{2,1,0:T(2,128)(2,1)} %reshape.113), calls=%async_computation | async-start | bytes 196608 | tf_op jit(solution)/shard_map/while/body/eval_jaxpr/all_to_all | solution.py:34
  86.7 18.6 %all-to-all-start.1 = ((bf16[96,2,192]{2,1,0:T(2,128)(2,1)}), bf16[96,2,192]{2,1,0:T(2,128)(2,1)S(1)}, u32[]{:S(2)}, u32[]{:S(2)}) async-start(bf16[96,2,192]{2,1,0:T(2,128)(2,1)} %reshape.115), calls=%async_computation.1 | async-start | bytes 196608 | tf_op jit(solution)/shard_map/while/body/eval_jaxpr/all_to_all | solution.py:38
  108.1 18.6 %all-to-all-start = ((bf16[96,2,192]{2,1,0:T(2,128)(2,1)}), bf16[96,2,192]{2,1,0:T(2,128)(2,1)S(1)}, u32[]{:S(2)}, u32[]{:S(2)}) async-start(bf16[96,2,192]{2,1,0:T(2,128)(2,1)} %reshape.113), calls=%async_computation | async-start | bytes 196608 | tf_op jit(solution)/shard_map/while/body/eval_jaxpr/all_to_all | solution.py:34
  129.6 18.6 %all-to-all-start.1 = ((bf16[96,2,192]{2,1,0:T(2,128)(2,1)}), bf16[96,2,192]{2,1,0:T(2,128)(2,1)S(1)}, u32[]{:S(2)}, u32[]{:S(2)}) async-start(bf16[96,2,192]{2,1,0:T(2,128)(2,1)} %reshape.115), calls=%async_computation.1 | async-start | bytes 196608 | tf_op jit(solution)/shard_map/while/body/eval_jaxpr/all_to_all | solution.py:38
  151.0 18.6 %all-to-all-start = ((bf16[96,2,192]{2,1,0:T(2,128)(2,1)}), bf16[96,2,192]{2,1,0:T(2,128)(2,1)S(1)}, u32[]{:S(2)}, u32[]{:S(2)}) async-start(bf16[96,2,192]{2,1,0:T(2,128)(2,1)} %reshape.113), calls=%async_computation | async-start | bytes 196608 | tf_op jit(solution)/shard_map/while/body/eval_jaxpr/all_to_all | solution.py:34
  172.6 18.6 %all-to-all-start.1 = ((bf16[96,2,192]{2,1,0:T(2,128)(2,1)}), bf16[96,2,192]{2,1,0:T(2,128)(2,1)S(1)}, u32[]{:S(2)}, u32[]{:S(2)}) async-start(bf16[96,2,192]{2,1,0:T(2,128)(2,1)} %reshape.115), calls=%async_computation.1 | async-start | bytes 196608 | tf_op jit(solution)/shard_map/while/body/eval_jaxpr/all_to_all | solution.py:38
  193.9 18.6 %all-to-all-start = ((bf16[96,2,192]{2,1,0:T(2,128)(2,1)}), bf16[96,2,192]{2,1,0:T(2,128)(2,1)S(1)}, u32[]{:S(2)}, u32[]{:S(2)}) async-start(bf16[96,2,192]{2,1,0:T(2,128)(2,1)} %reshape.113), calls=%async_computation | async-start | bytes 196608 | tf_op jit(solution)/shard_map/while/body/eval_jaxpr/all_to_all | solution.py:34
  236.8 18.6 %all-to-all-start = ((bf16[96,2,192]{2,1,0:T(2,128)(2,1)}), bf16[96,2,192]{2,1,0:T(2,128)(2,1)S(1)}, u32[]{:S(2)}, u32[]{:S(2)}) async-start(bf16[96,2,192]{2,1,0:T(2,128)(2,1)} %reshape.113), calls=%async_computation | async-start | bytes 196608 | tf_op jit(solution)/shard_map/while/body/eval_jaxpr/all_to_all | solution.py:34
  279.7 18.6 %all-to-all-start = ((bf16[96,2,192]{2,1,0:T(2,128)(2,1)}), bf16[96,2,192]{2,1,0:T(2,128)(2,1)S(1)}, u32[]{:S(2)}, u32[]{:S(2)}) async-start(bf16[96,2,192]{2,1,0:T(2,128)(2,1)} %reshape.113), calls=%async_computation | async-start | bytes 196608 | tf_op jit(solution)/shard_map/while/body/eval_jaxpr/all_to_all | solution.py:34
  301.3 18.6 %all-to-all-start.1 = ((bf16[96,2,192]{2,1,0:T(2,128)(2,1)}), bf16[96,2,192]{2,1,0:T(2,128)(2,1)S(1)}, u32[]{:S(2)}, u32[]{:S(2)}) async-start(bf16[96,2,192]{2,1,0:T(2,128)(2,1)} %reshape.115), calls=%async_computation.1 | async-start | bytes 196608 | tf_op jit(solution)/shard_map/while/body/eval_jaxpr/all_to_all | solution.py:38
  322.7 18.6 %all-to-all-start = ((bf16[96,2,192]{2,1,0:T(2,128)(2,1)}), bf16[96,2,192]{2,1,0:T(2,128)(2,1)S(1)}, u32[]{:S(2)}, u32[]{:S(2)}) async-start(bf16[96,2,192]{2,1,0:T(2,128)(2,1)} %reshape.113), calls=%async_computation | async-start | bytes 196608 | tf_op jit(solution)/shard_map/while/body/eval_jaxpr/all_to_all | solution.py:34
  387.1 19.0 %all-to-all-start.1 = ((bf16[96,2,192]{2,1,0:T(2,128)(2,1)}), bf16[96,2,192]{2,1,0:T(2,128)(2,1)S(1)}, u32[]{:S(2)}, u32[]{:S(2)}) async-start(bf16[96,2,192]{2,1,0:T(2,128)(2,1)} %reshape.115), calls=%async_computation.1 | async-start | bytes 196608 | tf_op jit(solution)/shard_map/while/body/eval_jaxpr/all_to_all | solution.py:38
  408.9 18.7 %all-to-all-start = ((bf16[96,2,192]{2,1,0:T(2,128)(2,1)}), bf16[96,2,192]{2,1,0:T(2,128)(2,1)S(1)}, u32[]{:S(2)}, u32[]{:S(2)}) async-start(bf16[96,2,192]{2,1,0:T(2,128)(2,1)} %reshape.113), calls=%async_computation | async-start | bytes 196608 | tf_op jit(solution)/shard_map/while/body/eval_jaxpr/all_to_all | solution.py:34
  451.9 18.6 %all-to-all-start = ((bf16[96,2,192]{2,1,0:T(2,128)(2,1)}), bf16[96,2,192]{2,1,0:T(2,128)(2,1)S(1)}, u32[]{:S(2)}, u32[]{:S(2)}) async-start(bf16[96,2,192]{2,1,0:T(2,128)(2,1)} %reshape.113), calls=%async_computation | async-start | bytes 196608 | tf_op jit(solution)/shard_map/while/body/eval_jaxpr/all_to_all | solution.py:34
  494.8 18.6 %all-to-all-start = ((bf16[96,2,192]{2,1,0:T(2,128)(2,1)}), bf16[96,2,192]{2,1,0:T(2,128)(2,1)S(1)}, u32[]{:S(2)}, u32[]{:S(2)}) async-start(bf16[96,2,192]{2,1,0:T(2,128)(2,1)} %reshape.113), calls=%async_computation | async-start | bytes 196608 | tf_op jit(solution)/shard_map/while/body/eval_jaxpr/all_to_all | solution.py:34
  516.4 18.6 %all-to-all-start.1 = ((bf16[96,2,192]{2,1,0:T(2,128)(2,1)}), bf16[96,2,192]{2,1,0:T(2,128)(2,1)S(1)}, u32[]{:S(2)}, u32[]{:S(2)}) async-start(bf16[96,2,192]{2,1,0:T(2,128)(2,1)} %reshape.115), calls=%async_computation.1 | async-start | bytes 196608 | tf_op jit(solution)/shard_map/while/body/eval_jaxpr/all_to_all | solution.py:38
  537.7 18.6 %all-to-all-start = ((bf16[96,2,192]{2,1,0:T(2,128)(2,1)}), bf16[96,2,192]{2,1,0:T(2,128)(2,1)S(1)}, u32[]{:S(2)}, u32[]{:S(2)}) async-start(bf16[96,2,192]{2,1,0:T(2,128)(2,1)} %reshape.113), calls=%async_computation | async-start | bytes 196608 | tf_op jit(solution)/shard_map/while/body/eval_jaxpr/all_to_all | solution.py:34
  580.6 18.6 %all-to-all-start = ((bf16[96,2,192]{2,1,0:T(2,128)(2,1)}), bf16[96,2,192]{2,1,0:T(2,128)(2,1)S(1)}, u32[]{:S(2)}, u32[]{:S(2)}) async-start(bf16[96,2,192]{2,1,0:T(2,128)(2,1)} %reshape.113), calls=%async_computation | async-start | bytes 196608 | tf_op jit(solution)/shard_map/while/body/eval_jaxpr/all_to_all | solution.py:34
  602.2 18.6 %all-to-all-start.1 = ((bf16[96,2,192]{2,1,0:T(2,128)(2,1)}), bf16[96,2,192]{2,1,0:T(2,128)(2,1)S(1)}, u32[]{:S(2)}, u32[]{:S(2)}) async-start(bf16[96,2,192]{2,1,0:T(2,128)(2,1)} %reshape.115), calls=%async_computation.1 | async-start | bytes 196608 | tf_op jit(solution)/shard_map/while/body/eval_jaxpr/all_to_all | solution.py:38
  623.6 18.6 %all-to-all-start = ((bf16[96,2,192]{2,1,0:T(2,128)(2,1)}), bf16[96,2,192]{2,1,0:T(2,128)(2,1)S(1)}, u32[]{:S(2)}, u32[]{:S(2)}) async-start(bf16[96,2,192]{2,1,0:T(2,128)(2,1)} %reshape.113), calls=%async_computation | async-start | bytes 196608 | tf_op jit(solution)/shard_map/while/body/eval_jaxpr/all_to_all | solution.py:34
  666.5 18.6 %all-to-all-start = ((bf16[96,2,192]{2,1,0:T(2,128)(2,1)}), bf16[96,2,192]{2,1,0:T(2,128)(2,1)S(1)}, u32[]{:S(2)}, u32[]{:S(2)}) async-start(bf16[96,2,192]{2,1,0:T(2,128)(2,1)} %reshape.113), calls=%async_computation | async-start | bytes 196608 | tf_op jit(solution)/shard_map/while/body/eval_jaxpr/all_to_all | solution.py:34
  (13 other events, 879.4 us)
Sparse Core Ops, SparseCore 0:
  10.5 44.5 all-gather.1
where the time goes:
time: 727 us; the launch traced here: 725 us
  waiting for transfers between devices  405 us (56%)
  starting transfers between devices  200 us (28%)
  local copies, waits for them, and re-layouts  75.2 us (10%)
  other arithmetic  26.2 us (4%)
  between operations  14.1 us (2%)
    all_to_all x16, waiting for transfers between devices, relay_step(): lax.all_to_all(routed, 'replica', split_axis=0, concat_axis=0, tiled=True)  203 us
    all_to_all x16, waiting for transfers between devices, relay_step(): lax.all_to_all(block_data, 'replica', split_axis=0, concat_axis=0, tiled=...  202 us
    all_to_all x16, starting transfers between devices, relay_step(): lax.all_to_all(block_data, 'replica', split_axis=0, concat_axis=0, tiled=...  105 us
    all_to_all x16, starting transfers between devices, relay_step(): lax.all_to_all(routed, 'replica', split_axis=0, concat_axis=0, tiled=True)  95 us
    while x80, local copies, waits for them, and re-layouts  29.2 us
  transfers between devices with their start and end apart: 33, of which 32 were waited for; matrix products, arithmetic and copies ran while one was open for 14% of the time, Pallas kernels for 0%

commit v1 on v0

v1 whole, which is shorter than its diff:
```python
import jax
import jax.numpy as jnp
from jax import lax
from jax.sharding import Mesh
from jax.sharding import PartitionSpec as P

LAYERS = 3
SLOTS = 18

decay_old = 0.5
grad_rate = 0.7
pull_rate = 0.9


def outer_step(weights, pseudo_grad, momentum, partner_weights, partner_grad):
    weights_f32 = weights.astype(jnp.float32)
    mean_weights = (weights_f32 + partner_weights.astype(jnp.float32)) * 0.5
    mean_grad = (pseudo_grad.astype(jnp.float32) + partner_grad.astype(jnp.float32)) * 0.5
    momentum_f = (
        decay_old * momentum.astype(jnp.float32)
        - grad_rate * mean_grad
        - pull_rate * (weights_f32 - mean_weights)
    )
    new_weights = weights_f32 + decay_old * momentum_f - grad_rate * mean_grad
    return new_weights.astype(jnp.bfloat16), momentum_f.astype(jnp.bfloat16)


def spread(array):
    columns = lax.axis_size("column")
    pieces = array.reshape(columns, array.shape[0] // columns, array.shape[1])
    return lax.all_to_all(pieces, "column", split_axis=0, concat_axis=0, tiled=True)


def deliver(pieces, send_index, take_index):
    crossed = lax.all_to_all(
        jnp.take(pieces, send_index, axis=0), "layer", split_axis=0, concat_axis=0, tiled=True
    )
    routed = jnp.take(crossed, take_index, axis=0)
    arrived = lax.all_to_all(routed, "column", split_axis=0, concat_axis=0, tiled=True)
    return arrived.reshape(-1, arrived.shape[-1])


def routes(target, rank, layer, slots):
    columns = target.shape[0]
    mine_to = jnp.take(target % LAYERS, layer, axis=1)
    mine_rank = jnp.take(rank, layer, axis=1)
    slot = mine_to * slots + mine_rank
    chosen = slot[None, :] == jnp.arange(LAYERS * slots, dtype=jnp.int32)[:, None]
    chosen = chosen & (mine_rank < slots)[None, :]
    send_index = jnp.sum(
        jnp.where(chosen, jnp.arange(columns, dtype=jnp.int32)[None, :], 0), axis=1
    )
    source = jnp.take(target, layer, axis=1)
    source_rank = jnp.take(rank.reshape(-1), source, axis=0)
    take_index = jnp.minimum(source % LAYERS * slots + source_rank, LAYERS * slots - 1)
    return send_index, take_index


def on_device(weights, pseudo_grad, momentum, partner, activations, key_cotangent):
    columns = lax.axis_size("column")
    layer = lax.axis_index("layer")
    weights, pseudo_grad, momentum = weights[0], pseudo_grad[0], momentum[0]

    target = partner.reshape(columns, LAYERS)
    to_layer = (target % LAYERS)[:, :, None] == jnp.arange(LAYERS, dtype=jnp.int32)
    before = jnp.tril(jnp.ones((columns, columns), jnp.int32), -1)
    earlier = jnp.sum(before[:, :, None, None] * to_layer[None].astype(jnp.int32), axis=1)
    rank = jnp.sum(jnp.where(to_layer, earlier, 0), axis=2)
    crowded = jnp.max(rank) >= SLOTS

    spread_weights = spread(weights)
    spread_grad = spread(pseudo_grad)
    send_index, take_index = routes(target, rank, layer, SLOTS)
    partner_weights = deliver(spread_weights, send_index, take_index)
    partner_grad = deliver(spread_grad, send_index, take_index)

    def as_arrived():
        return outer_step(weights, pseudo_grad, momentum, partner_weights, partner_grad)

    def again():
        index = routes(target, rank, layer, columns)
        return outer_step(
            weights,
            pseudo_grad,
            momentum,
            deliver(spread_weights, *index),
            deliver(spread_grad, *index),
        )

    new_weights, new_momentum = lax.cond(crowded, again, as_arrived)

    contract = (((0,), (0,)), ((), ()))
    gathered = lax.all_gather(key_cotangent, "fsdp", axis=0, tiled=True)
    grad_f32 = lax.dot_general(activations, gathered, contract, preferred_element_type=jnp.float32)
    weight_grad = grad_f32.astype(jnp.bfloat16)
    return (new_weights[None], new_momentum[None], weight_grad[None])


def solution(mesh):
    replicas, shards = mesh.devices.shape
    grid = Mesh(
        mesh.devices.reshape(replicas // LAYERS, LAYERS, shards), ("column", "layer", "fsdp")
    )
    replica = ("column", "layer")
    block = P(replica, "fsdp", None)
    return jax.shard_map(
        on_device,
        mesh=grid,
        in_specs=(
            block,
            block,
            block,
            P(),
            P(replica, "fsdp"),
            P(("column", "layer", "fsdp"), None),
        ),
        out_specs=(block, block, block),
        check_vma=False,
    )
```

time: 727 us -> 159 us (0.22)
  the two profiles are of different devices: /device:TPU:192 before, /device:TPU:200 now
where the time goes in v1:
time: 159 us; the launch traced here: 158 us
  waiting for transfers between devices  54.2 us (34%)
  blocking collectives  46.7 us (29%)
  starting transfers between devices  23.7 us (15%)
  between operations  14.9 us (9%)
  other arithmetic  8.67 us (5%)
  local copies, waits for them, and re-layouts  7.06 us (4%)
  matrix products  2.83 us (2%)
    all_to_all x2, waiting for transfers between devices, spread(): lax.all_to_all(pieces, 'column', split_axis=0, concat_axis=0, tiled=True)  32.3 us
    all_to_all x1, blocking collectives, deliver(): lax.all_to_all(routed, 'column', split_axis=0, concat_axis=0, tiled=True)  25.9 us
    all_to_all x1, blocking collectives, deliver(): lax.all_to_all(jnp.take(pieces, send_index, axis=0), 'layer', split_axis=...  20.8 us
    all_to_all x2, starting transfers between devices, spread(): lax.all_to_all(pieces, 'column', split_axis=0, concat_axis=0, tiled=True)  15.2 us
    all_to_all x1, waiting for transfers between devices, deliver(): lax.all_to_all(routed, 'column', split_axis=0, concat_axis=0, tiled=True)  12.6 us
    all_to_all x1, waiting for transfers between devices, deliver(): lax.all_to_all(jnp.take(pieces, send_index, axis=0), 'layer', split_axis=...  8.64 us
    all_to_all x1, starting transfers between devices, deliver(): lax.all_to_all(routed, 'column', split_axis=0, concat_axis=0, tiled=True)  4.92 us
    all_to_all x1, starting transfers between devices, deliver(): lax.all_to_all(jnp.take(pieces, send_index, axis=0), 'layer', split_axis=...  3.53 us
  transfers between devices with their start and end apart: 5, of which 4 were waited for; matrix products, arithmetic and copies ran while one was open for 7% of the time, Pallas kernels for 0%

profile of v1, /device:TPU:200, one launch (start us, length us, event | category | flops | bytes accessed | tf_op | source)
XLA Modules:
  0.0 158.0 jit_solution(8948418694871157525)
XLA Ops:
  7.2 10.3 %all-to-all-start.4 = ((bf16[32,16,512]{2,1,0:T(8,128)(2,1)}), bf16[32,16,512]{2,1,0:T(8,128)(2,1)S(1)}, u32[]{:S(2)}, u32[]{:S(2)}) async-start(bf16[32,16,512]{2,1,0:T(8,128)(2,1)} %bitcast.75), calls=%async_computation.4 | async-start | bytes 1048576 | tf_op jit(solution)/shard_map/all_to_all | solution.py:31
  17.5 0.8 reshape.92
  18.4 0.3 multiply_reduce_fusion
  18.7 16.4 %all-to-all-done.4 = bf16[32,16,512]{2,1,0:T(8,128)(2,1)S(1)} async-done(((bf16[32,16,512]{2,1,0:T(8,128)(2,1)}), bf16[32,16,512]{2,1,0:T(8,128)(2,1)S(1)}, u32[]{:S(2)}, u32[]{:S(2)}) %all-to-all-start.4) | async-done | bytes 524320 | tf_op jit(solution)/shard_map/all_to_all | solution.py:31
  35.1 4.9 %all-to-all-start.7 = ((bf16[32,16,512]{2,1,0:T(8,128)(2,1)}), bf16[32,16,512]{2,1,0:T(8,128)(2,1)S(1)}, u32[]{:S(2)}, u32[]{:S(2)}) async-start(bf16[32,16,512]{2,1,0:T(8,128)(2,1)} %bitcast.72), calls=%async_computation.7 | async-start | bytes 1048576 | tf_op jit(solution)/shard_map/all_to_all | solution.py:31
  40.4 0.6 gather_fusion.5
  41.0 15.9 %all-to-all-done.7 = bf16[32,16,512]{2,1,0:T(8,128)(2,1)S(1)} async-done(((bf16[32,16,512]{2,1,0:T(8,128)(2,1)}), bf16[32,16,512]{2,1,0:T(8,128)(2,1)S(1)}, u32[]{:S(2)}, u32[]{:S(2)}) %all-to-all-start.7) | async-done | bytes 524320 | tf_op jit(solution)/shard_map/all_to_all | solution.py:31
  56.9 1.6 gather_fusion.8
  58.5 2.3 %broadcast_select_fusion.7 = (bf16[54,16,512]{2,1,0:T(8,128)(2,1)}, bf16[54,16,512]{2,1,0:T(8,128)(2,1)S(1)}) fusion(bf16[54,16,512]{2,1,0:T(8,128)(2,1)} %gather_fusion.8, pred[54]{0:T(512)(128)(4,1)S(1)} %compare_and_fusion.3, bf16[54,16,512]{2,1,0:T(8,128)(2,1)S(1)} %gather_fusion.5), kind=kLoop, calls=%fused_computation.68 | loop fusion | flops 884736 | bytes 3538998 | tf_op jit(solution)/shard_map/jit(_take)/select_n | solution.py:36
  60.8 20.8 %all_to_all.49 = bf16[54,16,512]{2,1,0:T(8,128)(2,1)} all-to-all(bf16[54,16,512]{2,1,0:T(8,128)(2,1)S(1)} %get-tuple-element.108), channel_id=1, replica_groups=mesh['column'=32,'layer'=3,'fsdp'=8] {'layer'}, dimensions={0} | all-to-all | bytes 1769472 | tf_op jit(solution)/shard_map/all_to_all | solution.py:35
  81.6 3.5 %all-to-all-start.8 = ((bf16[54,16,512]{2,1,0:T(8,128)(2,1)}), bf16[54,16,512]{2,1,0:T(8,128)(2,1)S(1)}, u32[]{:S(2)}, u32[]{:S(2)}) async-start(bf16[54,16,512]{2,1,0:T(8,128)(2,1)} %get-tuple-element.107), calls=%async_computation.8 | async-start | bytes 1769472 | tf_op jit(solution)/shard_map/all_to_all | solution.py:35
  85.2 0.7 all-gather.2.cloned.1.call-update
  86.1 0.7 gather_fusion.6
  86.8 1.7 %gather_fusion.7 = bf16[32,16,512]{2,1,0:T(8,128)(2,1)S(1)} fusion(bf16[54,16,512]{2,1,0:T(8,128)(2,1)} %all_to_all.49, s32[1024]{0:T(1024)S(1)} %pad_clamp_fusion.3), kind=kCustom, calls=%fused_computation.2.clone | custom fusion | bytes 1048704 | tf_op jit(solution)/shard_map/jit(_take)/gather | solution.py:38
  88.6 8.6 %all-to-all-done.8 = bf16[54,16,512]{2,1,0:T(8,128)(2,1)S(1)} async-done(((bf16[54,16,512]{2,1,0:T(8,128)(2,1)}), bf16[54,16,512]{2,1,0:T(8,128)(2,1)S(1)}, u32[]{:S(2)}, u32[]{:S(2)}) %all-to-all-start.8) | async-done | bytes 884768 | tf_op jit(solution)/shard_map/all_to_all | solution.py:35
  97.2 1.4 gather_fusion.9
  98.6 2.0 %broadcast_select_fusion.9 = (bf16[32,16,512]{2,1,0:T(8,128)(2,1)}, bf16[32,16,512]{2,1,0:T(8,128)(2,1)S(1)}) fusion(bf16[32,16,512]{2,1,0:T(8,128)(2,1)} %gather_fusion.9, pred[32]{0:T(512)(128)(4,1)S(1)} %get-tuple-element.93, bf16[32,16,512]{2,1,0:T(8,128)(2,1)S(1)} %gather_fusion.7), kind=kLoop, calls=%fused_computation.70 | loop fusion | flops 524288 | bytes 2097184 | tf_op jit(solution)/shard_map/jit(_take)/select_n | solution.py:38
  100.6 25.9 %all_to_all.50 = bf16[32,16,512]{2,1,0:T(8,128)(2,1)} all-to-all(bf16[32,16,512]{2,1,0:T(8,128)(2,1)S(1)} %get-tuple-element.106), channel_id=1, replica_groups=mesh['column'=32,'layer'=3,'fsdp'=8] {'column'}, dimensions={0} | all-to-all | bytes 1048576 | tf_op jit(solution)/shard_map/all_to_all | solution.py:39
  126.6 4.9 %all-to-all-start.9 = ((bf16[32,16,512]{2,1,0:T(8,128)(2,1)}), bf16[32,16,512]{2,1,0:T(8,128)(2,1)}, u32[]{:S(2)}, u32[]{:S(2)}) async-start(bf16[32,16,512]{2,1,0:T(8,128)(2,1)} %get-tuple-element.105), calls=%async_computation.9 | async-start | bytes 1048576 | tf_op jit(solution)/shard_map/all_to_all | solution.py:39
  131.5 0.6 reduce_max.9
  132.8 2.8 %fusion.22 = bf16[1,512,512]{2,1,0:T(8,128)(2,1)} fusion(bf16[1024,512]{1,0:T(8,128)(2,1)S(1)} %copy-done, bf16[1024,512]{1,0:T(8,128)(2,1)} %all-gather.2.cloned.1.call-done), kind=kOutput, calls=%fused_computation.67 | convolution fusion | flops 537133056 | bytes 2621440 | tf_op jit(solution)/shard_map/dot_general | solution.py:94
  135.7 12.6 %all-to-all-done.9 = bf16[32,16,512]{2,1,0:T(8,128)(2,1)} async-done(((bf16[32,16,512]{2,1,0:T(8,128)(2,1)}), bf16[32,16,512]{2,1,0:T(8,128)(2,1)}, u32[]{:S(2)}, u32[]{:S(2)}) %all-to-all-start.9) | async-done | bytes 524320 | tf_op jit(solution)/shard_map/all_to_all | solution.py:39
  148.3 2.9 %conditional.1 = (bf16[1,512,512]{2,1,0:T(8,128)(2,1)}, bf16[1,512,512]{2,1,0:T(8,128)(2,1)}) conditional(s32[]{:T(128)} %convert_element_type.69, (bf16[512,512]{1,0:T(8,128)(2,1)S(1)}, bf16[512,512]{1,0:T(8,128)(2,1)}, bf16[512,512]{1,0:T(8,128)(2,1)S(1)}, bf16[32,16,512]{2,1,0:T(8,128)(2,1)}, bf16[32,16,512]{2,1,0:T(8,128)(2,1)}) %tuple.55, ...), branch_computations={%region_4.9_spmd, %region_5.0_spmd} | conditional | flops 7095654 | bytes 32526544 | solution.py:90
  148.3 2.9 %convert_bitcast_fusion = (bf16[1,512,512]{2,1,0:T(8,128)(2,1)}, bf16[1,512,512]{2,1,0:T(8,128)(2,1)}) fusion(bf16[32,16,512]{2,1,0:T(8,128)(2,1)} %get-tuple-element.40, bf16[512,512]{1,0:T(8,128)(2,1)S(1)} %get-tuple-element.26, bf16[32,16,512]{2,1,0:T(8,128)(2,1)} %get-tuple-element.39, bf16[512,512]{1,0:T(8,128)(2,1)S(1)} %get-tuple-element.38, ...), kind=kLoop, calls=%fused_computation.21 | loop fusion | flops 4980736 | bytes 3670016 | tf_op jit(solution)/shard_map/broadcast_in_dim | solution.py:96
  (27 shorter events, 0.8 us)
Async XLA Ops:
  7.2 125.7 %copy-start = (bf16[1024,512]{1,0:T(8,128)(2,1)S(1)}, bf16[1024,512]{1,0:T(8,128)(2,1)}, u32[]{:S(2)}) copy-start(bf16[1024,512]{1,0:T(8,128)(2,1)} %param.24) | copy-start | bytes 3145732
  7.2 27.9 %all-to-all-start.4 = ((bf16[32,16,512]{2,1,0:T(8,128)(2,1)}), bf16[32,16,512]{2,1,0:T(8,128)(2,1)S(1)}, u32[]{:S(2)}, u32[]{:S(2)}) async-start(bf16[32,16,512]{2,1,0:T(8,128)(2,1)} %bitcast.75), calls=%async_computation.4 | async-start | bytes 1048576 | tf_op jit(solution)/shard_map/all_to_all | solution.py:31
  35.1 21.8 %all-to-all-start.7 = ((bf16[32,16,512]{2,1,0:T(8,128)(2,1)}), bf16[32,16,512]{2,1,0:T(8,128)(2,1)S(1)}, u32[]{:S(2)}, u32[]{:S(2)}) async-start(bf16[32,16,512]{2,1,0:T(8,128)(2,1)} %bitcast.72), calls=%async_computation.7 | async-start | bytes 1048576 | tf_op jit(solution)/shard_map/all_to_all | solution.py:31
  81.6 15.6 %all-to-all-start.8 = ((bf16[54,16,512]{2,1,0:T(8,128)(2,1)}), bf16[54,16,512]{2,1,0:T(8,128)(2,1)S(1)}, u32[]{:S(2)}, u32[]{:S(2)}) async-start(bf16[54,16,512]{2,1,0:T(8,128)(2,1)} %get-tuple-element.107), calls=%async_computation.8 | async-start | bytes 1769472 | tf_op jit(solution)/shard_map/all_to_all | solution.py:35
  85.1 47.7 %all-gather.2.cloned.1.call-start = ((), (), s32[]{:S(2)}) async-start(), calls=%async_computation.10 | async-start | bytes 1179648 | tf_op jit(solution)/shard_map/all_gather | solution.py:93
  126.6 21.7 %all-to-all-start.9 = ((bf16[32,16,512]{2,1,0:T(8,128)(2,1)}), bf16[32,16,512]{2,1,0:T(8,128)(2,1)}, u32[]{:S(2)}, u32[]{:S(2)}) async-start(bf16[32,16,512]{2,1,0:T(8,128)(2,1)} %get-tuple-element.105), calls=%async_computation.9 | async-start | bytes 1048576 | tf_op jit(solution)/shard_map/all_to_all | solution.py:39
  132.8 15.5 %copy-start.1 = (bf16[1,512,512]{2,1,0:T(8,128)(2,1)S(1)}, bf16[1,512,512]{2,1,0:T(8,128)(2,1)}, u32[]{:S(2)}) copy-start(bf16[1,512,512]{2,1,0:T(8,128)(2,1)} %param.20) | copy-start | bytes 1572868
  132.8 15.5 %copy-start.2 = (bf16[1,512,512]{2,1,0:T(8,128)(2,1)S(1)}, bf16[1,512,512]{2,1,0:T(8,128)(2,1)}, u32[]{:S(2)}) copy-start(bf16[1,512,512]{2,1,0:T(8,128)(2,1)} %param.21) | copy-start | bytes 1572868
Sparse Core Ops, SparseCore 0:
  88.4 38.1 all-gather.1

commit v2 on v1

--- a/solution.py
+++ b/solution.py
@@ -5,7 +5,7 @@
 from jax.sharding import PartitionSpec as P
 
 LAYERS = 3
-SLOTS = 18
+SLOTS = 16
 
 decay_old = 0.5
 grad_rate = 0.7
@@ -31,28 +31,37 @@
     return lax.all_to_all(pieces, "column", split_axis=0, concat_axis=0, tiled=True)
 
 
-def deliver(pieces, send_index, take_index):
-    crossed = lax.all_to_all(
-        jnp.take(pieces, send_index, axis=0), "layer", split_axis=0, concat_axis=0, tiled=True
-    )
-    routed = jnp.take(crossed, take_index, axis=0)
+def take(array, index):
+    return array.at[index].get(mode="promise_in_bounds")
+
+
+def cross(pieces, send_index, slots):
+    packed = take(pieces, send_index)
+    up = lax.ppermute(packed[:slots], "layer", [(i, (i + 1) % LAYERS) for i in range(LAYERS)])
+    down = lax.ppermute(packed[slots:], "layer", [(i, (i + 2) % LAYERS) for i in range(LAYERS)])
+    return jnp.concatenate([pieces, up, down], axis=0)
+
+
+def deliver(held, take_index):
+    routed = take(held, take_index)
     arrived = lax.all_to_all(routed, "column", split_axis=0, concat_axis=0, tiled=True)
     return arrived.reshape(-1, arrived.shape[-1])
 
 
 def routes(target, rank, layer, slots):
     columns = target.shape[0]
-    mine_to = jnp.take(target % LAYERS, layer, axis=1)
+    ids = jnp.arange(columns, dtype=jnp.int32)
+    shift = (jnp.take(target, layer, axis=1) - layer + LAYERS) % LAYERS
     mine_rank = jnp.take(rank, layer, axis=1)
-    slot = mine_to * slots + mine_rank
-    chosen = slot[None, :] == jnp.arange(LAYERS * slots, dtype=jnp.int32)[:, None]
-    chosen = chosen & (mine_rank < slots)[None, :]
-    send_index = jnp.sum(
-        jnp.where(chosen, jnp.arange(columns, dtype=jnp.int32)[None, :], 0), axis=1
+    slot = jnp.where((shift > 0) & (mine_rank < slots), (shift - 1) * slots + mine_rank, -1)
+    chosen = slot[None, :] == jnp.arange(2 * slots, dtype=jnp.int32)[:, None]
+    send_index = jnp.sum(jnp.where(chosen, ids[None, :], 0), axis=1)
+    source = jnp.take(target, layer, axis=1)
+    came = (layer - source + LAYERS * columns) % LAYERS
+    source_rank = jnp.minimum(jnp.take(rank.reshape(-1), source, axis=0), slots - 1)
+    take_index = jnp.where(
+        came == 0, source // LAYERS, columns + (came - 1) * slots + source_rank
     )
-    source = jnp.take(target, layer, axis=1)
-    source_rank = jnp.take(rank.reshape(-1), source, axis=0)
-    take_index = jnp.minimum(source % LAYERS * slots + source_rank, LAYERS * slots - 1)
     return send_index, take_index
 
 
@@ -66,31 +75,35 @@
     before = jnp.tril(jnp.ones((columns, columns), jnp.int32), -1)
     earlier = jnp.sum(before[:, :, None, None] * to_layer[None].astype(jnp.int32), axis=1)
     rank = jnp.sum(jnp.where(to_layer, earlier, 0), axis=2)
-    crowded = jnp.max(rank) >= SLOTS
+    own = to_layer & (jnp.arange(LAYERS)[None, :, None] == jnp.arange(LAYERS)[None, None, :])
+    crowded = jnp.max(jnp.where(jnp.any(own, axis=2), 0, rank)) >= SLOTS
 
+    gathered = lax.all_gather(key_cotangent, "fsdp", axis=0, tiled=True)
+    send_index, take_index = routes(target, rank, layer, SLOTS)
     spread_weights = spread(weights)
     spread_grad = spread(pseudo_grad)
-    send_index, take_index = routes(target, rank, layer, SLOTS)
-    partner_weights = deliver(spread_weights, send_index, take_index)
-    partner_grad = deliver(spread_grad, send_index, take_index)
+    held_weights = cross(spread_weights, send_index, SLOTS)
+    held_grad = cross(spread_grad, send_index, SLOTS)
+    held_grad, gathered = lax.optimization_barrier((held_grad, gathered))
+    partner_weights = deliver(held_weights, take_index)
+    partner_grad = deliver(held_grad, take_index)
 
     def as_arrived():
         return outer_step(weights, pseudo_grad, momentum, partner_weights, partner_grad)
 
     def again():
-        index = routes(target, rank, layer, columns)
+        send_all, take_all = routes(target, rank, layer, columns)
         return outer_step(
             weights,
             pseudo_grad,
             momentum,
-            deliver(spread_weights, *index),
-            deliver(spread_grad, *index),
+            deliver(cross(spread_weights, send_all, columns), take_all),
+            deliver(cross(spread_grad, send_all, columns), take_all),
         )
 
     new_weights, new_momentum = lax.cond(crowded, again, as_arrived)
 
     contract = (((0,), (0,)), ((), ()))
-    gathered = lax.all_gather(key_cotangent, "fsdp", axis=0, tiled=True)
     grad_f32 = lax.dot_general(activations, gathered, contract, preferred_element_type=jnp.float32)
     weight_grad = grad_f32.astype(jnp.bfloat16)
     return (new_weights[None], new_momentum[None], weight_grad[None])

time: 159 us -> 133 us (0.84)
  the two profiles are of different devices: /device:TPU:200 before, /device:TPU:8 now
where the time goes in v2:
time: 133 us; the launch traced here: 132 us
  starting transfers between devices  52.2 us (39%)
  waiting for transfers between devices  49.5 us (37%)
  between operations  14.9 us (11%)
  local copies, waits for them, and re-layouts  7.77 us (6%)
  other arithmetic  4.65 us (3%)
  matrix products  2.84 us (2%)
    all_to_all x2, starting transfers between devices, deliver(): lax.all_to_all(routed, 'column', split_axis=0, concat_axis=0, tiled=True)  19.7 us
    all_to_all x2, starting transfers between devices, spread(): lax.all_to_all(pieces, 'column', split_axis=0, concat_axis=0, tiled=True)  17.7 us
    ppermute x2, waiting for transfers between devices, cross(): lax.ppermute(packed[:slots], 'layer', [(i, (i + 1) % LAYERS) for i in ran...  16.2 us
    all_to_all x2, waiting for transfers between devices, spread(): lax.all_to_all(pieces, 'column', split_axis=0, concat_axis=0, tiled=True)  12.5 us
    all_to_all x2, waiting for transfers between devices, deliver(): lax.all_to_all(routed, 'column', split_axis=0, concat_axis=0, tiled=True)  11.7 us
    ppermute x2, waiting for transfers between devices, cross(): lax.ppermute(packed[slots:], 'layer', [(i, (i + 2) % LAYERS) for i in ran...  8.45 us
    ppermute x2, starting transfers between devices, cross(): lax.ppermute(packed[slots:], 'layer', [(i, (i + 2) % LAYERS) for i in ran...  7.65 us
    ppermute x2, starting transfers between devices, cross(): lax.ppermute(packed[:slots], 'layer', [(i, (i + 1) % LAYERS) for i in ran...  7.08 us
  transfers between devices with their start and end apart: 9, of which 6 were waited for; matrix products, arithmetic and copies ran while one was open for 9% of the time, Pallas kernels for 0%

profile of v2, /device:TPU:8, one launch (start us, length us, event | category | flops | bytes accessed | tf_op | source)
XLA Modules:
  0.0 131.9 jit_solution(17539509622652138740)
XLA Ops:
  7.2 0.7 all-gather.2.cloned.1.call-update
  7.9 13.0 %all-to-all-start.4 = ((bf16[32,16,512]{2,1,0:T(8,128)(2,1)}), bf16[32,16,512]{2,1,0:T(8,128)(2,1)S(1)}, u32[]{:S(2)}, u32[]{:S(2)}) async-start(bf16[32,16,512]{2,1,0:T(8,128)(2,1)} %bitcast.64), calls=%async_computation.4 | async-start | bytes 1048576 | tf_op jit(solution)/shard_map/all_to_all | solution.py:31
  20.9 0.8 reshape.107
  22.7 0.7 gather_fusion.9
  23.4 12.5 %all-to-all-done.4 = bf16[32,16,512]{2,1,0:T(8,128)(2,1)S(1)} async-done(((bf16[32,16,512]{2,1,0:T(8,128)(2,1)}), bf16[32,16,512]{2,1,0:T(8,128)(2,1)S(1)}, u32[]{:S(2)}, u32[]{:S(2)}) %all-to-all-start.4) | async-done | bytes 524320 | tf_op jit(solution)/shard_map/all_to_all | solution.py:31
  35.9 4.7 %all-to-all-start.2 = ((bf16[32,16,512]{2,1,0:T(8,128)(2,1)}), bf16[32,16,512]{2,1,0:T(8,128)(2,1)S(1)}, u32[]{:S(2)}, u32[]{:S(2)}) async-start(bf16[32,16,512]{2,1,0:T(8,128)(2,1)} %bitcast.14), calls=%async_computation.2 | async-start | bytes 1048576 | tf_op jit(solution)/shard_map/all_to_all | solution.py:31
  41.4 4.3 %collective-permute-start.6 = (bf16[16,16,512]{2,1,0:T(8,128)(2,1)S(1)}, bf16[16,16,512]{2,1,0:T(8,128)(2,1)S(1)}, u32[]{:S(2)}, u32[]{:S(2)}) collective-permute-start(bf16[16,16,512]{2,1,0:T(8,128)(2,1)S(1)} %get-tuple-element.112), channel_id=1, source_target_pairs={{0,8},{8,16},{16,0},{1,9},{9,17},{17,1},{2,10},{10,18},{18,2},{3,1... | collective-permute-start | bytes 786440 | tf_op jit(solution)/shard_map/ppermute | solution.py:40
  45.6 3.7 %collective-permute-start.7 = (bf16[16,16,512]{2,1,0:T(8,128)(2,1)S(1)}, bf16[16,16,512]{2,1,0:T(8,128)(2,1)S(1)}, u32[]{:S(2)}, u32[]{:S(2)}) collective-permute-start(bf16[16,16,512]{2,1,0:T(8,128)(2,1)S(1)} %get-tuple-element.113), channel_id=1, source_target_pairs={{0,16},{8,0},{16,8},{1,17},{9,1},{17,9},{2,18},{10,2},{18,10},{3,1... | collective-permute-start | bytes 786440 | tf_op jit(solution)/shard_map/ppermute | solution.py:41
  49.4 10.9 %collective-permute-done.6 = bf16[16,16,512]{2,1,0:T(8,128)(2,1)S(1)} collective-permute-done((bf16[16,16,512]{2,1,0:T(8,128)(2,1)S(1)}, bf16[16,16,512]{2,1,0:T(8,128)(2,1)S(1)}, u32[]{:S(2)}, u32[]{:S(2)}) %collective-permute-start.6) | collective-permute-done | bytes 262176 | tf_op jit(solution)/shard_map/ppermute | solution.py:40
  60.3 4.8 %collective-permute-done.7 = bf16[16,16,512]{2,1,0:T(8,128)(2,1)S(1)} collective-permute-done((bf16[16,16,512]{2,1,0:T(8,128)(2,1)S(1)}, bf16[16,16,512]{2,1,0:T(8,128)(2,1)S(1)}, u32[]{:S(2)}, u32[]{:S(2)}) %collective-permute-start.7) | collective-permute-done | bytes 262176 | tf_op jit(solution)/shard_map/ppermute | solution.py:41
  65.2 1.4 %gather_fusion.8 = bf16[32,16,512]{2,1,0:T(8,128)(2,1)} fusion(bf16[64,16,512]{2,1,0:T(8,128)(2,1)S(1)} %pad_maximum_fusion.3, s32[1024]{0:T(1024)S(1)} %pad_clamp_fusion.3), kind=kCustom, calls=%fused_computation.9 | custom fusion | bytes 1048704 | tf_op jit(solution)/shard_map/gather | solution.py:35
  66.6 9.9 %all-to-all-start.5 = ((bf16[32,16,512]{2,1,0:T(8,128)(2,1)}), bf16[32,16,512]{2,1,0:T(8,128)(2,1)}, u32[]{:S(2)}, u32[]{:S(2)}) async-start(bf16[32,16,512]{2,1,0:T(8,128)(2,1)} %gather_fusion.8), calls=%async_computation.5 | async-start | bytes 1048576 | tf_op jit(solution)/shard_map/all_to_all | solution.py:47
  77.1 2.8 %collective-permute-start.4 = (bf16[16,16,512]{2,1,0:T(8,128)(2,1)S(1)}, bf16[16,16,512]{2,1,0:T(8,128)(2,1)S(1)}, u32[]{:S(2)}, u32[]{:S(2)}) collective-permute-start(bf16[16,16,512]{2,1,0:T(8,128)(2,1)S(1)} %get-tuple-element.114), channel_id=1, source_target_pairs={{0,8},{8,16},{16,0},{1,9},{9,17},{17,1},{2,10},{10,18},{18,2},{3,1... | collective-permute-start | bytes 786440 | tf_op jit(solution)/shard_map/ppermute | solution.py:40
  79.9 3.9 %collective-permute-start.5 = (bf16[16,16,512]{2,1,0:T(8,128)(2,1)S(1)}, bf16[16,16,512]{2,1,0:T(8,128)(2,1)S(1)}, u32[]{:S(2)}, u32[]{:S(2)}) collective-permute-start(bf16[16,16,512]{2,1,0:T(8,128)(2,1)S(1)} %get-tuple-element.115), channel_id=1, source_target_pairs={{0,16},{8,0},{16,8},{1,17},{9,1},{17,9},{2,18},{10,2},{18,10},{3,1... | collective-permute-start | bytes 786440 | tf_op jit(solution)/shard_map/ppermute | solution.py:41
  83.9 5.3 %collective-permute-done.4 = bf16[16,16,512]{2,1,0:T(8,128)(2,1)S(1)} collective-permute-done((bf16[16,16,512]{2,1,0:T(8,128)(2,1)S(1)}, bf16[16,16,512]{2,1,0:T(8,128)(2,1)S(1)}, u32[]{:S(2)}, u32[]{:S(2)}) %collective-permute-start.4) | collective-permute-done | bytes 262176 | tf_op jit(solution)/shard_map/ppermute | solution.py:40
  89.2 3.6 %collective-permute-done.5 = bf16[16,16,512]{2,1,0:T(8,128)(2,1)S(1)} collective-permute-done((bf16[16,16,512]{2,1,0:T(8,128)(2,1)S(1)}, bf16[16,16,512]{2,1,0:T(8,128)(2,1)S(1)}, u32[]{:S(2)}, u32[]{:S(2)}) %collective-permute-start.5) | collective-permute-done | bytes 262176 | tf_op jit(solution)/shard_map/ppermute | solution.py:41
  93.0 1.4 %gather_fusion.6 = bf16[32,16,512]{2,1,0:T(8,128)(2,1)} fusion(bf16[64,16,512]{2,1,0:T(8,128)(2,1)S(1)} %pad_maximum_fusion.2, s32[1024]{0:T(1024)S(1)} %pad_clamp_fusion.3), kind=kCustom, calls=%fused_computation.7 | custom fusion | bytes 1048704 | tf_op jit(solution)/shard_map/gather | solution.py:35
  94.4 9.8 %all-to-all-start.3 = ((bf16[32,16,512]{2,1,0:T(8,128)(2,1)}), bf16[32,16,512]{2,1,0:T(8,128)(2,1)}, u32[]{:S(2)}, u32[]{:S(2)}) async-start(bf16[32,16,512]{2,1,0:T(8,128)(2,1)} %gather_fusion.6), calls=%async_computation.3 | async-start | bytes 1048576 | tf_op jit(solution)/shard_map/all_to_all | solution.py:47
  104.2 0.6 select_reduce_fusion.5
  105.5 2.8 %fusion.16 = bf16[1,512,512]{1,2,0:T(8,128)(2,1)} fusion(bf16[1024,512]{1,0:T(8,128)(2,1)} %all-gather.2.cloned.1.call-done, bf16[1024,512]{1,0:T(8,128)(2,1)S(1)} %copy-done), kind=kOutput, calls=%fused_computation.55 | convolution fusion | flops 537133056 | bytes 2621440 | tf_op jit(solution)/shard_map/dot_general | solution.py:107
  108.4 2.0 %copy.17 = bf16[1,512,512]{2,1,0:T(8,128)(2,1)} copy(bf16[1,512,512]{1,2,0:T(8,128)(2,1)} %fusion.16) | data formatting | bytes 1048576
  110.4 11.7 %all-to-all-done.3 = bf16[32,16,512]{2,1,0:T(8,128)(2,1)} async-done(((bf16[32,16,512]{2,1,0:T(8,128)(2,1)}), bf16[32,16,512]{2,1,0:T(8,128)(2,1)}, u32[]{:S(2)}, u32[]{:S(2)}) %all-to-all-start.3) | async-done | bytes 524320 | tf_op jit(solution)/shard_map/all_to_all | solution.py:47
  122.1 2.9 %conditional.1 = (bf16[1,512,512]{2,1,0:T(8,128)(2,1)}, bf16[1,512,512]{2,1,0:T(8,128)(2,1)}) conditional(s32[]{:T(128)} %convert_element_type.72, (bf16[512,512]{1,0:T(8,128)(2,1)S(1)}, bf16[512,512]{1,0:T(8,128)(2,1)S(1)}, bf16[512,512]{1,0:T(8,128)(2,1)}, bf16[32,16,512]{2,1,0:T(8,128)(2,1)}, bf16[32,16,512]{2,1,0:T(8,128)(2,1)}) %tuple.54, ...), branch_computations={%region_5.8_spmd, %region_6.10_spmd} | conditional | flops 8137510 | bytes 31475988 | solution.py:104
  122.1 2.9 %convert_bitcast_fusion = (bf16[1,512,512]{2,1,0:T(8,128)(2,1)}, bf16[1,512,512]{2,1,0:T(8,128)(2,1)}) fusion(bf16[32,16,512]{2,1,0:T(8,128)(2,1)} %get-tuple-element.36, bf16[512,512]{1,0:T(8,128)(2,1)S(1)} %get-tuple-element.32, bf16[32,16,512]{2,1,0:T(8,128)(2,1)} %get-tuple-element.35, bf16[512,512]{1,0:T(8,128)(2,1)} %get-tuple-element.34, ...), kind=kLoop, calls=%fused_computation.21 | loop fusion | flops 4980736 | bytes 3670016 | tf_op jit(solution)/shard_map/broadcast_in_dim | solution.py:109
  (34 shorter events, 2.7 us)
Async XLA Ops:
  7.2 98.3 %copy-start = (bf16[1024,512]{1,0:T(8,128)(2,1)S(1)}, bf16[1024,512]{1,0:T(8,128)(2,1)}, u32[]{:S(2)}) copy-start(bf16[1024,512]{1,0:T(8,128)(2,1)} %param.16) | copy-start | bytes 3145732
  7.2 85.8 %all-gather.2.cloned.1.call-start = ((), (), s32[]{:S(2)}) async-start(), calls=%async_computation.6 | async-start | bytes 1179648 | tf_op jit(solution)/shard_map/all_gather | solution.py:81
  7.9 28.0 %all-to-all-start.4 = ((bf16[32,16,512]{2,1,0:T(8,128)(2,1)}), bf16[32,16,512]{2,1,0:T(8,128)(2,1)S(1)}, u32[]{:S(2)}, u32[]{:S(2)}) async-start(bf16[32,16,512]{2,1,0:T(8,128)(2,1)} %bitcast.64), calls=%async_computation.4 | async-start | bytes 1048576 | tf_op jit(solution)/shard_map/all_to_all | solution.py:31
  35.9 30.6 %all-to-all-start.2 = ((bf16[32,16,512]{2,1,0:T(8,128)(2,1)}), bf16[32,16,512]{2,1,0:T(8,128)(2,1)S(1)}, u32[]{:S(2)}, u32[]{:S(2)}) async-start(bf16[32,16,512]{2,1,0:T(8,128)(2,1)} %bitcast.14), calls=%async_computation.2 | async-start | bytes 1048576 | tf_op jit(solution)/shard_map/all_to_all | solution.py:31
  41.4 18.9 %collective-permute-start.6 = (bf16[16,16,512]{2,1,0:T(8,128)(2,1)S(1)}, bf16[16,16,512]{2,1,0:T(8,128)(2,1)S(1)}, u32[]{:S(2)}, u32[]{:S(2)}) collective-permute-start(bf16[16,16,512]{2,1,0:T(8,128)(2,1)S(1)} %get-tuple-element.112), channel_id=1, source_target_pairs={{0,8},{8,16},{16,0},{1,9},{9,17},{17,1},{2,10},{10,18},{18,2},{3,1... | collective-permute-start | bytes 786440 | tf_op jit(solution)/shard_map/ppermute | solution.py:40
  45.6 19.4 %collective-permute-start.7 = (bf16[16,16,512]{2,1,0:T(8,128)(2,1)S(1)}, bf16[16,16,512]{2,1,0:T(8,128)(2,1)S(1)}, u32[]{:S(2)}, u32[]{:S(2)}) collective-permute-start(bf16[16,16,512]{2,1,0:T(8,128)(2,1)S(1)} %get-tuple-element.113), channel_id=1, source_target_pairs={{0,16},{8,0},{16,8},{1,17},{9,1},{17,9},{2,18},{10,2},{18,10},{3,1... | collective-permute-start | bytes 786440 | tf_op jit(solution)/shard_map/ppermute | solution.py:41
  66.6 27.8 %all-to-all-start.5 = ((bf16[32,16,512]{2,1,0:T(8,128)(2,1)}), bf16[32,16,512]{2,1,0:T(8,128)(2,1)}, u32[]{:S(2)}, u32[]{:S(2)}) async-start(bf16[32,16,512]{2,1,0:T(8,128)(2,1)} %gather_fusion.8), calls=%async_computation.5 | async-start | bytes 1048576 | tf_op jit(solution)/shard_map/all_to_all | solution.py:47
  77.1 12.1 %collective-permute-start.4 = (bf16[16,16,512]{2,1,0:T(8,128)(2,1)S(1)}, bf16[16,16,512]{2,1,0:T(8,128)(2,1)S(1)}, u32[]{:S(2)}, u32[]{:S(2)}) collective-permute-start(bf16[16,16,512]{2,1,0:T(8,128)(2,1)S(1)} %get-tuple-element.114), channel_id=1, source_target_pairs={{0,8},{8,16},{16,0},{1,9},{9,17},{17,1},{2,10},{10,18},{18,2},{3,1... | collective-permute-start | bytes 786440 | tf_op jit(solution)/shard_map/ppermute | solution.py:40
  79.9 12.9 %collective-permute-start.5 = (bf16[16,16,512]{2,1,0:T(8,128)(2,1)S(1)}, bf16[16,16,512]{2,1,0:T(8,128)(2,1)S(1)}, u32[]{:S(2)}, u32[]{:S(2)}) collective-permute-start(bf16[16,16,512]{2,1,0:T(8,128)(2,1)S(1)} %get-tuple-element.115), channel_id=1, source_target_pairs={{0,16},{8,0},{16,8},{1,17},{9,1},{17,9},{2,18},{10,2},{18,10},{3,1... | collective-permute-start | bytes 786440 | tf_op jit(solution)/shard_map/ppermute | solution.py:41
  94.4 27.7 %all-to-all-start.3 = ((bf16[32,16,512]{2,1,0:T(8,128)(2,1)}), bf16[32,16,512]{2,1,0:T(8,128)(2,1)}, u32[]{:S(2)}, u32[]{:S(2)}) async-start(bf16[32,16,512]{2,1,0:T(8,128)(2,1)} %gather_fusion.6), calls=%async_computation.3 | async-start | bytes 1048576 | tf_op jit(solution)/shard_map/all_to_all | solution.py:47
  105.5 16.6 %copy-start.1 = (bf16[1,512,512]{2,1,0:T(8,128)(2,1)S(1)}, bf16[1,512,512]{2,1,0:T(8,128)(2,1)}, u32[]{:S(2)}) copy-start(bf16[1,512,512]{2,1,0:T(8,128)(2,1)} %param.12) | copy-start | bytes 1572868
  105.5 16.6 %copy-start.2 = (bf16[1,512,512]{2,1,0:T(8,128)(2,1)S(1)}, bf16[1,512,512]{2,1,0:T(8,128)(2,1)}, u32[]{:S(2)}) copy-start(bf16[1,512,512]{2,1,0:T(8,128)(2,1)} %param.14) | copy-start | bytes 1572868
Sparse Core Ops, SparseCore 0:
  10.5 48.4 all-gather.1

commit v3 on v0

v3 whole, which is shorter than its diff:
```python
import jax
import jax.numpy as jnp
from jax import lax
from jax.sharding import PartitionSpec as P

UNIT_ROWS = 4
UNIT_COLS = 128

decay_old = 0.5
grad_rate = 0.7
pull_rate = 0.9


def to_pieces(first, second, count):
    rows, cols = first.shape
    quads = [a.reshape(rows // UNIT_ROWS, UNIT_ROWS, cols) for a in (first, second)]
    wide = cols // UNIT_COLS
    per_piece = -(-2 * rows // UNIT_ROWS * wide // count)
    spare = (per_piece * count - 2 * rows // UNIT_ROWS * wide) // wide
    joined = jnp.concatenate([*quads, jnp.zeros((spare, UNIT_ROWS, cols), first.dtype)], axis=0)
    cut = joined.reshape(-1, UNIT_ROWS, wide, UNIT_COLS).transpose(0, 2, 1, 3)
    return cut.reshape(count, per_piece, UNIT_ROWS, UNIT_COLS)


def from_pieces(pieces, rows, cols):
    wide = cols // UNIT_COLS
    cut = pieces.reshape(-1, wide, UNIT_ROWS, UNIT_COLS)
    quads = rows // UNIT_ROWS
    parts = (cut[:quads], cut[quads : 2 * quads])
    return [p.transpose(0, 2, 1, 3).reshape(rows, cols) for p in parts]


def exchange(pieces):
    return lax.all_to_all(pieces, "replica", split_axis=0, concat_axis=0, tiled=True)


def on_device(weights, pseudo_grad, momentum, partner, activations, key_cotangent):
    replicas = lax.axis_size("replica")
    weights, pseudo_grad, momentum = weights[0], pseudo_grad[0], momentum[0]
    rows, cols = weights.shape
    gathered = lax.all_gather(key_cotangent, "fsdp", axis=0, tiled=True)

    pieces = exchange(to_pieces(weights, pseudo_grad, replicas))
    routed = pieces.at[partner].get(mode="promise_in_bounds")
    routed, gathered = lax.optimization_barrier((routed, gathered))
    partner_weights, partner_grad = lax.optimization_barrier(
        from_pieces(exchange(routed), rows, cols)
    )

    weights_f32 = weights.astype(jnp.float32)
    mean_weights = (weights_f32 + partner_weights.astype(jnp.float32)) * 0.5
    mean_grad = (pseudo_grad.astype(jnp.float32) + partner_grad.astype(jnp.float32)) * 0.5
    momentum_f = (
        decay_old * momentum.astype(jnp.float32)
        - grad_rate * mean_grad
        - pull_rate * (weights_f32 - mean_weights)
    )
    new_weights = weights_f32 + decay_old * momentum_f - grad_rate * mean_grad
    new_weights = new_weights.astype(jnp.bfloat16)
    new_momentum = momentum_f.astype(jnp.bfloat16)

    contract = (((0,), (0,)), ((), ()))
    grad_f32 = lax.dot_general(activations, gathered, contract, preferred_element_type=jnp.float32)
    weight_grad = grad_f32.astype(jnp.bfloat16)
    return (new_weights[None], new_momentum[None], weight_grad[None])


def solution(mesh):
    block = P("replica", "fsdp", None)
    return jax.shard_map(
        on_device,
        mesh=mesh,
        in_specs=(
            block,
            block,
            block,
            P(),
            P("replica", "fsdp"),
            P(("replica", "fsdp"), None),
        ),
        out_specs=(block, block, block),
        check_vma=False,
    )
```

time: 727 us -> 128 us (0.18)
  the two profiles are of different devices: /device:TPU:192 before, /device:TPU:1 now
where the time goes in v3:
time: 128 us
  waiting for transfers between devices  74 us (58%)
  starting transfers between devices  26.9 us (21%)
  between operations  14.2 us (11%)
  local copies, waits for them, and re-layouts  7.39 us (6%)
  other arithmetic  3.4 us (3%)
  matrix products  1.96 us (2%)
    all_to_all x2, waiting for transfers between devices, exchange(): lax.all_to_all(pieces, 'replica', split_axis=0, concat_axis=0, tiled=True)  55.6 us
    all_to_all x2, starting transfers between devices, exchange(): lax.all_to_all(pieces, 'replica', split_axis=0, concat_axis=0, tiled=True)  26.9 us
    all_gather x1, waiting for transfers between devices, on_device(): gathered = lax.all_gather(key_cotangent, 'fsdp', axis=0, tiled=True)  17.8 us
    gather x1, local copies, waits for them, and re-layouts, on_device(): routed = pieces.at[partner].get(mode='promise_in_bounds')  2.58 us
  transfers between devices with their start and end apart: 3, of which 3 were waited for; matrix products, arithmetic and copies ran while one was open for 4% of the time, Pallas kernels for 0%

profile of v3, /device:TPU:1, one launch (start us, length us, event | category | flops | bytes accessed | tf_op | source)
XLA Modules:
  0.0 127.9 jit_solution(15683497288446715768)
XLA Ops:
  7.2 0.0 copy-start
  7.2 1.3 %concatenate.8 = bf16[128,4,4,128]{3,2,1,0:T(4,128)(2,1)S(1)} reshape(bf16[1,512,512]{2,1,0:T(8,128)(2,1)} %param.6) | data formatting | bytes 1048576 | tf_op jit(solution)/shard_map/concatenate | solution.py:20
  8.5 0.2 copy.13
  8.7 0.1 concatenate.9
  8.8 0.2 copy.14
  9.1 1.8 %maximum_maximum_fusion = bf16[264,4,4,128]{3,1,2,0:T(4,128)(2,1)} fusion(bf16[128,4,4,128]{3,1,2,0:T(4,128)(2,1)S(1)} %copy.14, bf16[128,4,4,128]{3,1,2,0:T(4,128)(2,1)S(1)} %copy.13, bf16[264]{0:T(512)(128)(2,1)S(1)} %pad.2.clone), kind=kLoop, calls=%fused_computation.6 | loop fusion | flops 1081344 | bytes 2130448 | tf_op jit(solution)/shard_map/concatenate | solution.py:20
  10.9 15.5 %all-to-all-start = ((bf16[96,11,4,128]{3,2,1,0:T(4,128)(2,1)}), bf16[96,11,4,128]{3,2,1,0:T(4,128)(2,1)S(1)}, u32[]{:S(2)}, u32[]{:S(2)}) async-start(bf16[96,11,4,128]{3,2,1,0:T(4,128)(2,1)} %bitcast.4), calls=%async_computation | async-start | bytes 2162688 | tf_op jit(solution)/shard_map/all_to_all | solution.py:34
  26.3 0.0 all-gather.2.cloned.1.call-start
  26.4 0.7 all-gather.2.cloned.1.call-update
  27.1 28.7 %all-to-all-done = bf16[96,11,4,128]{3,2,1,0:T(4,128)(2,1)S(1)} async-done(((bf16[96,11,4,128]{3,2,1,0:T(4,128)(2,1)}), bf16[96,11,4,128]{3,2,1,0:T(4,128)(2,1)S(1)}, u32[]{:S(2)}, u32[]{:S(2)}) %all-to-all-start) | async-done | bytes 1081376 | tf_op jit(solution)/shard_map/all_to_all | solution.py:34
  55.8 2.6 %gather_fusion = bf16[96,11,4,128]{3,2,1,0:T(4,128)(2,1)} fusion(bf16[96,11,4,128]{3,2,1,0:T(4,128)(2,1)S(1)} %all-to-all-done, s32[1024]{0:T(1024)S(1)} %pad_clamp_fusion), kind=kCustom, calls=%fused_computation | custom fusion | bytes 2163072 | tf_op jit(solution)/shard_map/gather | solution.py:44
  58.4 17.8 %all-gather.2.cloned.1.call-done = bf16[1024,512]{1,0:T(8,128)(2,1)} async-done(((bf16[128,512]{1,0:T(8,128)(2,1)}), bf16[1024,512]{1,0:T(8,128)(2,1)}) %all-gather.2.cloned.1.call-update) | async-done | bytes 1048592 | tf_op jit(solution)/shard_map/all_gather | solution.py:41
  76.2 11.4 %all-to-all-start.1 = ((bf16[96,11,4,128]{3,2,1,0:T(4,128)(2,1)}), bf16[96,11,4,128]{3,2,1,0:T(4,128)(2,1)S(1)}, u32[]{:S(2)}, u32[]{:S(2)}) async-start(bf16[96,11,4,128]{3,2,1,0:T(4,128)(2,1)} %gather_fusion), calls=%async_computation.1 | async-start | bytes 2162688 | tf_op jit(solution)/shard_map/all_to_all | solution.py:34
  87.6 2.0 %fusion = bf16[1,512,512]{1,2,0:T(8,128)(2,1)S(1)} fusion(bf16[1024,512]{1,0:T(8,128)(2,1)} %all-gather.2.cloned.1.call-done, bf16[1024,512]{1,0:T(8,128)(2,1)S(1)} %copy-done), kind=kOutput, calls=%fused_computation.5 | convolution fusion | flops 537133056 | bytes 2621440 | tf_op jit(solution)/shard_map/dot_general | solution.py:63
  89.6 1.0 copy.17
  90.6 26.9 %all-to-all-done.1 = bf16[96,11,4,128]{3,2,1,0:T(4,128)(2,1)S(1)} async-done(((bf16[96,11,4,128]{3,2,1,0:T(4,128)(2,1)}), bf16[96,11,4,128]{3,2,1,0:T(4,128)(2,1)S(1)}, u32[]{:S(2)}, u32[]{:S(2)}) %all-to-all-start.1) | async-done | bytes 1081376 | tf_op jit(solution)/shard_map/all_to_all | solution.py:34
  117.5 0.4 slice_bitcast_fusion
  117.8 0.2 copy.15
  118.1 0.2 copy.16
  118.3 0.0 copy-start.3
  118.3 0.1 copy_bitcast_fusion
  118.5 0.9 copy-done.2
  119.3 0.2 copy-done.3
  119.5 1.6 %convert_bitcast_fusion = (bf16[1,512,512]{2,1,0:T(8,128)(2,1)}, bf16[1,512,512]{2,1,0:T(8,128)(2,1)}) fusion(bf16[512,512]{1,0:T(8,128)(2,1)S(1)} %get-tuple-element.9, bf16[1,512,512]{2,1,0:T(8,128)(2,1)S(1)} %copy-done.2, bf16[512,512]{1,0:T(8,128)(2,1)S(1)} %get-tuple-element.8, bf16[1,512,512]{2,1,0:T(8,128)(2,1)S(1)} %copy-done.1, ...), kind=kLoop, calls=%fused_computation.20 | loop fusion | flops 4980736 | bytes 3670016 | tf_op jit(solution)/shard_map/broadcast_in_dim | solution.py:65
  (10 shorter events, 0.0 us)
Async XLA Ops:
  7.2 80.5 %copy-start = (bf16[1024,512]{1,0:T(8,128)(2,1)S(1)}, bf16[1024,512]{1,0:T(8,128)(2,1)}, u32[]{:S(2)}) copy-start(bf16[1024,512]{1,0:T(8,128)(2,1)} %param.10) | copy-start | bytes 3145732
  7.2 1.5 %copy-start.1 = (bf16[1,512,512]{2,1,0:T(8,128)(2,1)S(1)}, bf16[1,512,512]{2,1,0:T(8,128)(2,1)}, u32[]{:S(2)}) copy-start(bf16[1,512,512]{2,1,0:T(8,128)(2,1)} %param.7) | copy-start | bytes 1572868
  10.9 16.2 %copy-start.4 = (s32[96]{0:T(128)S(1)}, s32[96]{0:T(128)}, u32[]{:S(2)}) copy-start(s32[96]{0:T(128)} %param.9) | copy-start | bytes 1156
  10.9 45.0 %all-to-all-start = ((bf16[96,11,4,128]{3,2,1,0:T(4,128)(2,1)}), bf16[96,11,4,128]{3,2,1,0:T(4,128)(2,1)S(1)}, u32[]{:S(2)}, u32[]{:S(2)}) async-start(bf16[96,11,4,128]{3,2,1,0:T(4,128)(2,1)} %bitcast.4), calls=%async_computation | async-start | bytes 2162688 | tf_op jit(solution)/shard_map/all_to_all | solution.py:34
  26.3 49.8 %all-gather.2.cloned.1.call-start = ((), (), s32[]{:S(2)}) async-start(), calls=%async_computation.2 | async-start | bytes 1179648 | tf_op jit(solution)/shard_map/all_gather | solution.py:41
  76.2 41.3 %all-to-all-start.1 = ((bf16[96,11,4,128]{3,2,1,0:T(4,128)(2,1)}), bf16[96,11,4,128]{3,2,1,0:T(4,128)(2,1)S(1)}, u32[]{:S(2)}, u32[]{:S(2)}) async-start(bf16[96,11,4,128]{3,2,1,0:T(4,128)(2,1)} %gather_fusion), calls=%async_computation.1 | async-start | bytes 2162688 | tf_op jit(solution)/shard_map/all_to_all | solution.py:34
  118.3 1.0 copy-start.2
  118.3 1.2 copy-start.3
Sparse Core Ops, SparseCore 0:
  29.6 46.5 all-gather.1

commit v4 on v3

--- a/solution.py
+++ b/solution.py
@@ -42,7 +42,6 @@
 
     pieces = exchange(to_pieces(weights, pseudo_grad, replicas))
     routed = pieces.at[partner].get(mode="promise_in_bounds")
-    routed, gathered = lax.optimization_barrier((routed, gathered))
     partner_weights, partner_grad = lax.optimization_barrier(
         from_pieces(exchange(routed), rows, cols)
     )

time: 128 us -> 130 us (1.016)
  waiting for transfers between devices: 74 us -> 80.5 us
  starting transfers between devices: 26.9 us -> 22.9 us
    all_gather x1, waiting for transfers between devices: 17.8 us -> 50.3 us  [on_device(): gathered = lax.all_gather(key_cotangent, 'fsdp', axis=0, tiled=True)]
    all_to_all x2, waiting for transfers between devices: 55.6 us -> 29.5 us  [exchange(): lax.all_to_all(pieces, 'replica', split_axis=0, concat_axis=0, tiled=True)]
    all_to_all x2, starting transfers between devices: 26.9 us -> 22.8 us  [exchange(): lax.all_to_all(pieces, 'replica', split_axis=0, concat_axis=0, tiled=True)]
  transfers between devices with their start and end apart: 3 -> 3, of which waited for: 3 -> 2; matrix products, arithmetic and copies ran while one was open for 4% -> 2% of each run, Pallas kernels for 0% -> 0%
where the time goes in v4:
time: 130 us
  waiting for transfers between devices  80.5 us (62%)
  starting transfers between devices  22.9 us (18%)
  between operations  14.2 us (11%)
  local copies, waits for them, and re-layouts  6.38 us (5%)
  other arithmetic  3.4 us (3%)
  matrix products  2.75 us (2%)
    all_gather x1, waiting for transfers between devices, on_device(): gathered = lax.all_gather(key_cotangent, 'fsdp', axis=0, tiled=True)  50.3 us
    all_to_all x2, waiting for transfers between devices, exchange(): lax.all_to_all(pieces, 'replica', split_axis=0, concat_axis=0, tiled=True)  29.5 us
    all_to_all x2, starting transfers between devices, exchange(): lax.all_to_all(pieces, 'replica', split_axis=0, concat_axis=0, tiled=True)  22.8 us
    dot_general x1, matrix products, on_device(): lax.dot_general(activations, gathered, contract, preferred_element_type=j...  2.75 us
  transfers between devices with their start and end apart: 3, of which 2 were waited for; matrix products, arithmetic and copies ran while one was open for 2% of the time, Pallas kernels for 0%

profile of v4, /device:TPU:1, one launch (start us, length us, event | category | flops | bytes accessed | tf_op | source)
XLA Modules:
  0.0 130.1 jit_solution(1581950107595607602)
XLA Ops:
  7.2 0.0 copy-start
  7.2 1.3 concatenate.8
  8.5 0.2 copy.11
  8.7 0.1 concatenate.9
  8.8 0.2 copy.12
  9.1 1.8 %maximum_maximum_fusion = bf16[264,4,4,128]{3,1,2,0:T(4,128)(2,1)} fusion(bf16[128,4,4,128]{3,1,2,0:T(4,128)(2,1)S(1)} %copy.12, bf16[128,4,4,128]{3,1,2,0:T(4,128)(2,1)S(1)} %copy.11, bf16[264]{0:T(512)(128)(2,1)S(1)} %pad.2.clone), kind=kLoop, calls=%fused_computation.6 | loop fusion | flops 1081344 | bytes 2130448 | tf_op jit(solution)/shard_map/concatenate | solution.py:20
  10.9 15.5 %all-to-all-start = ((bf16[96,11,4,128]{3,2,1,0:T(4,128)(2,1)}), bf16[96,11,4,128]{3,2,1,0:T(4,128)(2,1)S(1)}, u32[]{:S(2)}, u32[]{:S(2)}) async-start(bf16[96,11,4,128]{3,2,1,0:T(4,128)(2,1)} %bitcast.4), calls=%async_computation | async-start | bytes 2162688 | tf_op jit(solution)/shard_map/all_to_all | solution.py:34
  26.4 29.4 %all-to-all-done = bf16[96,11,4,128]{3,2,1,0:T(4,128)(2,1)S(1)} async-done(((bf16[96,11,4,128]{3,2,1,0:T(4,128)(2,1)}), bf16[96,11,4,128]{3,2,1,0:T(4,128)(2,1)S(1)}, u32[]{:S(2)}, u32[]{:S(2)}) %all-to-all-start) | async-done | bytes 1081376 | tf_op jit(solution)/shard_map/all_to_all | solution.py:34
  55.8 2.6 %gather_fusion = bf16[96,11,4,128]{3,2,1,0:T(4,128)(2,1)} fusion(bf16[96,11,4,128]{3,2,1,0:T(4,128)(2,1)S(1)} %all-to-all-done, s32[1024]{0:T(1024)S(1)} %pad_clamp_fusion), kind=kCustom, calls=%fused_computation | custom fusion | bytes 2163072 | tf_op jit(solution)/shard_map/gather | solution.py:44
  58.4 7.4 %all-to-all-start.1 = ((bf16[96,11,4,128]{3,2,1,0:T(4,128)(2,1)}), bf16[96,11,4,128]{3,2,1,0:T(4,128)(2,1)S(1)}, u32[]{:S(2)}, u32[]{:S(2)}) async-start(bf16[96,11,4,128]{3,2,1,0:T(4,128)(2,1)} %gather_fusion), calls=%async_computation.1 | async-start | bytes 2162688 | tf_op jit(solution)/shard_map/all_to_all | solution.py:34
  65.8 0.0 all-gather.2.cloned.1.call-start
  65.8 0.7 all-gather.2.cloned.1.call-update
  66.5 50.3 %all-gather.2.cloned.1.call-done = bf16[1024,512]{1,0:T(8,128)(2,1)} async-done(((bf16[128,512]{1,0:T(8,128)(2,1)}), bf16[1024,512]{1,0:T(8,128)(2,1)}) %all-gather.2.cloned.1.call-update) | async-done | bytes 1048592 | tf_op jit(solution)/shard_map/all_gather | solution.py:41
  116.9 2.8 %fusion = bf16[1,512,512]{2,1,0:T(8,128)(2,1)} fusion(bf16[1024,512]{1,0:T(8,128)(2,1)S(1)} %copy-done, bf16[1024,512]{1,0:T(8,128)(2,1)} %all-gather.2.cloned.1.call-done), kind=kOutput, calls=%fused_computation.5 | convolution fusion | flops 537133056 | bytes 2621440 | tf_op jit(solution)/shard_map/dot_general | solution.py:62
  119.6 0.0 all-to-all-done.1
  119.6 0.4 slice_bitcast_fusion
  120.0 0.2 copy.13
  120.2 0.2 copy.14
  120.4 0.0 copy-start.2
  120.4 0.0 copy-start.3
  120.5 0.1 copy_bitcast_fusion
  120.6 0.9 copy-done.2
  121.5 0.2 copy-done.3
  121.6 1.6 %convert_bitcast_fusion = (bf16[1,512,512]{2,1,0:T(8,128)(2,1)}, bf16[1,512,512]{2,1,0:T(8,128)(2,1)}) fusion(bf16[512,512]{1,0:T(8,128)(2,1)S(1)} %get-tuple-element.6, bf16[1,512,512]{2,1,0:T(8,128)(2,1)S(1)} %copy-done.2, bf16[512,512]{1,0:T(8,128)(2,1)S(1)} %get-tuple-element.5, bf16[1,512,512]{2,1,0:T(8,128)(2,1)S(1)} %copy-done.1, ...), kind=kLoop, calls=%fused_computation.20 | loop fusion | flops 4980736 | bytes 3670016 | tf_op jit(solution)/shard_map/broadcast_in_dim | solution.py:64
  (9 shorter events, 0.0 us)
Async XLA Ops:
  7.2 109.7 %copy-start = (bf16[1024,512]{1,0:T(8,128)(2,1)S(1)}, bf16[1024,512]{1,0:T(8,128)(2,1)}, u32[]{:S(2)}) copy-start(bf16[1024,512]{1,0:T(8,128)(2,1)} %param.10) | copy-start | bytes 3145732
  7.2 1.5 %copy-start.1 = (bf16[1,512,512]{2,1,0:T(8,128)(2,1)S(1)}, bf16[1,512,512]{2,1,0:T(8,128)(2,1)}, u32[]{:S(2)}) copy-start(bf16[1,512,512]{2,1,0:T(8,128)(2,1)} %param.7) | copy-start | bytes 1572868
  10.9 15.5 %copy-start.4 = (s32[96]{0:T(128)S(1)}, s32[96]{0:T(128)}, u32[]{:S(2)}) copy-start(s32[96]{0:T(128)} %param.9) | copy-start | bytes 1156
  10.9 45.0 %all-to-all-start = ((bf16[96,11,4,128]{3,2,1,0:T(4,128)(2,1)}), bf16[96,11,4,128]{3,2,1,0:T(4,128)(2,1)S(1)}, u32[]{:S(2)}, u32[]{:S(2)}) async-start(bf16[96,11,4,128]{3,2,1,0:T(4,128)(2,1)} %bitcast.4), calls=%async_computation | async-start | bytes 2162688 | tf_op jit(solution)/shard_map/all_to_all | solution.py:34
  58.4 61.2 %all-to-all-start.1 = ((bf16[96,11,4,128]{3,2,1,0:T(4,128)(2,1)}), bf16[96,11,4,128]{3,2,1,0:T(4,128)(2,1)S(1)}, u32[]{:S(2)}, u32[]{:S(2)}) async-start(bf16[96,11,4,128]{3,2,1,0:T(4,128)(2,1)} %gather_fusion), calls=%async_computation.1 | async-start | bytes 2162688 | tf_op jit(solution)/shard_map/all_to_all | solution.py:34
  65.8 51.1 %all-gather.2.cloned.1.call-start = ((), (), s32[]{:S(2)}) async-start(), calls=%async_computation.2 | async-start | bytes 1179648 | tf_op jit(solution)/shard_map/all_gather | solution.py:41
  120.4 1.0 copy-start.2
  120.4 1.2 copy-start.3
Sparse Core Ops, SparseCore 0:
  69.1 47.7 all-gather.1

commit v5 on v4

--- a/solution.py
+++ b/solution.py
@@ -5,6 +5,7 @@
 
 UNIT_ROWS = 4
 UNIT_COLS = 128
+CORES = 2
 
 decay_old = 0.5
 grad_rate = 0.7
@@ -34,14 +35,40 @@
     return lax.all_to_all(pieces, "replica", split_axis=0, concat_axis=0, tiled=True)
 
 
+def same_core_shards(shard):
+    chips = lax.axis_size("fsdp") // CORES
+    here = lax.axis_index("fsdp") // CORES
+    arrived = [shard]
+    for shift in range(1, chips):
+        pairs = [
+            (chip * CORES + core, (chip + shift) % chips * CORES + core)
+            for chip in range(chips)
+            for core in range(CORES)
+        ]
+        arrived.append(lax.ppermute(shard, "fsdp", pairs))
+    order = (here - jnp.arange(chips, dtype=jnp.int32) + chips) % chips
+    return jnp.stack(arrived), order
+
+
+def both_cores_shards(arrived, order):
+    ordered = arrived.at[order].get(mode="promise_in_bounds")
+    shards = lax.axis_size("fsdp")
+    swap = [(i, i ^ 1) for i in range(shards)]
+    other = lax.ppermute(ordered, "fsdp", swap)
+    first = lax.axis_index("fsdp") % CORES == 0
+    pair = (jnp.where(first, ordered, other), jnp.where(first, other, ordered))
+    return jnp.stack(pair, axis=1).reshape(-1, arrived.shape[-1])
+
+
 def on_device(weights, pseudo_grad, momentum, partner, activations, key_cotangent):
     replicas = lax.axis_size("replica")
     weights, pseudo_grad, momentum = weights[0], pseudo_grad[0], momentum[0]
     rows, cols = weights.shape
-    gathered = lax.all_gather(key_cotangent, "fsdp", axis=0, tiled=True)
 
     pieces = exchange(to_pieces(weights, pseudo_grad, replicas))
     routed = pieces.at[partner].get(mode="promise_in_bounds")
+    arrived, order = same_core_shards(key_cotangent)
+    routed, arrived = lax.optimization_barrier((routed, arrived))
     partner_weights, partner_grad = lax.optimization_barrier(
         from_pieces(exchange(routed), rows, cols)
     )
@@ -58,6 +85,7 @@
     new_weights = new_weights.astype(jnp.bfloat16)
     new_momentum = momentum_f.astype(jnp.bfloat16)
 
+    gathered = both_cores_shards(arrived, order)
     contract = (((0,), (0,)), ((), ()))
     grad_f32 = lax.dot_general(activations, gathered, contract, preferred_element_type=jnp.float32)
     weight_grad = grad_f32.astype(jnp.bfloat16)

time: 130 us -> 110 us (0.85)
  the two profiles are of different devices: /device:TPU:1 before, /device:TPU:192 now
where the time goes in v5:
time: 110 us; the launch traced here: 109 us
  starting transfers between devices  53.6 us (49%)
  waiting for transfers between devices  39.7 us (36%)
  local copies, waits for them, and re-layouts  9.02 us (8%)
  other arithmetic  5.5 us (5%)
    all_to_all x2, starting transfers between devices, exchange(): lax.all_to_all(pieces, 'replica', split_axis=0, concat_axis=0, tiled=True)  33.4 us
    all_to_all x2, waiting for transfers between devices, exchange(): lax.all_to_all(pieces, 'replica', split_axis=0, concat_axis=0, tiled=True)  27.1 us
    ppermute x3, starting transfers between devices, same_core_shards(): arrived.append(lax.ppermute(shard, 'fsdp', pairs))  18.3 us
    ppermute x3, waiting for transfers between devices, same_core_shards(): arrived.append(lax.ppermute(shard, 'fsdp', pairs))  10.6 us
    gather x1, local copies, waits for them, and re-layouts, on_device(): routed = pieces.at[partner].get(mode='promise_in_bounds')  2.58 us
  transfers between devices with their start and end apart: 6, of which 4 were waited for; matrix products, arithmetic and copies ran while one was open for 5% of the time, Pallas kernels for 0%

profile of v5, /device:TPU:192, one launch (start us, length us, event | category | flops | bytes accessed | tf_op | source)
XLA Modules:
  0.0 109.4 jit_solution(4807527624597673254)
XLA Ops:
  0.7 1.3 %concatenate.8 = bf16[128,4,4,128]{3,2,1,0:T(4,128)(2,1)S(1)} reshape(bf16[1,512,512]{2,1,0:T(8,128)(2,1)} %param.6) | data formatting | bytes 1048576 | tf_op jit(solution)/shard_map/concatenate | solution.py:21
  1.9 0.2 copy.14
  2.3 0.2 copy.15
  2.5 1.8 %maximum_maximum_fusion = bf16[264,4,4,128]{3,1,2,0:T(4,128)(2,1)} fusion(bf16[128,4,4,128]{3,1,2,0:T(4,128)(2,1)S(1)} %copy.15, bf16[128,4,4,128]{3,1,2,0:T(4,128)(2,1)S(1)} %copy.14, bf16[264]{0:T(512)(128)(2,1)S(1)} %pad.8.clone), kind=kLoop, calls=%fused_computation.7 | loop fusion | flops 1081344 | bytes 2130448 | tf_op jit(solution)/shard_map/concatenate | solution.py:21
  4.3 16.1 %all-to-all-start = ((bf16[96,11,4,128]{3,2,1,0:T(4,128)(2,1)}), bf16[96,11,4,128]{3,2,1,0:T(4,128)(2,1)S(1)}, u32[]{:S(2)}, u32[]{:S(2)}) async-start(bf16[96,11,4,128]{3,2,1,0:T(4,128)(2,1)} %bitcast.4), calls=%async_computation | async-start | bytes 2162688 | tf_op jit(solution)/shard_map/all_to_all | solution.py:35
  20.5 6.7 %collective-permute-start = (bf16[128,512]{1,0:T(8,128)(2,1)S(1)}, bf16[128,512]{1,0:T(8,128)(2,1)S(1)}, u32[]{:S(2)}, u32[]{:S(2)}) collective-permute-start(bf16[128,512]{1,0:T(8,128)(2,1)S(1)} %copy-done.4), channel_id=1, source_target_pairs={{0,2},{1,3},{2,4},{3,5},{4,6},{5,7},{6,0},{7,1},{8,10},{9,11},{10,... | collective-permute-start | bytes 393224 | tf_op jit(solution)/shard_map/ppermute | solution.py:48
  27.2 1.9 %collective-permute-start.2 = (bf16[128,512]{1,0:T(8,128)(2,1)S(1)}, bf16[128,512]{1,0:T(8,128)(2,1)S(1)}, u32[]{:S(2)}, u32[]{:S(2)}) collective-permute-start(bf16[128,512]{1,0:T(8,128)(2,1)S(1)} %copy-done.4), channel_id=1, source_target_pairs={{0,6},{1,7},{2,0},{3,1},{4,2},{5,3},{6,4},{7,5},{8,14},{9,15},{10,... | collective-permute-start | bytes 393224 | tf_op jit(solution)/shard_map/ppermute | solution.py:48
  29.1 9.7 %collective-permute-start.1 = (bf16[128,512]{1,0:T(8,128)(2,1)S(1)}, bf16[128,512]{1,0:T(8,128)(2,1)S(1)}, u32[]{:S(2)}, u32[]{:S(2)}) collective-permute-start(bf16[128,512]{1,0:T(8,128)(2,1)S(1)} %copy-done.4), channel_id=1, source_target_pairs={{0,4},{1,5},{2,6},{3,7},{4,0},{5,1},{6,2},{7,3},{8,12},{9,13},{10,... | collective-permute-start | bytes 393224 | tf_op jit(solution)/shard_map/ppermute | solution.py:48
  38.8 10.5 %collective-permute-done = bf16[128,512]{1,0:T(8,128)(2,1)S(1)} collective-permute-done((bf16[128,512]{1,0:T(8,128)(2,1)S(1)}, bf16[128,512]{1,0:T(8,128)(2,1)S(1)}, u32[]{:S(2)}, u32[]{:S(2)}) %collective-permute-start) | collective-permute-done | bytes 131104 | tf_op jit(solution)/shard_map/ppermute | solution.py:48
  49.4 0.9 pad_maximum_fusion.1
  50.2 6.0 %all-to-all-done = bf16[96,11,4,128]{3,2,1,0:T(4,128)(2,1)S(1)} async-done(((bf16[96,11,4,128]{3,2,1,0:T(4,128)(2,1)}), bf16[96,11,4,128]{3,2,1,0:T(4,128)(2,1)S(1)}, u32[]{:S(2)}, u32[]{:S(2)}) %all-to-all-start) | async-done | bytes 1081376 | tf_op jit(solution)/shard_map/all_to_all | solution.py:35
  56.3 2.6 %gather_fusion = bf16[96,11,4,128]{3,2,1,0:T(4,128)(2,1)} fusion(bf16[96,11,4,128]{3,2,1,0:T(4,128)(2,1)S(1)} %all-to-all-done, s32[1024]{0:T(1024)S(1)} %pad_clamp_fusion.1), kind=kCustom, calls=%fused_computation | custom fusion | bytes 2163072 | tf_op jit(solution)/shard_map/gather | solution.py:69
  58.8 17.3 %all-to-all-start.1 = ((bf16[96,11,4,128]{3,2,1,0:T(4,128)(2,1)}), bf16[96,11,4,128]{3,2,1,0:T(4,128)(2,1)S(1)}, u32[]{:S(2)}, u32[]{:S(2)}) async-start(bf16[96,11,4,128]{3,2,1,0:T(4,128)(2,1)} %gather_fusion), calls=%async_computation.1 | async-start | bytes 2162688 | tf_op jit(solution)/shard_map/all_to_all | solution.py:35
  76.2 1.6 %gather_fusion.1 = bf16[4,128,512]{2,1,0:T(8,128)(2,1)S(1)} fusion(bf16[4,128,512]{2,1,0:T(8,128)(2,1)} %pad_maximum_fusion.1, s32[1024]{0:T(1024)S(1)} %pad_clamp_fusion), kind=kCustom, calls=%fused_computation.1 | custom fusion | bytes 1048592 | tf_op jit(solution)/shard_map/gather | solution.py:54
  77.8 1.9 %collective-permute-start.3 = (bf16[4,128,512]{2,1,0:T(8,128)(2,1)S(1)}, bf16[4,128,512]{2,1,0:T(8,128)(2,1)}, u32[]{:S(2)}, u32[]{:S(2)}) collective-permute-start(bf16[4,128,512]{2,1,0:T(8,128)(2,1)S(1)} %gather_fusion.1), channel_id=1, source_target_pairs={{0,1},{1,0},{2,3},{3,2},{4,5},{5,4},{6,7},{7,6},{8,9},{9,8},{10,11... | collective-permute-start | bytes 1572872 | tf_op jit(solution)/shard_map/ppermute | solution.py:57
  79.7 2.0 %collective-permute-done.3 = bf16[4,128,512]{2,1,0:T(8,128)(2,1)} collective-permute-done((bf16[4,128,512]{2,1,0:T(8,128)(2,1)S(1)}, bf16[4,128,512]{2,1,0:T(8,128)(2,1)}, u32[]{:S(2)}, u32[]{:S(2)}) %collective-permute-start.3) | collective-permute-done | bytes 524320 | tf_op jit(solution)/shard_map/ppermute | solution.py:57
  81.7 1.1 %select_bitcast_fusion.1 = (bf16[4,1,128,512]{3,2,1,0:T(8,128)(2,1)S(1)}, bf16[4,1,128,512]{3,2,1,0:T(8,128)(2,1)S(1)}) fusion(bf16[4,128,512]{2,1,0:T(8,128)(2,1)S(1)} %gather_fusion.1, bf16[4,128,512]{2,1,0:T(8,128)(2,1)} %collective-permute-done.3, pred[]{:T(512)S(6)} %eq.7), kind=kLoop, calls=%fused_computation.24 | loop fusion | flops 524288 | bytes 2097153 | tf_op jit(solution)/shard_map/stack | solution.py:60
  83.0 0.7 fusion
  83.7 1.0 copy.19
  84.7 21.1 %all-to-all-done.1 = bf16[96,11,4,128]{3,2,1,0:T(4,128)(2,1)S(1)} async-done(((bf16[96,11,4,128]{3,2,1,0:T(4,128)(2,1)}), bf16[96,11,4,128]{3,2,1,0:T(4,128)(2,1)S(1)}, u32[]{:S(2)}, u32[]{:S(2)}) %all-to-all-start.1) | async-done | bytes 1081376 | tf_op jit(solution)/shard_map/all_to_all | solution.py:35
  105.8 0.4 slice_bitcast_fusion
  106.2 0.2 copy.17
  106.8 0.9 copy-done.2
  107.8 1.6 %convert_bitcast_fusion = (bf16[1,512,512]{2,1,0:T(8,128)(2,1)}, bf16[1,512,512]{2,1,0:T(8,128)(2,1)}) fusion(bf16[512,512]{1,0:T(8,128)(2,1)S(1)} %get-tuple-element.9, bf16[1,512,512]{2,1,0:T(8,128)(2,1)S(1)} %copy-done.2, bf16[512,512]{1,0:T(8,128)(2,1)S(1)} %get-tuple-element.8, bf16[1,512,512]{2,1,0:T(8,128)(2,1)S(1)} %copy-done.1, ...), kind=kLoop, calls=%fused_computation.25 | loop fusion | flops 4980736 | bytes 3670016 | tf_op jit(solution)/shard_map/broadcast_in_dim | solution.py:92
  (23 shorter events, 0.8 us)
Async XLA Ops:
  0.6 82.3 %copy-start = (bf16[1024,512]{1,0:T(8,128)(2,1)S(1)}, bf16[1024,512]{1,0:T(8,128)(2,1)}, u32[]{:S(2)}) copy-start(bf16[1024,512]{1,0:T(8,128)(2,1)} %param.10) | copy-start | bytes 3145732
  0.6 1.5 %copy-start.1 = (bf16[1,512,512]{2,1,0:T(8,128)(2,1)S(1)}, bf16[1,512,512]{2,1,0:T(8,128)(2,1)}, u32[]{:S(2)}) copy-start(bf16[1,512,512]{2,1,0:T(8,128)(2,1)} %param.7) | copy-start | bytes 1572868
  4.3 16.1 %copy-start.4 = (bf16[128,512]{1,0:T(8,128)(2,1)S(1)}, bf16[128,512]{1,0:T(8,128)(2,1)}, u32[]{:S(2)}) copy-start(bf16[128,512]{1,0:T(8,128)(2,1)} %param.11) | copy-start | bytes 393220
  4.3 34.5 %copy-start.5 = (s32[96]{0:T(128)S(1)}, s32[96]{0:T(128)}, u32[]{:S(2)}) copy-start(s32[96]{0:T(128)} %param.9) | copy-start | bytes 1156
  4.3 51.9 %all-to-all-start = ((bf16[96,11,4,128]{3,2,1,0:T(4,128)(2,1)}), bf16[96,11,4,128]{3,2,1,0:T(4,128)(2,1)S(1)}, u32[]{:S(2)}, u32[]{:S(2)}) async-start(bf16[96,11,4,128]{3,2,1,0:T(4,128)(2,1)} %bitcast.4), calls=%async_computation | async-start | bytes 2162688 | tf_op jit(solution)/shard_map/all_to_all | solution.py:35
  20.5 28.9 %collective-permute-start = (bf16[128,512]{1,0:T(8,128)(2,1)S(1)}, bf16[128,512]{1,0:T(8,128)(2,1)S(1)}, u32[]{:S(2)}, u32[]{:S(2)}) collective-permute-start(bf16[128,512]{1,0:T(8,128)(2,1)S(1)} %copy-done.4), channel_id=1, source_target_pairs={{0,2},{1,3},{2,4},{3,5},{4,6},{5,7},{6,0},{7,1},{8,10},{9,11},{10,... | collective-permute-start | bytes 393224 | tf_op jit(solution)/shard_map/ppermute | solution.py:48
  27.2 22.2 %collective-permute-start.2 = (bf16[128,512]{1,0:T(8,128)(2,1)S(1)}, bf16[128,512]{1,0:T(8,128)(2,1)S(1)}, u32[]{:S(2)}, u32[]{:S(2)}) collective-permute-start(bf16[128,512]{1,0:T(8,128)(2,1)S(1)} %copy-done.4), channel_id=1, source_target_pairs={{0,6},{1,7},{2,0},{3,1},{4,2},{5,3},{6,4},{7,5},{8,14},{9,15},{10,... | collective-permute-start | bytes 393224 | tf_op jit(solution)/shard_map/ppermute | solution.py:48
  29.1 20.3 %collective-permute-start.1 = (bf16[128,512]{1,0:T(8,128)(2,1)S(1)}, bf16[128,512]{1,0:T(8,128)(2,1)S(1)}, u32[]{:S(2)}, u32[]{:S(2)}) collective-permute-start(bf16[128,512]{1,0:T(8,128)(2,1)S(1)} %copy-done.4), channel_id=1, source_target_pairs={{0,4},{1,5},{2,6},{3,7},{4,0},{5,1},{6,2},{7,3},{8,12},{9,13},{10,... | collective-permute-start | bytes 393224 | tf_op jit(solution)/shard_map/ppermute | solution.py:48
  58.8 47.0 %all-to-all-start.1 = ((bf16[96,11,4,128]{3,2,1,0:T(4,128)(2,1)}), bf16[96,11,4,128]{3,2,1,0:T(4,128)(2,1)S(1)}, u32[]{:S(2)}, u32[]{:S(2)}) async-start(bf16[96,11,4,128]{3,2,1,0:T(4,128)(2,1)} %gather_fusion), calls=%async_computation.1 | async-start | bytes 2162688 | tf_op jit(solution)/shard_map/all_to_all | solution.py:35
  77.8 3.9 %collective-permute-start.3 = (bf16[4,128,512]{2,1,0:T(8,128)(2,1)S(1)}, bf16[4,128,512]{2,1,0:T(8,128)(2,1)}, u32[]{:S(2)}, u32[]{:S(2)}) collective-permute-start(bf16[4,128,512]{2,1,0:T(8,128)(2,1)S(1)} %gather_fusion.1), channel_id=1, source_target_pairs={{0,1},{1,0},{2,3},{3,2},{4,5},{5,4},{6,7},{7,6},{8,9},{9,8},{10,11... | collective-permute-start | bytes 1572872 | tf_op jit(solution)/shard_map/ppermute | solution.py:57
  106.6 1.0 copy-start.2
  106.6 1.2 %copy-start.3 = (bf16[1,512,512]{2,1,0:T(8,128)(2,1)S(1)}, bf16[1,512,512]{2,1,0:T(8,128)(2,1)}, u32[]{:S(2)}) copy-start(bf16[1,512,512]{2,1,0:T(8,128)(2,1)} %param.8) | copy-start | bytes 1572868

commit v6 on v4

--- a/solution.py
+++ b/solution.py
@@ -5,6 +5,7 @@
 
 UNIT_ROWS = 4
 UNIT_COLS = 128
+CORES = 2
 
 decay_old = 0.5
 grad_rate = 0.7
@@ -34,14 +35,51 @@
     return lax.all_to_all(pieces, "replica", split_axis=0, concat_axis=0, tiled=True)
 
 
+def core_pairs(chips, shifts):
+    return [
+        (chip * CORES + core, (chip + shifts[core]) % chips * CORES + core)
+        for chip in range(chips)
+        for core in range(CORES)
+    ]
+
+
+def by_core(mine, other):
+    first = lax.axis_index("fsdp") % CORES == 0
+    return jnp.where(first, mine, other), jnp.where(first, other, mine)
+
+
+def swap_cores(array):
+    return lax.ppermute(array, "fsdp", [(i, i ^ 1) for i in range(lax.axis_size("fsdp"))])
+
+
+def chips_shards(shard):
+    chips = lax.axis_size("fsdp") // CORES
+    far = lax.ppermute(shard, "fsdp", core_pairs(chips, (2, 2)))
+    chip = jnp.concatenate(by_core(shard, swap_cores(shard)), axis=0)
+    near = lax.ppermute(chip, "fsdp", core_pairs(chips, (1, chips - 1)))
+    return chip, jnp.concatenate([near, far], axis=0)
+
+
+def all_shards(chip, fetched):
+    tokens = chip.shape[0]
+    chips = lax.axis_size("fsdp") // CORES
+    here = lax.axis_index("fsdp") // CORES
+    even, odd = by_core(fetched, swap_cores(fetched))
+    blocks = (chip, even[:tokens], jnp.concatenate([even[tokens:], odd[tokens:]]), odd[:tokens])
+    order = (here - jnp.arange(chips, dtype=jnp.int32) + chips) % chips
+    ordered = jnp.stack(blocks).at[order].get(mode="promise_in_bounds")
+    return ordered.reshape(-1, chip.shape[-1])
+
+
 def on_device(weights, pseudo_grad, momentum, partner, activations, key_cotangent):
     replicas = lax.axis_size("replica")
     weights, pseudo_grad, momentum = weights[0], pseudo_grad[0], momentum[0]
     rows, cols = weights.shape
-    gathered = lax.all_gather(key_cotangent, "fsdp", axis=0, tiled=True)
 
     pieces = exchange(to_pieces(weights, pseudo_grad, replicas))
     routed = pieces.at[partner].get(mode="promise_in_bounds")
+    chip, fetched = chips_shards(key_cotangent)
+    routed, fetched = lax.optimization_barrier((routed, fetched))
     partner_weights, partner_grad = lax.optimization_barrier(
         from_pieces(exchange(routed), rows, cols)
     )
@@ -58,6 +96,7 @@
     new_weights = new_weights.astype(jnp.bfloat16)
     new_momentum = momentum_f.astype(jnp.bfloat16)
 
+    gathered = all_shards(chip, fetched)
     contract = (((0,), (0,)), ((), ()))
     grad_f32 = lax.dot_general(activations, gathered, contract, preferred_element_type=jnp.float32)
     weight_grad = grad_f32.astype(jnp.bfloat16)

time: 130 us -> 109 us (0.84)
  waiting for transfers between devices: 80.5 us -> 37 us
  starting transfers between devices: 22.9 us -> 55.8 us
  between operations: 14.2 us -> 0.97 us
  local copies, waits for them, and re-layouts: 6.38 us -> 9.21 us
    all_gather x1 -> x0, waiting for transfers between devices: 50.3 us -> none  [on_device(): gathered = lax.all_gather(key_cotangent, 'fsdp', axis=0, tiled=True)]
    ppermute x0 -> x4, starting transfers between devices: none -> 22.9 us  [the longest x1 13.5 us: chips_shards(): far = lax.ppermute(shard, 'fsdp', core_pairs(chips, (2, 2)))]
    ppermute x0 -> x4, waiting for transfers between devices: none -> 18.3 us  [the longest x1 17 us: chips_shards(): far = lax.ppermute(shard, 'fsdp', core_pairs(chips, (2, 2)))]
    all_to_all x2, waiting for transfers between devices: 29.5 us -> 18.8 us  [exchange(): lax.all_to_all(pieces, 'replica', split_axis=0, concat_axis=0, tiled=True)]
    all_to_all x2, starting transfers between devices: 22.8 us -> 32.9 us  [exchange(): lax.all_to_all(pieces, 'replica', split_axis=0, concat_axis=0, tiled=True)]
    gather x0 -> x1, local copies, waits for them, and re-layouts: none -> 1.58 us  [all_shards(): ordered = jnp.stack(blocks).at[order].get(mode='promise_in_bounds')]
  transfers between devices with their start and end apart: 3 -> 6, of which waited for: 2 -> 3; matrix products, arithmetic and copies ran while one was open for 2% -> 5% of each run, Pallas kernels for 0% -> 0%
where the time goes in v6:
time: 109 us
  starting transfers between devices  55.8 us (51%)
  waiting for transfers between devices  37 us (34%)
  local copies, waits for them, and re-layouts  9.21 us (8%)
  other arithmetic  3.74 us (3%)
  matrix products  1.95 us (2%)
    all_to_all x2, starting transfers between devices, exchange(): lax.all_to_all(pieces, 'replica', split_axis=0, concat_axis=0, tiled=True)  32.9 us
    all_to_all x2, waiting for transfers between devices, exchange(): lax.all_to_all(pieces, 'replica', split_axis=0, concat_axis=0, tiled=True)  18.8 us
    ppermute x1, waiting for transfers between devices, chips_shards(): far = lax.ppermute(shard, 'fsdp', core_pairs(chips, (2, 2)))  17 us
    ppermute x1, starting transfers between devices, chips_shards(): far = lax.ppermute(shard, 'fsdp', core_pairs(chips, (2, 2)))  13.5 us
    ppermute x2, starting transfers between devices, swap_cores(): lax.ppermute(array, 'fsdp', [(i, i ^ 1) for i in range(lax.axis_size('fsd...  7.46 us
    gather x1, local copies, waits for them, and re-layouts, on_device(): routed = pieces.at[partner].get(mode='promise_in_bounds')  2.6 us
    unnamed x15, local copies, waits for them, and re-layouts  2.21 us
  transfers between devices with their start and end apart: 6, of which 3 were waited for; matrix products, arithmetic and copies ran while one was open for 5% of the time, Pallas kernels for 0%

profile of v6, /device:TPU:1, one launch (start us, length us, event | category | flops | bytes accessed | tf_op | source)
XLA Modules:
  0.0 108.7 jit_solution(15116086532403436552)
XLA Ops:
  0.7 1.3 %concatenate.17 = bf16[128,4,4,128]{3,2,1,0:T(4,128)(2,1)S(1)} reshape(bf16[1,512,512]{2,1,0:T(8,128)(2,1)} %param.6) | data formatting | bytes 1048576 | tf_op jit(solution)/shard_map/concatenate | solution.py:21
  1.9 0.2 copy.13
  2.3 0.2 copy.14
  2.5 1.8 %maximum_maximum_fusion = bf16[264,4,4,128]{3,1,2,0:T(4,128)(2,1)} fusion(bf16[128,4,4,128]{3,1,2,0:T(4,128)(2,1)S(1)} %copy.14, bf16[128,4,4,128]{3,1,2,0:T(4,128)(2,1)S(1)} %copy.13, bf16[264]{0:T(512)(128)(2,1)S(1)} %pad.12.clone), kind=kLoop, calls=%fused_computation.7 | loop fusion | flops 1081344 | bytes 2130448 | tf_op jit(solution)/shard_map/concatenate | solution.py:21
  4.4 15.5 %all-to-all-start = ((bf16[96,11,4,128]{3,2,1,0:T(4,128)(2,1)}), bf16[96,11,4,128]{3,2,1,0:T(4,128)(2,1)S(1)}, u32[]{:S(2)}, u32[]{:S(2)}) async-start(bf16[96,11,4,128]{3,2,1,0:T(4,128)(2,1)} %bitcast.4), calls=%async_computation | async-start | bytes 2162688 | tf_op jit(solution)/shard_map/all_to_all | solution.py:35
  19.9 3.0 %collective-permute-start = (bf16[128,512]{1,0:T(8,128)(2,1)S(1)}, bf16[128,512]{1,0:T(8,128)(2,1)S(1)}, u32[]{:S(2)}, u32[]{:S(2)}) collective-permute-start(bf16[128,512]{1,0:T(8,128)(2,1)S(1)} %copy-done.5), channel_id=1, source_target_pairs={{0,1},{1,0},{2,3},{3,2},{4,5},{5,4},{6,7},{7,6},{8,9},{9,8},{10,11... | collective-permute-start | bytes 393224 | tf_op jit(solution)/shard_map/ppermute | solution.py:52
  22.9 13.5 %collective-permute-start.2 = (bf16[128,512]{1,0:T(8,128)(2,1)S(1)}, bf16[128,512]{1,0:T(8,128)(2,1)S(1)}, u32[]{:S(2)}, u32[]{:S(2)}) collective-permute-start(bf16[128,512]{1,0:T(8,128)(2,1)S(1)} %copy-done.5), channel_id=1, source_target_pairs={{0,4},{1,5},{2,6},{3,7},{4,0},{5,1},{6,2},{7,3},{8,12},{9,13},{10,... | collective-permute-start | bytes 393224 | tf_op jit(solution)/shard_map/ppermute | solution.py:57
  36.5 1.9 %collective-permute-start.1 = (bf16[256,512]{1,0:T(8,128)(2,1)S(1)}, bf16[256,512]{1,0:T(8,128)(2,1)S(1)}, u32[]{:S(2)}, u32[]{:S(2)}) collective-permute-start(bf16[256,512]{1,0:T(8,128)(2,1)S(1)} %get-tuple-element.27), channel_id=1, source_target_pairs={{0,2},{1,7},{2,4},{3,1},{4,6},{5,3},{6,0},{7,5},{8,10},{9,15},{10,... | collective-permute-start | bytes 786440 | tf_op jit(solution)/shard_map/ppermute | solution.py:59
  38.5 17.0 %collective-permute-done.2 = bf16[128,512]{1,0:T(8,128)(2,1)S(1)} collective-permute-done((bf16[128,512]{1,0:T(8,128)(2,1)S(1)}, bf16[128,512]{1,0:T(8,128)(2,1)S(1)}, u32[]{:S(2)}, u32[]{:S(2)}) %collective-permute-start.2) | collective-permute-done | bytes 131104 | tf_op jit(solution)/shard_map/ppermute | solution.py:57
  55.5 2.6 %gather_fusion = bf16[96,11,4,128]{3,2,1,0:T(4,128)(2,1)} fusion(bf16[96,11,4,128]{3,2,1,0:T(4,128)(2,1)S(1)} %all-to-all-done, s32[1024]{0:T(1024)S(1)} %pad_clamp_fusion.1), kind=kCustom, calls=%fused_computation | custom fusion | bytes 2163072 | tf_op jit(solution)/shard_map/gather | solution.py:80
  58.1 17.5 %all-to-all-start.1 = ((bf16[96,11,4,128]{3,2,1,0:T(4,128)(2,1)}), bf16[96,11,4,128]{3,2,1,0:T(4,128)(2,1)S(1)}, u32[]{:S(2)}, u32[]{:S(2)}) async-start(bf16[96,11,4,128]{3,2,1,0:T(4,128)(2,1)} %gather_fusion), calls=%async_computation.1 | async-start | bytes 2162688 | tf_op jit(solution)/shard_map/all_to_all | solution.py:35
  75.5 4.4 %collective-permute-start.3 = (bf16[384,512]{1,0:T(8,128)(2,1)S(1)}, bf16[384,512]{1,0:T(8,128)(2,1)S(1)}, u32[]{:S(2)}, u32[]{:S(2)}) collective-permute-start(bf16[384,512]{1,0:T(8,128)(2,1)S(1)} %pad_maximum_fusion.1), channel_id=1, source_target_pairs={{0,1},{1,0},{2,3},{3,2},{4,5},{5,4},{6,7},{7,6},{8,9},{9,8},{10,11... | collective-permute-start | bytes 1179656 | tf_op jit(solution)/shard_map/ppermute | solution.py:52
  80.0 1.3 %collective-permute-done.3 = bf16[384,512]{1,0:T(8,128)(2,1)S(1)} collective-permute-done((bf16[384,512]{1,0:T(8,128)(2,1)S(1)}, bf16[384,512]{1,0:T(8,128)(2,1)S(1)}, u32[]{:S(2)}, u32[]{:S(2)}) %collective-permute-start.3) | collective-permute-done | bytes 393248 | tf_op jit(solution)/shard_map/ppermute | solution.py:52
  81.6 1.6 %gather_fusion.1 = bf16[4,256,512]{2,1,0:T(8,128)(2,1)} fusion(bf16[4,256,512]{2,1,0:T(8,128)(2,1)S(1)} %pad_maximum_fusion, s32[1024]{0:T(1024)S(1)} %pad_clamp_fusion), kind=kCustom, calls=%fused_computation.1 | custom fusion | bytes 2097168 | tf_op jit(solution)/shard_map/gather | solution.py:70
  83.2 2.0 %fusion = bf16[1,512,512]{1,2,0:T(8,128)(2,1)S(1)} fusion(bf16[1024,512]{1,0:T(8,128)(2,1)} %bitcast.64, bf16[1024,512]{1,0:T(8,128)(2,1)S(1)} %copy-done), kind=kOutput, calls=%fused_computation.6 | convolution fusion | flops 537133056 | bytes 2621440 | tf_op jit(solution)/shard_map/dot_general | solution.py:101
  85.1 1.0 copy.17
  86.2 18.8 %all-to-all-done.1 = bf16[96,11,4,128]{3,2,1,0:T(4,128)(2,1)S(1)} async-done(((bf16[96,11,4,128]{3,2,1,0:T(4,128)(2,1)}), bf16[96,11,4,128]{3,2,1,0:T(4,128)(2,1)S(1)}, u32[]{:S(2)}, u32[]{:S(2)}) %all-to-all-start.1) | async-done | bytes 1081376 | tf_op jit(solution)/shard_map/all_to_all | solution.py:35
  104.9 0.4 slice_bitcast_fusion
  105.3 0.2 copy.16
  105.5 0.2 copy.15
  105.9 0.9 copy-done.2
  106.8 0.2 copy-done.3
  106.9 0.2 copy-done.4
  107.1 1.6 %convert_bitcast_fusion = (bf16[1,512,512]{2,1,0:T(8,128)(2,1)}, bf16[1,512,512]{2,1,0:T(8,128)(2,1)}) fusion(bf16[512,512]{1,0:T(8,128)(2,1)S(1)} %get-tuple-element.9, bf16[1,512,512]{2,1,0:T(8,128)(2,1)S(1)} %copy-done.3, bf16[512,512]{1,0:T(8,128)(2,1)S(1)} %get-tuple-element.8, bf16[1,512,512]{2,1,0:T(8,128)(2,1)S(1)} %copy-done.2, ...), kind=kLoop, calls=%fused_computation.22 | loop fusion | flops 4980736 | bytes 3670016 | tf_op jit(solution)/shard_map/broadcast_in_dim | solution.py:103
  (31 shorter events, 0.7 us)
Async XLA Ops:
  0.6 82.6 %copy-start = (bf16[1024,512]{1,0:T(8,128)(2,1)S(1)}, bf16[1024,512]{1,0:T(8,128)(2,1)}, u32[]{:S(2)}) copy-start(bf16[1024,512]{1,0:T(8,128)(2,1)} %param.10) | copy-start | bytes 3145732
  0.6 1.5 %copy-start.1 = (bf16[1,512,512]{2,1,0:T(8,128)(2,1)S(1)}, bf16[1,512,512]{2,1,0:T(8,128)(2,1)}, u32[]{:S(2)}) copy-start(bf16[1,512,512]{2,1,0:T(8,128)(2,1)} %param.7) | copy-start | bytes 1572868
  4.4 15.5 %copy-start.5 = (bf16[128,512]{1,0:T(8,128)(2,1)S(1)}, bf16[128,512]{1,0:T(8,128)(2,1)}, u32[]{:S(2)}) copy-start(bf16[128,512]{1,0:T(8,128)(2,1)} %param.11) | copy-start | bytes 393220
  4.4 51.1 %all-to-all-start = ((bf16[96,11,4,128]{3,2,1,0:T(4,128)(2,1)}), bf16[96,11,4,128]{3,2,1,0:T(4,128)(2,1)S(1)}, u32[]{:S(2)}, u32[]{:S(2)}) async-start(bf16[96,11,4,128]{3,2,1,0:T(4,128)(2,1)} %bitcast.4), calls=%async_computation | async-start | bytes 2162688 | tf_op jit(solution)/shard_map/all_to_all | solution.py:35
  19.8 18.6 %copy-start.6 = (s32[96]{0:T(128)S(1)}, s32[96]{0:T(128)}, u32[]{:S(2)}) copy-start(s32[96]{0:T(128)} %param.9) | copy-start | bytes 1156
  19.9 16.6 %collective-permute-start = (bf16[128,512]{1,0:T(8,128)(2,1)S(1)}, bf16[128,512]{1,0:T(8,128)(2,1)S(1)}, u32[]{:S(2)}, u32[]{:S(2)}) collective-permute-start(bf16[128,512]{1,0:T(8,128)(2,1)S(1)} %copy-done.5), channel_id=1, source_target_pairs={{0,1},{1,0},{2,3},{3,2},{4,5},{5,4},{6,7},{7,6},{8,9},{9,8},{10,11... | collective-permute-start | bytes 393224 | tf_op jit(solution)/shard_map/ppermute | solution.py:52
  22.9 32.5 %collective-permute-start.2 = (bf16[128,512]{1,0:T(8,128)(2,1)S(1)}, bf16[128,512]{1,0:T(8,128)(2,1)S(1)}, u32[]{:S(2)}, u32[]{:S(2)}) collective-permute-start(bf16[128,512]{1,0:T(8,128)(2,1)S(1)} %copy-done.5), channel_id=1, source_target_pairs={{0,4},{1,5},{2,6},{3,7},{4,0},{5,1},{6,2},{7,3},{8,12},{9,13},{10,... | collective-permute-start | bytes 393224 | tf_op jit(solution)/shard_map/ppermute | solution.py:57
  36.5 18.9 %collective-permute-start.1 = (bf16[256,512]{1,0:T(8,128)(2,1)S(1)}, bf16[256,512]{1,0:T(8,128)(2,1)S(1)}, u32[]{:S(2)}, u32[]{:S(2)}) collective-permute-start(bf16[256,512]{1,0:T(8,128)(2,1)S(1)} %get-tuple-element.27), channel_id=1, source_target_pairs={{0,2},{1,7},{2,4},{3,1},{4,6},{5,3},{6,0},{7,5},{8,10},{9,15},{10,... | collective-permute-start | bytes 786440 | tf_op jit(solution)/shard_map/ppermute | solution.py:59
  58.1 46.9 %all-to-all-start.1 = ((bf16[96,11,4,128]{3,2,1,0:T(4,128)(2,1)}), bf16[96,11,4,128]{3,2,1,0:T(4,128)(2,1)S(1)}, u32[]{:S(2)}, u32[]{:S(2)}) async-start(bf16[96,11,4,128]{3,2,1,0:T(4,128)(2,1)} %gather_fusion), calls=%async_computation.1 | async-start | bytes 2162688 | tf_op jit(solution)/shard_map/all_to_all | solution.py:35
  75.5 5.7 %collective-permute-start.3 = (bf16[384,512]{1,0:T(8,128)(2,1)S(1)}, bf16[384,512]{1,0:T(8,128)(2,1)S(1)}, u32[]{:S(2)}, u32[]{:S(2)}) collective-permute-start(bf16[384,512]{1,0:T(8,128)(2,1)S(1)} %pad_maximum_fusion.1), channel_id=1, source_target_pairs={{0,1},{1,0},{2,3},{3,2},{4,5},{5,4},{6,7},{7,6},{8,9},{9,8},{10,11... | collective-permute-start | bytes 1179656 | tf_op jit(solution)/shard_map/ppermute | solution.py:52
  105.7 1.0 copy-start.2
  105.7 1.2 %copy-start.3 = (bf16[1,512,512]{2,1,0:T(8,128)(2,1)S(1)}, bf16[1,512,512]{2,1,0:T(8,128)(2,1)}, u32[]{:S(2)}) copy-start(bf16[1,512,512]{2,1,0:T(8,128)(2,1)} %param.6) | copy-start | bytes 1572868
  105.8 1.3 %copy-start.4 = (bf16[1,512,512]{2,1,0:T(8,128)(2,1)S(1)}, bf16[1,512,512]{2,1,0:T(8,128)(2,1)}, u32[]{:S(2)}) copy-start(bf16[1,512,512]{2,1,0:T(8,128)(2,1)} %param.8) | copy-start | bytes 1572868

commit v7 on v6

--- a/solution.py
+++ b/solution.py
@@ -1,6 +1,8 @@
 import jax
 import jax.numpy as jnp
 from jax import lax
+from jax.experimental import pallas as pl
+from jax.experimental.pallas import tpu as pltpu
 from jax.sharding import PartitionSpec as P
 
 UNIT_ROWS = 4
@@ -18,7 +20,10 @@
     wide = cols // UNIT_COLS
     per_piece = -(-2 * rows // UNIT_ROWS * wide // count)
     spare = (per_piece * count - 2 * rows // UNIT_ROWS * wide) // wide
-    joined = jnp.concatenate([*quads, jnp.zeros((spare, UNIT_ROWS, cols), first.dtype)], axis=0)
+    total = 2 * rows // UNIT_ROWS + spare
+    joined = jnp.zeros((total, UNIT_ROWS, cols), first.dtype)
+    for i, q in enumerate(quads):
+        joined = lax.dynamic_update_slice(joined, q, (i * rows // UNIT_ROWS, 0, 0))
     cut = joined.reshape(-1, UNIT_ROWS, wide, UNIT_COLS).transpose(0, 2, 1, 3)
     return cut.reshape(count, per_piece, UNIT_ROWS, UNIT_COLS)
 
@@ -33,6 +38,33 @@
 
 def exchange(pieces):
     return lax.all_to_all(pieces, "replica", split_axis=0, concat_axis=0, tiled=True)
+
+
+def route_body(partner_ref, pieces_ref, routed_ref, sem):
+    def start(i, carry):
+        source = pieces_ref.at[partner_ref[i]]
+        pltpu.make_async_copy(source, routed_ref.at[i], sem).start()
+        return carry
+
+    lax.fori_loop(0, routed_ref.shape[0], start, 0, unroll=8)
+    pltpu.make_async_copy(pieces_ref, routed_ref, sem).wait()
+
+
+def route(pieces, partner):
+    return pl.pallas_call(
+        route_body,
+        out_shape=jax.ShapeDtypeStruct(pieces.shape, pieces.dtype),
+        in_specs=[
+            pl.BlockSpec(memory_space=pltpu.SMEM),
+            pl.BlockSpec(memory_space=pl.ANY),
+        ],
+        out_specs=pl.BlockSpec(memory_space=pl.ANY),
+        scratch_shapes=[pltpu.SemaphoreType.DMA],
+        compiler_params=pltpu.CompilerParams(vmem_limit_bytes=1 << 20),
+        cost_estimate=pl.CostEstimate(
+            flops=0, bytes_accessed=2 * pieces.size * pieces.dtype.itemsize, transcendentals=0
+        ),
+    )(partner, pieces)
 
 
 def core_pairs(chips, shifts):
@@ -77,7 +109,7 @@
     rows, cols = weights.shape
 
     pieces = exchange(to_pieces(weights, pseudo_grad, replicas))
-    routed = pieces.at[partner].get(mode="promise_in_bounds")
+    routed = route(pieces, partner)
     chip, fetched = chips_shards(key_cotangent)
     routed, fetched = lax.optimization_barrier((routed, fetched))
     partner_weights, partner_grad = lax.optimization_barrier(

time: 109 us -> 109 us (level)
  the two profiles are of different devices: /device:TPU:1 before, /device:TPU:192 now
where the time goes in v7:
time: 109 us
  starting transfers between devices  47.3 us (43%)
  waiting for transfers between devices  46.7 us (43%)
  local copies, waits for them, and re-layouts  8.5 us (8%)
  matrix products  1.95 us (2%)
  other arithmetic  1.92 us (2%)
  Pallas kernels  1.57 us (1%)
    all_to_all x2, starting transfers between devices, exchange(): lax.all_to_all(pieces, 'replica', split_axis=0, concat_axis=0, tiled=True)  32 us
    all_to_all x2, waiting for transfers between devices, exchange(): lax.all_to_all(pieces, 'replica', split_axis=0, concat_axis=0, tiled=True)  28.4 us
    ppermute x1, waiting for transfers between devices, chips_shards(): far = lax.ppermute(shard, 'fsdp', core_pairs(chips, (2, 2)))  9.07 us
    ppermute x1, starting transfers between devices, chips_shards(): near = lax.ppermute(chip, 'fsdp', core_pairs(chips, (1, chips - 1)))  6.7 us
    ppermute x1, waiting for transfers between devices, chips_shards(): near = lax.ppermute(chip, 'fsdp', core_pairs(chips, (1, chips - 1)))  6.41 us
    ppermute x1, starting transfers between devices, chips_shards(): far = lax.ppermute(shard, 'fsdp', core_pairs(chips, (2, 2)))  4.65 us
    ppermute x2, starting transfers between devices, swap_cores(): lax.ppermute(array, 'fsdp', [(i, i ^ 1) for i in range(lax.axis_size('fsd...  4 us
    ppermute x2, waiting for transfers between devices, swap_cores(): lax.ppermute(array, 'fsdp', [(i, i ^ 1) for i in range(lax.axis_size('fsd...  2.78 us
  transfers between devices with their start and end apart: 6, of which 6 were waited for; matrix products, arithmetic and copies ran while one was open for 5% of the time, Pallas kernels for 0%

profile of v7, /device:TPU:192, one launch (start us, length us, event | category | flops | bytes accessed | tf_op | source)
XLA Modules:
  0.0 108.9 jit_solution(7499786001627648406)
XLA Ops:
  0.7 1.3 %reshape_squeeze.6 = bf16[128,4,512]{2,1,0:T(4,128)(2,1)S(1)} reshape(bf16[1,512,512]{2,1,0:T(8,128)(2,1)} %param.6) | data formatting | bytes 1048576 | tf_op jit(solution)/shard_map/reshape;squeeze | solution.py:19
  2.1 1.3 %dynamic_update_slice.6 = bf16[264,4,512]{2,1,0:T(4,128)(2,1)} pad(bf16[128,4,512]{2,1,0:T(4,128)(2,1)S(1)} %reshape_squeeze.6, bf16[]{:T(256)} %constant.47.clone.1), padding=0_136x0_0x0_0 | pad | bytes 1605634 | tf_op jit(solution)/shard_map/dynamic_update_slice | solution.py:26
  3.4 1.0 constant_dynamic-update-slice_fusion
  4.4 16.1 %all-to-all-start = ((bf16[96,11,4,128]{3,2,1,0:T(4,128)(2,1)}), bf16[96,11,4,128]{3,2,1,0:T(4,128)(2,1)S(1)}, u32[]{:S(2)}, u32[]{:S(2)}) async-start(bf16[96,11,4,128]{3,2,1,0:T(4,128)(2,1)} %bitcast.5), calls=%async_computation | async-start | bytes 2162688 | tf_op jit(solution)/shard_map/all_to_all | solution.py:40
  20.6 1.9 %collective-permute-start = (bf16[128,512]{1,0:T(8,128)(2,1)S(1)}, bf16[128,512]{1,0:T(8,128)(2,1)S(1)}, u32[]{:S(2)}, u32[]{:S(2)}) collective-permute-start(bf16[128,512]{1,0:T(8,128)(2,1)S(1)} %copy-done.6), channel_id=1, source_target_pairs={{0,1},{1,0},{2,3},{3,2},{4,5},{5,4},{6,7},{7,6},{8,9},{9,8},{10,11... | collective-permute-start | bytes 393224 | tf_op jit(solution)/shard_map/ppermute | solution.py:84
  22.5 1.3 %collective-permute-done = bf16[128,512]{1,0:T(8,128)(2,1)S(1)} collective-permute-done((bf16[128,512]{1,0:T(8,128)(2,1)S(1)}, bf16[128,512]{1,0:T(8,128)(2,1)S(1)}, u32[]{:S(2)}, u32[]{:S(2)}) %collective-permute-start) | collective-permute-done | bytes 131104 | tf_op jit(solution)/shard_map/ppermute | solution.py:84
  23.9 6.7 %collective-permute-start.1 = (bf16[256,512]{1,0:T(8,128)(2,1)S(1)}, bf16[256,512]{1,0:T(8,128)(2,1)S(1)}, u32[]{:S(2)}, u32[]{:S(2)}) collective-permute-start(bf16[256,512]{1,0:T(8,128)(2,1)S(1)} %get-tuple-element.21), channel_id=1, source_target_pairs={{0,2},{1,7},{2,4},{3,1},{4,6},{5,3},{6,0},{7,5},{8,10},{9,15},{10,... | collective-permute-start | bytes 786440 | tf_op jit(solution)/shard_map/ppermute | solution.py:91
  30.6 4.6 %collective-permute-start.2 = (bf16[128,512]{1,0:T(8,128)(2,1)S(1)}, bf16[128,512]{1,0:T(8,128)(2,1)S(1)}, u32[]{:S(2)}, u32[]{:S(2)}) collective-permute-start(bf16[128,512]{1,0:T(8,128)(2,1)S(1)} %copy-done.6), channel_id=1, source_target_pairs={{0,4},{1,5},{2,6},{3,7},{4,0},{5,1},{6,2},{7,3},{8,12},{9,13},{10,... | collective-permute-start | bytes 393224 | tf_op jit(solution)/shard_map/ppermute | solution.py:89
  35.2 9.1 %collective-permute-done.2 = bf16[128,512]{1,0:T(8,128)(2,1)S(1)} collective-permute-done((bf16[128,512]{1,0:T(8,128)(2,1)S(1)}, bf16[128,512]{1,0:T(8,128)(2,1)S(1)}, u32[]{:S(2)}, u32[]{:S(2)}) %collective-permute-start.2) | collective-permute-done | bytes 131104 | tf_op jit(solution)/shard_map/ppermute | solution.py:89
  44.3 6.4 %collective-permute-done.1 = bf16[256,512]{1,0:T(8,128)(2,1)S(1)} collective-permute-done((bf16[256,512]{1,0:T(8,128)(2,1)S(1)}, bf16[256,512]{1,0:T(8,128)(2,1)S(1)}, u32[]{:S(2)}, u32[]{:S(2)}) %collective-permute-start.1) | collective-permute-done | bytes 262176 | tf_op jit(solution)/shard_map/ppermute | solution.py:91
  50.8 5.6 %all-to-all-done.pieces_ref = bf16[96,11,4,128]{3,2,1,0:T(4,128)(2,1)S(1)} async-done(((bf16[96,11,4,128]{3,2,1,0:T(4,128)(2,1)}), bf16[96,11,4,128]{3,2,1,0:T(4,128)(2,1)S(1)}, u32[]{:S(2)}, u32[]{:S(2)}) %all-to-all-start) | async-done | bytes 1081376 | tf_op jit(solution)/shard_map/all_to_all | solution.py:40
  56.3 1.6 %shard_map.85 = bf16[96,11,4,128]{3,2,1,0:T(4,128)(2,1)} custom-call(s32[96]{0:T(128)S(1)} %copy-done.1, bf16[96,11,4,128]{3,2,1,0:T(4,128)(2,1)S(1)} %all-to-all-done.pieces_ref), custom_call_target="tpu_custom_call" | custom-call | bytes 2162688 | tf_op jit(solution)/shard_map/pallas_call | solution.py:54
  57.9 15.8 %all-to-all-start.1 = ((bf16[96,11,4,128]{3,2,1,0:T(4,128)(2,1)}), bf16[96,11,4,128]{3,2,1,0:T(4,128)(2,1)S(1)}, u32[]{:S(2)}, u32[]{:S(2)}) async-start(bf16[96,11,4,128]{3,2,1,0:T(4,128)(2,1)} %shard_map.85), calls=%async_computation.1 | async-start | bytes 2162688 | tf_op jit(solution)/shard_map/all_to_all | solution.py:40
  73.8 2.1 %collective-permute-start.3 = (bf16[384,512]{1,0:T(8,128)(2,1)S(1)}, bf16[384,512]{1,0:T(8,128)(2,1)S(1)}, u32[]{:S(2)}, u32[]{:S(2)}) collective-permute-start(bf16[384,512]{1,0:T(8,128)(2,1)S(1)} %pad_maximum_fusion.1), channel_id=1, source_target_pairs={{0,1},{1,0},{2,3},{3,2},{4,5},{5,4},{6,7},{7,6},{8,9},{9,8},{10,11... | collective-permute-start | bytes 1179656 | tf_op jit(solution)/shard_map/ppermute | solution.py:84
  75.9 1.5 %collective-permute-done.3 = bf16[384,512]{1,0:T(8,128)(2,1)S(1)} collective-permute-done((bf16[384,512]{1,0:T(8,128)(2,1)S(1)}, bf16[384,512]{1,0:T(8,128)(2,1)S(1)}, u32[]{:S(2)}, u32[]{:S(2)}) %collective-permute-start.3) | collective-permute-done | bytes 393248 | tf_op jit(solution)/shard_map/ppermute | solution.py:84
  77.7 1.6 %gather_fusion = bf16[4,256,512]{2,1,0:T(8,128)(2,1)} fusion(bf16[4,256,512]{2,1,0:T(8,128)(2,1)S(1)} %pad_maximum_fusion, s32[1024]{0:T(1024)S(1)} %pad_clamp_fusion), kind=kCustom, calls=%fused_computation | custom fusion | bytes 2097168 | tf_op jit(solution)/shard_map/gather | solution.py:102
  79.3 2.0 %fusion = bf16[1,512,512]{1,2,0:T(8,128)(2,1)S(1)} fusion(bf16[1024,512]{1,0:T(8,128)(2,1)} %bitcast.66, bf16[1024,512]{1,0:T(8,128)(2,1)S(1)} %copy-done), kind=kOutput, calls=%fused_computation.5 | convolution fusion | flops 537133056 | bytes 2621440 | tf_op jit(solution)/shard_map/dot_general | solution.py:133
  81.2 1.0 copy.11
  82.2 22.8 %all-to-all-done.1 = bf16[96,11,4,128]{3,2,1,0:T(4,128)(2,1)S(1)} async-done(((bf16[96,11,4,128]{3,2,1,0:T(4,128)(2,1)}), bf16[96,11,4,128]{3,2,1,0:T(4,128)(2,1)S(1)}, u32[]{:S(2)}, u32[]{:S(2)}) %all-to-all-start.1) | async-done | bytes 1081376 | tf_op jit(solution)/shard_map/all_to_all | solution.py:40
  105.1 0.4 slice_bitcast_fusion
  105.4 0.2 copy.10
  105.7 0.2 copy.9
  106.1 0.9 copy-done.2
  107.2 1.6 %convert_bitcast_fusion = (bf16[1,512,512]{2,1,0:T(8,128)(2,1)}, bf16[1,512,512]{2,1,0:T(8,128)(2,1)}) fusion(bf16[512,512]{1,0:T(8,128)(2,1)S(1)} %get-tuple-element.9, bf16[1,512,512]{2,1,0:T(8,128)(2,1)S(1)} %copy-done.2, bf16[512,512]{1,0:T(8,128)(2,1)S(1)} %get-tuple-element.8, bf16[1,512,512]{2,1,0:T(8,128)(2,1)S(1)} %copy-done.4, ...), kind=kLoop, calls=%fused_computation.20 | loop fusion | flops 4980736 | bytes 3670016 | tf_op jit(solution)/shard_map/broadcast_in_dim | solution.py:135
  (26 shorter events, 1.0 us)
Async XLA Ops:
  0.6 78.6 %copy-start = (bf16[1024,512]{1,0:T(8,128)(2,1)S(1)}, bf16[1024,512]{1,0:T(8,128)(2,1)}, u32[]{:S(2)}) copy-start(bf16[1024,512]{1,0:T(8,128)(2,1)} %param.10) | copy-start | bytes 3145732
  0.6 1.3 %copy-start.3 = (bf16[1,512,512]{2,1,0:T(8,128)(2,1)S(1)}, bf16[1,512,512]{2,1,0:T(8,128)(2,1)}, u32[]{:S(2)}) copy-start(bf16[1,512,512]{2,1,0:T(8,128)(2,1)} %param.7) | copy-start | bytes 1572868
  4.4 16.1 %copy-start.6 = (bf16[128,512]{1,0:T(8,128)(2,1)S(1)}, bf16[128,512]{1,0:T(8,128)(2,1)}, u32[]{:S(2)}) copy-start(bf16[128,512]{1,0:T(8,128)(2,1)} %param.11) | copy-start | bytes 393220
  4.4 51.9 %all-to-all-start = ((bf16[96,11,4,128]{3,2,1,0:T(4,128)(2,1)}), bf16[96,11,4,128]{3,2,1,0:T(4,128)(2,1)S(1)}, u32[]{:S(2)}, u32[]{:S(2)}) async-start(bf16[96,11,4,128]{3,2,1,0:T(4,128)(2,1)} %bitcast.5), calls=%async_computation | async-start | bytes 2162688 | tf_op jit(solution)/shard_map/all_to_all | solution.py:40
  20.6 35.8 %copy-start.1 = (s32[96]{0:T(128)S(1)}, s32[96]{0:T(128)}, u32[]{:S(2)}) copy-start(s32[96]{0:T(128)} %partner_ref.1) | copy-start | bytes 1156
  20.6 3.2 %collective-permute-start = (bf16[128,512]{1,0:T(8,128)(2,1)S(1)}, bf16[128,512]{1,0:T(8,128)(2,1)S(1)}, u32[]{:S(2)}, u32[]{:S(2)}) collective-permute-start(bf16[128,512]{1,0:T(8,128)(2,1)S(1)} %copy-done.6), channel_id=1, source_target_pairs={{0,1},{1,0},{2,3},{3,2},{4,5},{5,4},{6,7},{7,6},{8,9},{9,8},{10,11... | collective-permute-start | bytes 393224 | tf_op jit(solution)/shard_map/ppermute | solution.py:84
  23.9 26.8 %collective-permute-start.1 = (bf16[256,512]{1,0:T(8,128)(2,1)S(1)}, bf16[256,512]{1,0:T(8,128)(2,1)S(1)}, u32[]{:S(2)}, u32[]{:S(2)}) collective-permute-start(bf16[256,512]{1,0:T(8,128)(2,1)S(1)} %get-tuple-element.21), channel_id=1, source_target_pairs={{0,2},{1,7},{2,4},{3,1},{4,6},{5,3},{6,0},{7,5},{8,10},{9,15},{10,... | collective-permute-start | bytes 786440 | tf_op jit(solution)/shard_map/ppermute | solution.py:91
  30.6 13.7 %collective-permute-start.2 = (bf16[128,512]{1,0:T(8,128)(2,1)S(1)}, bf16[128,512]{1,0:T(8,128)(2,1)S(1)}, u32[]{:S(2)}, u32[]{:S(2)}) collective-permute-start(bf16[128,512]{1,0:T(8,128)(2,1)S(1)} %copy-done.6), channel_id=1, source_target_pairs={{0,4},{1,5},{2,6},{3,7},{4,0},{5,1},{6,2},{7,3},{8,12},{9,13},{10,... | collective-permute-start | bytes 393224 | tf_op jit(solution)/shard_map/ppermute | solution.py:89
  57.9 47.2 %all-to-all-start.1 = ((bf16[96,11,4,128]{3,2,1,0:T(4,128)(2,1)}), bf16[96,11,4,128]{3,2,1,0:T(4,128)(2,1)S(1)}, u32[]{:S(2)}, u32[]{:S(2)}) async-start(bf16[96,11,4,128]{3,2,1,0:T(4,128)(2,1)} %shard_map.85), calls=%async_computation.1 | async-start | bytes 2162688 | tf_op jit(solution)/shard_map/all_to_all | solution.py:40
  73.8 3.6 %collective-permute-start.3 = (bf16[384,512]{1,0:T(8,128)(2,1)S(1)}, bf16[384,512]{1,0:T(8,128)(2,1)S(1)}, u32[]{:S(2)}, u32[]{:S(2)}) collective-permute-start(bf16[384,512]{1,0:T(8,128)(2,1)S(1)} %pad_maximum_fusion.1), channel_id=1, source_target_pairs={{0,1},{1,0},{2,3},{3,2},{4,5},{5,4},{6,7},{7,6},{8,9},{9,8},{10,11... | collective-permute-start | bytes 1179656 | tf_op jit(solution)/shard_map/ppermute | solution.py:84
  105.9 1.0 copy-start.2
  105.9 1.2 %copy-start.4 = (bf16[1,512,512]{2,1,0:T(8,128)(2,1)S(1)}, bf16[1,512,512]{2,1,0:T(8,128)(2,1)}, u32[]{:S(2)}) copy-start(bf16[1,512,512]{2,1,0:T(8,128)(2,1)} %param.7) | copy-start | bytes 1572868
  105.9 1.3 %copy-start.5 = (bf16[1,512,512]{2,1,0:T(8,128)(2,1)S(1)}, bf16[1,512,512]{2,1,0:T(8,128)(2,1)}, u32[]{:S(2)}) copy-start(bf16[1,512,512]{2,1,0:T(8,128)(2,1)} %param.8) | copy-start | bytes 1572868

commit v8 on v7

--- a/solution.py
+++ b/solution.py
@@ -3,15 +3,45 @@
 from jax import lax
 from jax.experimental import pallas as pl
 from jax.experimental.pallas import tpu as pltpu
+from jax.sharding import Mesh
 from jax.sharding import PartitionSpec as P
 
 UNIT_ROWS = 4
 UNIT_COLS = 128
 CORES = 2
+LAYERS = 3
+RANKS = ("layer", "column")
 
 decay_old = 0.5
 grad_rate = 0.7
 pull_rate = 0.9
+
+
+def join_body(first_ref, second_ref, joined_ref, sems):
+    half = first_ref.shape[0]
+    spare = joined_ref.shape[0] - 2 * half
+    copies = (
+        (first_ref, joined_ref.at[pl.ds(0, half)]),
+        (second_ref, joined_ref.at[pl.ds(half, half)]),
+        (first_ref.at[pl.ds(0, spare)], joined_ref.at[pl.ds(2 * half, spare)]),
+    )
+    started = [pltpu.make_async_copy(a, b, sems.at[i]) for i, (a, b) in enumerate(copies)]
+    for copy in started:
+        copy.start()
+    for copy in started:
+        copy.wait()
+
+
+def join(first, second, spare):
+    shape = (2 * first.shape[0] + spare, *first.shape[1:])
+    return pl.pallas_call(
+        join_body,
+        out_shape=jax.ShapeDtypeStruct(shape, first.dtype),
+        in_specs=[pl.BlockSpec(memory_space=pl.ANY)] * 2,
+        out_specs=pl.BlockSpec(memory_space=pl.ANY),
+        scratch_shapes=[pltpu.SemaphoreType.DMA((3,))],
+        compiler_params=pltpu.CompilerParams(vmem_limit_bytes=1 << 20),
+    )(first, second)
 
 
 def to_pieces(first, second, count):
@@ -20,10 +50,7 @@
     wide = cols // UNIT_COLS
     per_piece = -(-2 * rows // UNIT_ROWS * wide // count)
     spare = (per_piece * count - 2 * rows // UNIT_ROWS * wide) // wide
-    total = 2 * rows // UNIT_ROWS + spare
-    joined = jnp.zeros((total, UNIT_ROWS, cols), first.dtype)
-    for i, q in enumerate(quads):
-        joined = lax.dynamic_update_slice(joined, q, (i * rows // UNIT_ROWS, 0, 0))
+    joined = join(*quads, spare)
     cut = joined.reshape(-1, UNIT_ROWS, wide, UNIT_COLS).transpose(0, 2, 1, 3)
     return cut.reshape(count, per_piece, UNIT_ROWS, UNIT_COLS)
 
@@ -37,7 +64,7 @@
 
 
 def exchange(pieces):
-    return lax.all_to_all(pieces, "replica", split_axis=0, concat_axis=0, tiled=True)
+    return lax.all_to_all(pieces, RANKS, split_axis=0, concat_axis=0, tiled=True)
 
 
 def route_body(partner_ref, pieces_ref, routed_ref, sem):
@@ -104,12 +131,14 @@
 
 
 def on_device(weights, pseudo_grad, momentum, partner, activations, key_cotangent):
-    replicas = lax.axis_size("replica")
+    columns = lax.axis_size("column")
+    replicas = columns * LAYERS
     weights, pseudo_grad, momentum = weights[0], pseudo_grad[0], momentum[0]
     rows, cols = weights.shape
 
     pieces = exchange(to_pieces(weights, pseudo_grad, replicas))
-    routed = route(pieces, partner)
+    by_rank = partner.reshape(columns, LAYERS).T.reshape(-1)
+    routed = route(pieces, by_rank % LAYERS * columns + by_rank // LAYERS)
     chip, fetched = chips_shards(key_cotangent)
     routed, fetched = lax.optimization_barrier((routed, fetched))
     partner_weights, partner_grad = lax.optimization_barrier(
@@ -136,17 +165,22 @@
 
 
 def solution(mesh):
-    block = P("replica", "fsdp", None)
+    replicas, shards = mesh.devices.shape
+    grid = Mesh(
+        mesh.devices.reshape(replicas // LAYERS, LAYERS, shards), ("column", "layer", "fsdp")
+    )
+    replica = ("column", "layer")
+    block = P(replica, "fsdp", None)
     return jax.shard_map(
         on_device,
-        mesh=mesh,
+        mesh=grid,
         in_specs=(
             block,
             block,
             block,
             P(),
-            P("replica", "fsdp"),
-            P(("replica", "fsdp"), None),
+            P(replica, "fsdp"),
+            P(("column", "layer", "fsdp"), None),
         ),
         out_specs=(block, block, block),
         check_vma=False,

time: 109 us -> 107 us (0.982)
  the two profiles are of different devices: /device:TPU:192 before, /device:TPU:2 now
where the time goes in v8:
time: 107 us; the launch traced here: 106 us
  starting transfers between devices  51.2 us (48%)
  waiting for transfers between devices  39.6 us (37%)
  local copies, waits for them, and re-layouts  7.02 us (7%)
  other arithmetic  2.86 us (3%)
  Pallas kernels  2.62 us (2%)
  matrix products  1.95 us (2%)
    all_to_all x2, starting transfers between devices, exchange(): lax.all_to_all(pieces, RANKS, split_axis=0, concat_axis=0, tiled=True)  28.9 us
    all_to_all x2, waiting for transfers between devices, exchange(): lax.all_to_all(pieces, RANKS, split_axis=0, concat_axis=0, tiled=True)  19 us
    ppermute x1, waiting for transfers between devices, chips_shards(): far = lax.ppermute(shard, 'fsdp', core_pairs(chips, (2, 2)))  14.7 us
    ppermute x1, starting transfers between devices, chips_shards(): far = lax.ppermute(shard, 'fsdp', core_pairs(chips, (2, 2)))  13.8 us
    ppermute x1, starting transfers between devices, chips_shards(): near = lax.ppermute(chip, 'fsdp', core_pairs(chips, (1, chips - 1)))  4.6 us
    ppermute x1, waiting for transfers between devices, chips_shards(): near = lax.ppermute(chip, 'fsdp', core_pairs(chips, (1, chips - 1)))  4.31 us
    ppermute x2, starting transfers between devices, swap_cores(): lax.ppermute(array, 'fsdp', [(i, i ^ 1) for i in range(lax.axis_size('fsd...  3.84 us
    unnamed x15, local copies, waits for them, and re-layouts  2.22 us
  transfers between devices with their start and end apart: 6, of which 4 were waited for; matrix products, arithmetic and copies ran while one was open for 6% of the time, Pallas kernels for 0%

profile of v8, /device:TPU:2, one launch (start us, length us, event | category | flops | bytes accessed | tf_op | source)
XLA Modules:
  0.0 106.2 jit_solution(12941264362599216084)
XLA Ops:
  0.7 1.3 %reshape_squeeze.6.first_ref = bf16[128,4,512]{2,1,0:T(4,128)(2,1)S(1)} reshape(bf16[1,512,512]{2,1,0:T(8,128)(2,1)} %param.6) | data formatting | bytes 1048576 | tf_op jit(solution)/shard_map/reshape;squeeze | solution.py:49
  2.1 1.0 shard_map.85
  3.1 14.9 %all-to-all-start = ((bf16[96,11,4,128]{3,2,1,0:T(4,128)(2,1)}), bf16[96,11,4,128]{3,2,1,0:T(4,128)(2,1)S(1)}, u32[]{:S(2)}, u32[]{:S(2)}) async-start(bf16[96,11,4,128]{3,2,1,0:T(4,128)(2,1)} %bitcast.8), calls=%async_computation | async-start | bytes 2162688 | tf_op jit(solution)/shard_map/all_to_all | solution.py:67
  18.1 1.9 %collective-permute-start = (bf16[128,512]{1,0:T(8,128)(2,1)S(1)}, bf16[128,512]{1,0:T(8,128)(2,1)S(1)}, u32[]{:S(2)}, u32[]{:S(2)}) collective-permute-start(bf16[128,512]{1,0:T(8,128)(2,1)S(1)} %copy-done.5), channel_id=1, source_target_pairs={{0,1},{1,0},{2,3},{3,2},{4,5},{5,4},{6,7},{7,6},{8,9},{9,8},{10,11... | collective-permute-start | bytes 393224 | tf_op jit(solution)/shard_map/ppermute | solution.py:111
  20.0 13.8 %collective-permute-start.2 = (bf16[128,512]{1,0:T(8,128)(2,1)S(1)}, bf16[128,512]{1,0:T(8,128)(2,1)}, u32[]{:S(2)}, u32[]{:S(2)}) collective-permute-start(bf16[128,512]{1,0:T(8,128)(2,1)S(1)} %copy-done.5), channel_id=1, source_target_pairs={{0,4},{1,5},{2,6},{3,7},{4,0},{5,1},{6,2},{7,3},{8,12},{9,13},{10,... | collective-permute-start | bytes 393224 | tf_op jit(solution)/shard_map/ppermute | solution.py:116
  34.0 4.6 %collective-permute-start.1 = (bf16[256,512]{1,0:T(8,128)(2,1)S(1)}, bf16[256,512]{1,0:T(8,128)(2,1)S(1)}, u32[]{:S(2)}, u32[]{:S(2)}) collective-permute-start(bf16[256,512]{1,0:T(8,128)(2,1)S(1)} %get-tuple-element.24), channel_id=1, source_target_pairs={{0,2},{1,7},{2,4},{3,1},{4,6},{5,3},{6,0},{7,5},{8,10},{9,15},{10,... | collective-permute-start | bytes 786440 | tf_op jit(solution)/shard_map/ppermute | solution.py:118
  39.5 14.7 %collective-permute-done.2 = bf16[128,512]{1,0:T(8,128)(2,1)} collective-permute-done((bf16[128,512]{1,0:T(8,128)(2,1)S(1)}, bf16[128,512]{1,0:T(8,128)(2,1)}, u32[]{:S(2)}, u32[]{:S(2)}) %collective-permute-start.2) | collective-permute-done | bytes 131104 | tf_op jit(solution)/shard_map/ppermute | solution.py:116
  54.1 4.3 %collective-permute-done.1 = bf16[256,512]{1,0:T(8,128)(2,1)S(1)} collective-permute-done((bf16[256,512]{1,0:T(8,128)(2,1)S(1)}, bf16[256,512]{1,0:T(8,128)(2,1)S(1)}, u32[]{:S(2)}, u32[]{:S(2)}) %collective-permute-start.1) | collective-permute-done | bytes 262176 | tf_op jit(solution)/shard_map/ppermute | solution.py:118
  58.4 0.9 pad_maximum_fusion.1
  59.4 1.6 %shard_map.86 = bf16[96,11,4,128]{3,2,1,0:T(4,128)(2,1)} custom-call(s32[96]{0:T(128)S(1)} %fusion.9.partner_ref, bf16[96,11,4,128]{3,2,1,0:T(4,128)(2,1)S(1)} %all-to-all-done.pieces_ref), custom_call_target="tpu_custom_call" | custom-call | bytes 2162688 | tf_op jit(solution)/shard_map/pallas_call | solution.py:81
  61.0 14.0 %all-to-all-start.1 = ((bf16[96,11,4,128]{3,2,1,0:T(4,128)(2,1)}), bf16[96,11,4,128]{3,2,1,0:T(4,128)(2,1)S(1)}, u32[]{:S(2)}, u32[]{:S(2)}) async-start(bf16[96,11,4,128]{3,2,1,0:T(4,128)(2,1)} %shard_map.86), calls=%async_computation.1 | async-start | bytes 2162688 | tf_op jit(solution)/shard_map/all_to_all | solution.py:67
  75.0 1.9 %collective-permute-start.3 = (bf16[384,512]{1,0:T(8,128)(2,1)S(1)}, bf16[384,512]{1,0:T(8,128)(2,1)S(1)}, u32[]{:S(2)}, u32[]{:S(2)}) collective-permute-start(bf16[384,512]{1,0:T(8,128)(2,1)S(1)} %pad_maximum_fusion.1), channel_id=1, source_target_pairs={{0,1},{1,0},{2,3},{3,2},{4,5},{5,4},{6,7},{7,6},{8,9},{9,8},{10,11... | collective-permute-start | bytes 1179656 | tf_op jit(solution)/shard_map/ppermute | solution.py:111
  76.9 1.6 %collective-permute-done.3 = bf16[384,512]{1,0:T(8,128)(2,1)S(1)} collective-permute-done((bf16[384,512]{1,0:T(8,128)(2,1)S(1)}, bf16[384,512]{1,0:T(8,128)(2,1)S(1)}, u32[]{:S(2)}, u32[]{:S(2)}) %collective-permute-start.3) | collective-permute-done | bytes 393248 | tf_op jit(solution)/shard_map/ppermute | solution.py:111
  78.9 1.6 %gather_fusion = bf16[4,256,512]{2,1,0:T(8,128)(2,1)} fusion(bf16[4,256,512]{2,1,0:T(8,128)(2,1)S(1)} %pad_maximum_fusion, s32[1024]{0:T(1024)S(1)} %pad_clamp_fusion), kind=kCustom, calls=%fused_computation | custom fusion | bytes 2097168 | tf_op jit(solution)/shard_map/gather | solution.py:129
  80.5 2.0 %fusion = bf16[1,512,512]{1,2,0:T(8,128)(2,1)S(1)} fusion(bf16[1024,512]{1,0:T(8,128)(2,1)} %bitcast.69, bf16[1024,512]{1,0:T(8,128)(2,1)S(1)} %copy-done), kind=kOutput, calls=%fused_computation.5 | convolution fusion | flops 537133056 | bytes 2621440 | tf_op jit(solution)/shard_map/dot_general | solution.py:162
  82.5 1.0 copy.22
  83.5 19.0 %all-to-all-done.1 = bf16[96,11,4,128]{3,2,1,0:T(4,128)(2,1)S(1)} async-done(((bf16[96,11,4,128]{3,2,1,0:T(4,128)(2,1)}), bf16[96,11,4,128]{3,2,1,0:T(4,128)(2,1)S(1)}, u32[]{:S(2)}, u32[]{:S(2)}) %all-to-all-start.1) | async-done | bytes 1081376 | tf_op jit(solution)/shard_map/all_to_all | solution.py:67
  102.4 0.4 slice_bitcast_fusion
  102.8 0.2 copy.21
  103.0 0.2 copy.20
  103.4 0.9 copy-done.1
  104.3 0.2 copy-done.3
  104.4 0.2 copy-done.4
  104.6 1.6 %convert_bitcast_fusion = (bf16[1,512,512]{2,1,0:T(8,128)(2,1)}, bf16[1,512,512]{2,1,0:T(8,128)(2,1)}) fusion(bf16[512,512]{1,0:T(8,128)(2,1)S(1)} %get-tuple-element.9, bf16[1,512,512]{2,1,0:T(8,128)(2,1)S(1)} %copy-done.1, bf16[512,512]{1,0:T(8,128)(2,1)S(1)} %get-tuple-element.8, bf16[1,512,512]{2,1,0:T(8,128)(2,1)S(1)} %copy-done.3, ...), kind=kLoop, calls=%fused_computation.20 | loop fusion | flops 4980736 | bytes 3670016 | tf_op jit(solution)/shard_map/broadcast_in_dim | solution.py:164
  (37 shorter events, 1.5 us)
Async XLA Ops:
  0.6 79.9 %copy-start = (bf16[1024,512]{1,0:T(8,128)(2,1)S(1)}, bf16[1024,512]{1,0:T(8,128)(2,1)}, u32[]{:S(2)}) copy-start(bf16[1024,512]{1,0:T(8,128)(2,1)} %param.10) | copy-start | bytes 3145732
  0.6 1.3 %copy-start.2 = (bf16[1,512,512]{2,1,0:T(8,128)(2,1)S(1)}, bf16[1,512,512]{2,1,0:T(8,128)(2,1)}, u32[]{:S(2)}) copy-start(bf16[1,512,512]{2,1,0:T(8,128)(2,1)} %param.7) | copy-start | bytes 1572868
  3.1 14.9 %copy-start.5 = (bf16[128,512]{1,0:T(8,128)(2,1)S(1)}, bf16[128,512]{1,0:T(8,128)(2,1)}, u32[]{:S(2)}) copy-start(bf16[128,512]{1,0:T(8,128)(2,1)} %param.11) | copy-start | bytes 393220
  3.1 30.7 %copy-start.6 = (s32[96]{0:T(128)S(1)}, s32[96]{0:T(128)}, u32[]{:S(2)}) copy-start(s32[96]{0:T(128)} %param.9) | copy-start | bytes 1156
  3.1 56.2 %all-to-all-start = ((bf16[96,11,4,128]{3,2,1,0:T(4,128)(2,1)}), bf16[96,11,4,128]{3,2,1,0:T(4,128)(2,1)S(1)}, u32[]{:S(2)}, u32[]{:S(2)}) async-start(bf16[96,11,4,128]{3,2,1,0:T(4,128)(2,1)} %bitcast.8), calls=%async_computation | async-start | bytes 2162688 | tf_op jit(solution)/shard_map/all_to_all | solution.py:67
  18.1 15.8 %collective-permute-start = (bf16[128,512]{1,0:T(8,128)(2,1)S(1)}, bf16[128,512]{1,0:T(8,128)(2,1)S(1)}, u32[]{:S(2)}, u32[]{:S(2)}) collective-permute-start(bf16[128,512]{1,0:T(8,128)(2,1)S(1)} %copy-done.5), channel_id=1, source_target_pairs={{0,1},{1,0},{2,3},{3,2},{4,5},{5,4},{6,7},{7,6},{8,9},{9,8},{10,11... | collective-permute-start | bytes 393224 | tf_op jit(solution)/shard_map/ppermute | solution.py:111
  20.0 34.1 %collective-permute-start.2 = (bf16[128,512]{1,0:T(8,128)(2,1)S(1)}, bf16[128,512]{1,0:T(8,128)(2,1)}, u32[]{:S(2)}, u32[]{:S(2)}) collective-permute-start(bf16[128,512]{1,0:T(8,128)(2,1)S(1)} %copy-done.5), channel_id=1, source_target_pairs={{0,4},{1,5},{2,6},{3,7},{4,0},{5,1},{6,2},{7,3},{8,12},{9,13},{10,... | collective-permute-start | bytes 393224 | tf_op jit(solution)/shard_map/ppermute | solution.py:116
  34.0 24.5 %collective-permute-start.1 = (bf16[256,512]{1,0:T(8,128)(2,1)S(1)}, bf16[256,512]{1,0:T(8,128)(2,1)S(1)}, u32[]{:S(2)}, u32[]{:S(2)}) collective-permute-start(bf16[256,512]{1,0:T(8,128)(2,1)S(1)} %get-tuple-element.24), channel_id=1, source_target_pairs={{0,2},{1,7},{2,4},{3,1},{4,6},{5,3},{6,0},{7,5},{8,10},{9,15},{10,... | collective-permute-start | bytes 786440 | tf_op jit(solution)/shard_map/ppermute | solution.py:118
  61.0 41.4 %all-to-all-start.1 = ((bf16[96,11,4,128]{3,2,1,0:T(4,128)(2,1)}), bf16[96,11,4,128]{3,2,1,0:T(4,128)(2,1)S(1)}, u32[]{:S(2)}, u32[]{:S(2)}) async-start(bf16[96,11,4,128]{3,2,1,0:T(4,128)(2,1)} %shard_map.86), calls=%async_computation.1 | async-start | bytes 2162688 | tf_op jit(solution)/shard_map/all_to_all | solution.py:67
  75.0 3.6 %collective-permute-start.3 = (bf16[384,512]{1,0:T(8,128)(2,1)S(1)}, bf16[384,512]{1,0:T(8,128)(2,1)S(1)}, u32[]{:S(2)}, u32[]{:S(2)}) collective-permute-start(bf16[384,512]{1,0:T(8,128)(2,1)S(1)} %pad_maximum_fusion.1), channel_id=1, source_target_pairs={{0,1},{1,0},{2,3},{3,2},{4,5},{5,4},{6,7},{7,6},{8,9},{9,8},{10,11... | collective-permute-start | bytes 1179656 | tf_op jit(solution)/shard_map/ppermute | solution.py:111
  103.2 1.0 copy-start.1
  103.2 1.2 %copy-start.3 = (bf16[1,512,512]{2,1,0:T(8,128)(2,1)S(1)}, bf16[1,512,512]{2,1,0:T(8,128)(2,1)}, u32[]{:S(2)}) copy-start(bf16[1,512,512]{2,1,0:T(8,128)(2,1)} %param.7) | copy-start | bytes 1572868
  103.2 1.3 %copy-start.4 = (bf16[1,512,512]{2,1,0:T(8,128)(2,1)S(1)}, bf16[1,512,512]{2,1,0:T(8,128)(2,1)}, u32[]{:S(2)}) copy-start(bf16[1,512,512]{2,1,0:T(8,128)(2,1)} %param.8) | copy-start | bytes 1572868

commit v9 on v8

--- a/solution.py
+++ b/solution.py
@@ -111,18 +111,19 @@
     return lax.ppermute(array, "fsdp", [(i, i ^ 1) for i in range(lax.axis_size("fsdp"))])
 
 
-def chips_shards(shard):
+def near_shards(shard):
     chips = lax.axis_size("fsdp") // CORES
-    far = lax.ppermute(shard, "fsdp", core_pairs(chips, (2, 2)))
     chip = jnp.concatenate(by_core(shard, swap_cores(shard)), axis=0)
-    near = lax.ppermute(chip, "fsdp", core_pairs(chips, (1, chips - 1)))
-    return chip, jnp.concatenate([near, far], axis=0)
+    return chip, lax.ppermute(chip, "fsdp", core_pairs(chips, (1, chips - 1)))
 
 
-def all_shards(chip, fetched):
+def all_shards(chip, near):
     tokens = chip.shape[0]
     chips = lax.axis_size("fsdp") // CORES
     here = lax.axis_index("fsdp") // CORES
+    own_core = by_core(near[: tokens // CORES], near[tokens // CORES :])[0]
+    far = lax.ppermute(own_core, "fsdp", core_pairs(chips, (1, chips - 1)))
+    fetched = jnp.concatenate([near, far], axis=0)
     even, odd = by_core(fetched, swap_cores(fetched))
     blocks = (chip, even[:tokens], jnp.concatenate([even[tokens:], odd[tokens:]]), odd[:tokens])
     order = (here - jnp.arange(chips, dtype=jnp.int32) + chips) % chips
@@ -139,8 +140,8 @@
     pieces = exchange(to_pieces(weights, pseudo_grad, replicas))
     by_rank = partner.reshape(columns, LAYERS).T.reshape(-1)
     routed = route(pieces, by_rank % LAYERS * columns + by_rank // LAYERS)
-    chip, fetched = chips_shards(key_cotangent)
-    routed, fetched = lax.optimization_barrier((routed, fetched))
+    chip, near = near_shards(key_cotangent)
+    routed, near = lax.optimization_barrier((routed, near))
     partner_weights, partner_grad = lax.optimization_barrier(
         from_pieces(exchange(routed), rows, cols)
     )
@@ -157,7 +158,7 @@
     new_weights = new_weights.astype(jnp.bfloat16)
     new_momentum = momentum_f.astype(jnp.bfloat16)
 
-    gathered = all_shards(chip, fetched)
+    gathered = all_shards(chip, near)
     contract = (((0,), (0,)), ((), ()))
     grad_f32 = lax.dot_general(activations, gathered, contract, preferred_element_type=jnp.float32)
     weight_grad = grad_f32.astype(jnp.bfloat16)

time: 107 us -> 99 us (0.925)
  the two profiles are of different devices: /device:TPU:2 before, /device:TPU:1 now
where the time goes in v9:
time: 99 us; the launch traced here: 98.5 us
  starting transfers between devices  70.1 us (71%)
  waiting for transfers between devices  13.9 us (14%)
  local copies, waits for them, and re-layouts  7.05 us (7%)
  Pallas kernels  2.61 us (3%)
  matrix products  1.95 us (2%)
  other arithmetic  1.94 us (2%)
  between operations  0.99 us (1%)
    all_to_all x2, starting transfers between devices, exchange(): lax.all_to_all(pieces, RANKS, split_axis=0, concat_axis=0, tiled=True)  33.1 us
    ppermute x2, starting transfers between devices, swap_cores(): lax.ppermute(array, 'fsdp', [(i, i ^ 1) for i in range(lax.axis_size('fsd...  19 us
    ppermute x1, starting transfers between devices, near_shards(): return (chip, lax.ppermute(chip, 'fsdp', core_pairs(chips, (1, chips - 1))))  12.3 us
    all_to_all x2, waiting for transfers between devices, exchange(): lax.all_to_all(pieces, RANKS, split_axis=0, concat_axis=0, tiled=True)  8.26 us
    ppermute x1, starting transfers between devices, all_shards(): far = lax.ppermute(own_core, 'fsdp', core_pairs(chips, (1, chips - 1)))  5.7 us
    ppermute x1, waiting for transfers between devices, all_shards(): far = lax.ppermute(own_core, 'fsdp', core_pairs(chips, (1, chips - 1)))  3.38 us
    unnamed x16, local copies, waits for them, and re-layouts  2.24 us
    ppermute x2, waiting for transfers between devices, swap_cores(): lax.ppermute(array, 'fsdp', [(i, i ^ 1) for i in range(lax.axis_size('fsd...  2.21 us
  transfers between devices with their start and end apart: 6, of which 4 were waited for; matrix products, arithmetic and copies ran while one was open for 6% of the time, Pallas kernels for 2%

profile of v9, /device:TPU:1, one launch (start us, length us, event | category | flops | bytes accessed | tf_op | source)
XLA Modules:
  0.0 98.5 jit_solution(12143938859767633775)
XLA Ops:
  0.7 1.3 %reshape_squeeze.6.first_ref = bf16[128,4,512]{2,1,0:T(4,128)(2,1)S(1)} reshape(bf16[1,512,512]{2,1,0:T(8,128)(2,1)} %param.6) | data formatting | bytes 1048576 | tf_op jit(solution)/shard_map/reshape;squeeze | solution.py:49
  2.1 1.0 %shard_map.85 = bf16[264,4,512]{2,1,0:T(4,128)(2,1)} custom-call(bf16[128,4,512]{2,1,0:T(4,128)(2,1)S(1)} %reshape_squeeze.6.first_ref, bf16[128,4,512]{2,1,0:T(4,128)(2,1)S(1)} %reshape_squeeze.7.second_ref), custom_call_target="tpu_custom_call" | custom-call | tf_op jit(solution)/shard_map/pallas_call | solution.py:37
  3.1 15.5 %all-to-all-start = ((bf16[96,11,4,128]{3,2,1,0:T(4,128)(2,1)}), bf16[96,11,4,128]{3,2,1,0:T(4,128)(2,1)S(1)}, u32[]{:S(2)}, u32[]{:S(2)}) async-start(bf16[96,11,4,128]{3,2,1,0:T(4,128)(2,1)} %bitcast.8), calls=%async_computation | async-start | bytes 2162688 | tf_op jit(solution)/shard_map/all_to_all | solution.py:67
  18.6 3.0 %collective-permute-start = (bf16[128,512]{1,0:T(8,128)(2,1)S(1)}, bf16[128,512]{1,0:T(8,128)(2,1)S(1)}, u32[]{:S(2)}, u32[]{:S(2)}) collective-permute-start(bf16[128,512]{1,0:T(8,128)(2,1)S(1)} %copy-done.5), channel_id=1, source_target_pairs={{0,1},{1,0},{2,3},{3,2},{4,5},{5,4},{6,7},{7,6},{8,9},{9,8},{10,11... | collective-permute-start | bytes 393224 | tf_op jit(solution)/shard_map/ppermute | solution.py:111
  21.7 0.9 collective-permute-done
  22.7 12.3 %collective-permute-start.1 = (bf16[256,512]{1,0:T(8,128)(2,1)S(1)}, bf16[256,512]{1,0:T(8,128)(2,1)S(1)}, u32[]{:S(2)}, u32[]{:S(2)}) collective-permute-start(bf16[256,512]{1,0:T(8,128)(2,1)S(1)} %get-tuple-element.24), channel_id=1, source_target_pairs={{0,2},{1,7},{2,4},{3,1},{4,6},{5,3},{6,0},{7,5},{8,10},{9,15},{10,... | collective-permute-start | bytes 786440 | tf_op jit(solution)/shard_map/ppermute | solution.py:117
  35.9 8.3 %all-to-all-done.pieces_ref = bf16[96,11,4,128]{3,2,1,0:T(4,128)(2,1)S(1)} async-done(((bf16[96,11,4,128]{3,2,1,0:T(4,128)(2,1)}), bf16[96,11,4,128]{3,2,1,0:T(4,128)(2,1)S(1)}, u32[]{:S(2)}, u32[]{:S(2)}) %all-to-all-start) | async-done | bytes 1081376 | tf_op jit(solution)/shard_map/all_to_all | solution.py:67
  44.2 1.6 %shard_map.86 = bf16[96,11,4,128]{3,2,1,0:T(4,128)(2,1)} custom-call(s32[96]{0:T(128)S(1)} %fusion.9.partner_ref, bf16[96,11,4,128]{3,2,1,0:T(4,128)(2,1)S(1)} %all-to-all-done.pieces_ref), custom_call_target="tpu_custom_call" | custom-call | bytes 2162688 | tf_op jit(solution)/shard_map/pallas_call | solution.py:81
  45.8 17.6 %all-to-all-start.1 = ((bf16[96,11,4,128]{3,2,1,0:T(4,128)(2,1)}), bf16[96,11,4,128]{3,2,1,0:T(4,128)(2,1)S(1)}, u32[]{:S(2)}, u32[]{:S(2)}) async-start(bf16[96,11,4,128]{3,2,1,0:T(4,128)(2,1)} %shard_map.86), calls=%async_computation.1 | async-start | bytes 2162688 | tf_op jit(solution)/shard_map/all_to_all | solution.py:67
  63.5 5.7 %collective-permute-start.2 = (bf16[128,512]{1,0:T(8,128)(2,1)S(1)}, bf16[128,512]{1,0:T(8,128)(2,1)S(1)}, u32[]{:S(2)}, u32[]{:S(2)}) collective-permute-start(bf16[128,512]{1,0:T(8,128)(2,1)S(1)} %slice_select_fusion), channel_id=1, source_target_pairs={{0,2},{1,7},{2,4},{3,1},{4,6},{5,3},{6,0},{7,5},{8,10},{9,15},{10,... | collective-permute-start | bytes 393224 | tf_op jit(solution)/shard_map/ppermute | solution.py:125
  69.2 3.4 %collective-permute-done.2 = bf16[128,512]{1,0:T(8,128)(2,1)S(1)} collective-permute-done((bf16[128,512]{1,0:T(8,128)(2,1)S(1)}, bf16[128,512]{1,0:T(8,128)(2,1)S(1)}, u32[]{:S(2)}, u32[]{:S(2)}) %collective-permute-start.2) | collective-permute-done | bytes 131104 | tf_op jit(solution)/shard_map/ppermute | solution.py:125
  72.6 15.9 %collective-permute-start.3 = (bf16[384,512]{1,0:T(8,128)(2,1)S(1)}, bf16[384,512]{1,0:T(8,128)(2,1)S(1)}, u32[]{:S(2)}, u32[]{:S(2)}) collective-permute-start(bf16[384,512]{1,0:T(8,128)(2,1)S(1)} %constant_dynamic-update-slice_fusion), channel_id=1, source_target_pairs={{0,1},{1,0},{2,3},{3,2},{4,5},{5,4},{6,7},{7,6},{8,9},{9,8},{10,11... | collective-permute-start | bytes 1179656 | tf_op jit(solution)/shard_map/ppermute | solution.py:111
  88.6 1.3 %collective-permute-done.3 = bf16[384,512]{1,0:T(8,128)(2,1)S(1)} collective-permute-done((bf16[384,512]{1,0:T(8,128)(2,1)S(1)}, bf16[384,512]{1,0:T(8,128)(2,1)S(1)}, u32[]{:S(2)}, u32[]{:S(2)}) %collective-permute-start.3) | collective-permute-done | bytes 393248 | tf_op jit(solution)/shard_map/ppermute | solution.py:111
  90.2 1.6 %gather_fusion = bf16[4,256,512]{2,1,0:T(8,128)(2,1)} fusion(bf16[4,256,512]{2,1,0:T(8,128)(2,1)S(1)} %pad_maximum_fusion, s32[1024]{0:T(1024)S(1)} %pad_clamp_fusion), kind=kCustom, calls=%fused_computation | custom fusion | bytes 2097168 | tf_op jit(solution)/shard_map/gather | solution.py:130
  91.8 2.0 %fusion = bf16[1,512,512]{1,2,0:T(8,128)(2,1)S(1)} fusion(bf16[1024,512]{1,0:T(8,128)(2,1)} %bitcast.69, bf16[1024,512]{1,0:T(8,128)(2,1)S(1)} %copy-done), kind=kOutput, calls=%fused_computation.5 | convolution fusion | flops 537133056 | bytes 2621440 | tf_op jit(solution)/shard_map/dot_general | solution.py:163
  93.7 1.0 %copy.22 = bf16[1,512,512]{2,1,0:T(8,128)(2,1)} copy(bf16[1,512,512]{1,2,0:T(8,128)(2,1)S(1)} %fusion) | data formatting | bytes 1048576
  94.7 0.4 slice_bitcast_fusion
  95.1 0.2 copy.21
  95.3 0.2 copy.20
  95.6 0.1 copy_bitcast_fusion
  95.7 0.9 copy-done.1
  96.6 0.2 copy-done.3
  96.7 0.2 copy-done.4
  96.9 1.6 %convert_bitcast_fusion = (bf16[1,512,512]{2,1,0:T(8,128)(2,1)}, bf16[1,512,512]{2,1,0:T(8,128)(2,1)}) fusion(bf16[512,512]{1,0:T(8,128)(2,1)S(1)} %get-tuple-element.9, bf16[1,512,512]{2,1,0:T(8,128)(2,1)S(1)} %copy-done.1, bf16[512,512]{1,0:T(8,128)(2,1)S(1)} %get-tuple-element.8, bf16[1,512,512]{2,1,0:T(8,128)(2,1)S(1)} %copy-done.3, ...), kind=kLoop, calls=%fused_computation.20 | loop fusion | flops 4980736 | bytes 3670016 | tf_op jit(solution)/shard_map/broadcast_in_dim | solution.py:165
  (39 shorter events, 1.4 us)
Async XLA Ops:
  0.6 91.1 %copy-start = (bf16[1024,512]{1,0:T(8,128)(2,1)S(1)}, bf16[1024,512]{1,0:T(8,128)(2,1)}, u32[]{:S(2)}) copy-start(bf16[1024,512]{1,0:T(8,128)(2,1)} %param.10) | copy-start | bytes 3145732
  0.6 1.3 %copy-start.2 = (bf16[1,512,512]{2,1,0:T(8,128)(2,1)S(1)}, bf16[1,512,512]{2,1,0:T(8,128)(2,1)}, u32[]{:S(2)}) copy-start(bf16[1,512,512]{2,1,0:T(8,128)(2,1)} %param.7) | copy-start | bytes 1572868
  3.1 15.5 %copy-start.5 = (bf16[128,512]{1,0:T(8,128)(2,1)S(1)}, bf16[128,512]{1,0:T(8,128)(2,1)}, u32[]{:S(2)}) copy-start(bf16[128,512]{1,0:T(8,128)(2,1)} %param.11) | copy-start | bytes 393220
  3.1 18.6 %copy-start.6 = (s32[96]{0:T(128)S(1)}, s32[96]{0:T(128)}, u32[]{:S(2)}) copy-start(s32[96]{0:T(128)} %param.9) | copy-start | bytes 1156
  3.1 41.1 %all-to-all-start = ((bf16[96,11,4,128]{3,2,1,0:T(4,128)(2,1)}), bf16[96,11,4,128]{3,2,1,0:T(4,128)(2,1)S(1)}, u32[]{:S(2)}, u32[]{:S(2)}) async-start(bf16[96,11,4,128]{3,2,1,0:T(4,128)(2,1)} %bitcast.8), calls=%async_computation | async-start | bytes 2162688 | tf_op jit(solution)/shard_map/all_to_all | solution.py:67
  18.6 4.0 %collective-permute-start = (bf16[128,512]{1,0:T(8,128)(2,1)S(1)}, bf16[128,512]{1,0:T(8,128)(2,1)S(1)}, u32[]{:S(2)}, u32[]{:S(2)}) collective-permute-start(bf16[128,512]{1,0:T(8,128)(2,1)S(1)} %copy-done.5), channel_id=1, source_target_pairs={{0,1},{1,0},{2,3},{3,2},{4,5},{5,4},{6,7},{7,6},{8,9},{9,8},{10,11... | collective-permute-start | bytes 393224 | tf_op jit(solution)/shard_map/ppermute | solution.py:111
  22.7 23.1 %collective-permute-start.1 = (bf16[256,512]{1,0:T(8,128)(2,1)S(1)}, bf16[256,512]{1,0:T(8,128)(2,1)S(1)}, u32[]{:S(2)}, u32[]{:S(2)}) collective-permute-start(bf16[256,512]{1,0:T(8,128)(2,1)S(1)} %get-tuple-element.24), channel_id=1, source_target_pairs={{0,2},{1,7},{2,4},{3,1},{4,6},{5,3},{6,0},{7,5},{8,10},{9,15},{10,... | collective-permute-start | bytes 786440 | tf_op jit(solution)/shard_map/ppermute | solution.py:117
  45.8 48.9 %all-to-all-start.1 = ((bf16[96,11,4,128]{3,2,1,0:T(4,128)(2,1)}), bf16[96,11,4,128]{3,2,1,0:T(4,128)(2,1)S(1)}, u32[]{:S(2)}, u32[]{:S(2)}) async-start(bf16[96,11,4,128]{3,2,1,0:T(4,128)(2,1)} %shard_map.86), calls=%async_computation.1 | async-start | bytes 2162688 | tf_op jit(solution)/shard_map/all_to_all | solution.py:67
  63.5 9.1 %collective-permute-start.2 = (bf16[128,512]{1,0:T(8,128)(2,1)S(1)}, bf16[128,512]{1,0:T(8,128)(2,1)S(1)}, u32[]{:S(2)}, u32[]{:S(2)}) collective-permute-start(bf16[128,512]{1,0:T(8,128)(2,1)S(1)} %slice_select_fusion), channel_id=1, source_target_pairs={{0,2},{1,7},{2,4},{3,1},{4,6},{5,3},{6,0},{7,5},{8,10},{9,15},{10,... | collective-permute-start | bytes 393224 | tf_op jit(solution)/shard_map/ppermute | solution.py:125
  72.6 17.3 %collective-permute-start.3 = (bf16[384,512]{1,0:T(8,128)(2,1)S(1)}, bf16[384,512]{1,0:T(8,128)(2,1)S(1)}, u32[]{:S(2)}, u32[]{:S(2)}) collective-permute-start(bf16[384,512]{1,0:T(8,128)(2,1)S(1)} %constant_dynamic-update-slice_fusion), channel_id=1, source_target_pairs={{0,1},{1,0},{2,3},{3,2},{4,5},{5,4},{6,7},{7,6},{8,9},{9,8},{10,11... | collective-permute-start | bytes 1179656 | tf_op jit(solution)/shard_map/ppermute | solution.py:111
  95.5 1.0 %copy-start.1 = (bf16[1,512,512]{2,1,0:T(8,128)(2,1)S(1)}, bf16[1,512,512]{2,1,0:T(8,128)(2,1)}, u32[]{:S(2)}) copy-start(bf16[1,512,512]{2,1,0:T(8,128)(2,1)} %param.6) | copy-start | bytes 1572868
  95.5 1.2 %copy-start.3 = (bf16[1,512,512]{2,1,0:T(8,128)(2,1)S(1)}, bf16[1,512,512]{2,1,0:T(8,128)(2,1)}, u32[]{:S(2)}) copy-start(bf16[1,512,512]{2,1,0:T(8,128)(2,1)} %param.7) | copy-start | bytes 1572868
  95.5 1.3 %copy-start.4 = (bf16[1,512,512]{2,1,0:T(8,128)(2,1)S(1)}, bf16[1,512,512]{2,1,0:T(8,128)(2,1)}, u32[]{:S(2)}) copy-start(bf16[1,512,512]{2,1,0:T(8,128)(2,1)} %param.8) | copy-start | bytes 1572868

commit v10 on v9

--- a/solution.py
+++ b/solution.py
@@ -120,15 +120,19 @@
 def all_shards(chip, near):
     tokens = chip.shape[0]
     chips = lax.axis_size("fsdp") // CORES
-    here = lax.axis_index("fsdp") // CORES
     own_core = by_core(near[: tokens // CORES], near[tokens // CORES :])[0]
     far = lax.ppermute(own_core, "fsdp", core_pairs(chips, (1, chips - 1)))
     fetched = jnp.concatenate([near, far], axis=0)
     even, odd = by_core(fetched, swap_cores(fetched))
-    blocks = (chip, even[:tokens], jnp.concatenate([even[tokens:], odd[tokens:]]), odd[:tokens])
+    return jnp.concatenate([chip, even[:tokens], even[tokens:], odd[tokens:], odd[:tokens]])
+
+
+def in_arrival_order(activations):
+    chips = lax.axis_size("fsdp") // CORES
+    here = lax.axis_index("fsdp") // CORES
     order = (here - jnp.arange(chips, dtype=jnp.int32) + chips) % chips
-    ordered = jnp.stack(blocks).at[order].get(mode="promise_in_bounds")
-    return ordered.reshape(-1, chip.shape[-1])
+    blocks = activations.reshape(chips, -1, activations.shape[-1])
+    return blocks.at[order].get(mode="promise_in_bounds").reshape(activations.shape)
 
 
 def on_device(weights, pseudo_grad, momentum, partner, activations, key_cotangent):
@@ -141,7 +145,8 @@
     by_rank = partner.reshape(columns, LAYERS).T.reshape(-1)
     routed = route(pieces, by_rank % LAYERS * columns + by_rank // LAYERS)
     chip, near = near_shards(key_cotangent)
-    routed, near = lax.optimization_barrier((routed, near))
+    activations = in_arrival_order(activations)
+    routed, near, activations = lax.optimization_barrier((routed, near, activations))
     partner_weights, partner_grad = lax.optimization_barrier(
         from_pieces(exchange(routed), rows, cols)
     )

time: 99 us -> 96.7 us (0.977)
  waiting for transfers between devices: 13.9 us -> 11.3 us
  other arithmetic: 1.94 us -> 3.19 us
    all_to_all x2, waiting for transfers between devices: 8.26 us -> 5.66 us  [exchange(): lax.all_to_all(pieces, RANKS, split_axis=0, concat_axis=0, tiled=True)]
    unnamed x0 -> x2, other arithmetic: none -> 1.38 us
    unnamed x16 -> x18, local copies, waits for them, and re-layouts: 2.24 us -> 2.13 us
where the time goes in v10:
time: 96.7 us; the launch traced here: 96.2 us
  starting transfers between devices  69.8 us (72%)
  waiting for transfers between devices  11.3 us (12%)
  local copies, waits for them, and re-layouts  6.92 us (7%)
  other arithmetic  3.19 us (3%)
  Pallas kernels  2.61 us (3%)
  matrix products  1.53 us (2%)
    all_to_all x2, starting transfers between devices, exchange(): lax.all_to_all(pieces, RANKS, split_axis=0, concat_axis=0, tiled=True)  32.8 us
    ppermute x2, starting transfers between devices, swap_cores(): lax.ppermute(array, 'fsdp', [(i, i ^ 1) for i in range(lax.axis_size('fsd...  18.8 us
    ppermute x1, starting transfers between devices, near_shards(): return (chip, lax.ppermute(chip, 'fsdp', core_pairs(chips, (1, chips - 1))))  12.3 us
    ppermute x1, starting transfers between devices, all_shards(): far = lax.ppermute(own_core, 'fsdp', core_pairs(chips, (1, chips - 1)))  5.83 us
    all_to_all x2, waiting for transfers between devices, exchange(): lax.all_to_all(pieces, RANKS, split_axis=0, concat_axis=0, tiled=True)  5.66 us
    ppermute x1, waiting for transfers between devices, all_shards(): far = lax.ppermute(own_core, 'fsdp', core_pairs(chips, (1, chips - 1)))  3.39 us
    ppermute x2, waiting for transfers between devices, swap_cores(): lax.ppermute(array, 'fsdp', [(i, i ^ 1) for i in range(lax.axis_size('fsd...  2.21 us
    unnamed x18, local copies, waits for them, and re-layouts  2.13 us
  transfers between devices with their start and end apart: 6, of which 4 were waited for; matrix products, arithmetic and copies ran while one was open for 6% of the time, Pallas kernels for 2%

profile of v10, /device:TPU:1, one launch (start us, length us, event | category | flops | bytes accessed | tf_op | source)
XLA Modules:
  0.0 96.2 jit_solution(11544089782768473214)
XLA Ops:
  0.7 1.3 %reshape_squeeze.6.first_ref = bf16[128,4,512]{2,1,0:T(4,128)(2,1)S(1)} reshape(bf16[1,512,512]{2,1,0:T(8,128)(2,1)} %param.6) | data formatting | bytes 1048576 | tf_op jit(solution)/shard_map/reshape;squeeze | solution.py:49
  2.1 1.0 %shard_map.85 = bf16[264,4,512]{2,1,0:T(4,128)(2,1)} custom-call(bf16[128,4,512]{2,1,0:T(4,128)(2,1)S(1)} %reshape_squeeze.6.first_ref, bf16[128,4,512]{2,1,0:T(4,128)(2,1)S(1)} %reshape_squeeze.7.second_ref), custom_call_target="tpu_custom_call" | custom-call | tf_op jit(solution)/shard_map/pallas_call | solution.py:37
  3.1 15.5 %all-to-all-start = ((bf16[96,11,4,128]{3,2,1,0:T(4,128)(2,1)}), bf16[96,11,4,128]{3,2,1,0:T(4,128)(2,1)S(1)}, u32[]{:S(2)}, u32[]{:S(2)}) async-start(bf16[96,11,4,128]{3,2,1,0:T(4,128)(2,1)} %bitcast.8), calls=%async_computation | async-start | bytes 2162688 | tf_op jit(solution)/shard_map/all_to_all | solution.py:67
  18.6 3.0 %collective-permute-start = (bf16[128,512]{1,0:T(8,128)(2,1)S(1)}, bf16[128,512]{1,0:T(8,128)(2,1)S(1)}, u32[]{:S(2)}, u32[]{:S(2)}) collective-permute-start(bf16[128,512]{1,0:T(8,128)(2,1)S(1)} %copy-done.5), channel_id=1, source_target_pairs={{0,1},{1,0},{2,3},{3,2},{4,5},{5,4},{6,7},{7,6},{8,9},{9,8},{10,11... | collective-permute-start | bytes 393224 | tf_op jit(solution)/shard_map/ppermute | solution.py:111
  21.8 0.9 collective-permute-done
  22.7 0.7 constant_dynamic-update-slice_fusion.3
  23.4 0.7 constant_dynamic-update-slice_fusion.2
  24.1 12.3 %collective-permute-start.1 = (bf16[256,512]{1,0:T(8,128)(2,1)S(1)}, bf16[256,512]{1,0:T(8,128)(2,1)S(1)}, u32[]{:S(2)}, u32[]{:S(2)}) collective-permute-start(bf16[256,512]{1,0:T(8,128)(2,1)S(1)} %pad_maximum_fusion), channel_id=1, source_target_pairs={{0,2},{1,7},{2,4},{3,1},{4,6},{5,3},{6,0},{7,5},{8,10},{9,15},{10,... | collective-permute-start | bytes 786440 | tf_op jit(solution)/shard_map/ppermute | solution.py:117
  37.2 1.6 %gather_fusion = bf16[4,256,512]{2,1,0:T(8,128)(2,1)} fusion(bf16[4,256,512]{2,1,0:T(8,128)(2,1)S(1)} %bitcast.57, s32[1024]{0:T(1024)S(1)} %pad_clamp_fusion), kind=kCustom, calls=%fused_computation | custom fusion | bytes 2097168 | tf_op jit(solution)/shard_map/gather | solution.py:135
  38.9 5.7 %all-to-all-done.pieces_ref = bf16[96,11,4,128]{3,2,1,0:T(4,128)(2,1)S(1)} async-done(((bf16[96,11,4,128]{3,2,1,0:T(4,128)(2,1)}), bf16[96,11,4,128]{3,2,1,0:T(4,128)(2,1)S(1)}, u32[]{:S(2)}, u32[]{:S(2)}) %all-to-all-start) | async-done | bytes 1081376 | tf_op jit(solution)/shard_map/all_to_all | solution.py:67
  44.5 1.6 %shard_map.86 = bf16[96,11,4,128]{3,2,1,0:T(4,128)(2,1)} custom-call(s32[96]{0:T(128)S(1)} %fusion.9.partner_ref, bf16[96,11,4,128]{3,2,1,0:T(4,128)(2,1)S(1)} %all-to-all-done.pieces_ref), custom_call_target="tpu_custom_call" | custom-call | bytes 2162688 | tf_op jit(solution)/shard_map/pallas_call | solution.py:81
  46.1 17.3 %all-to-all-start.1 = ((bf16[96,11,4,128]{3,2,1,0:T(4,128)(2,1)}), bf16[96,11,4,128]{3,2,1,0:T(4,128)(2,1)S(1)}, u32[]{:S(2)}, u32[]{:S(2)}) async-start(bf16[96,11,4,128]{3,2,1,0:T(4,128)(2,1)} %shard_map.86), calls=%async_computation.1 | async-start | bytes 2162688 | tf_op jit(solution)/shard_map/all_to_all | solution.py:67
  63.5 5.8 %collective-permute-start.2 = (bf16[128,512]{1,0:T(8,128)(2,1)S(1)}, bf16[128,512]{1,0:T(8,128)(2,1)S(1)}, u32[]{:S(2)}, u32[]{:S(2)}) collective-permute-start(bf16[128,512]{1,0:T(8,128)(2,1)S(1)} %slice_select_fusion), channel_id=1, source_target_pairs={{0,2},{1,7},{2,4},{3,1},{4,6},{5,3},{6,0},{7,5},{8,10},{9,15},{10,... | collective-permute-start | bytes 393224 | tf_op jit(solution)/shard_map/ppermute | solution.py:124
  69.3 3.4 %collective-permute-done.2 = bf16[128,512]{1,0:T(8,128)(2,1)S(1)} collective-permute-done((bf16[128,512]{1,0:T(8,128)(2,1)S(1)}, bf16[128,512]{1,0:T(8,128)(2,1)S(1)}, u32[]{:S(2)}, u32[]{:S(2)}) %collective-permute-start.2) | collective-permute-done | bytes 131104 | tf_op jit(solution)/shard_map/ppermute | solution.py:124
  72.7 15.8 %collective-permute-start.3 = (bf16[384,512]{1,0:T(8,128)(2,1)S(1)}, bf16[384,512]{1,0:T(8,128)(2,1)S(1)}, u32[]{:S(2)}, u32[]{:S(2)}) collective-permute-start(bf16[384,512]{1,0:T(8,128)(2,1)S(1)} %constant_dynamic-update-slice_fusion), channel_id=1, source_target_pairs={{0,1},{1,0},{2,3},{3,2},{4,5},{5,4},{6,7},{7,6},{8,9},{9,8},{10,11... | collective-permute-start | bytes 1179656 | tf_op jit(solution)/shard_map/ppermute | solution.py:111
  88.5 1.3 %collective-permute-done.3 = bf16[384,512]{1,0:T(8,128)(2,1)S(1)} collective-permute-done((bf16[384,512]{1,0:T(8,128)(2,1)S(1)}, bf16[384,512]{1,0:T(8,128)(2,1)S(1)}, u32[]{:S(2)}, u32[]{:S(2)}) %collective-permute-start.3) | collective-permute-done | bytes 393248 | tf_op jit(solution)/shard_map/ppermute | solution.py:111
  90.1 1.0 %copy-done.3 = bf16[4,256,512]{2,1,0:T(8,128)(2,1)S(1)} copy-done((bf16[4,256,512]{2,1,0:T(8,128)(2,1)S(1)}, bf16[4,256,512]{2,1,0:T(8,128)(2,1)}, u32[]{:S(2)}) %copy-start.3) | copy-done | bytes 1048600
  91.1 1.5 %fusion = bf16[1,512,512]{2,1,0:T(8,128)(2,1)} fusion(bf16[1024,512]{1,0:T(8,128)(2,1)S(1)} %bitcast.61, bf16[1024,512]{1,0:T(8,128)(2,1)S(1)} %slice_dynamic-update-slice_fusion), kind=kOutput, calls=%fused_computation.5 | convolution fusion | flops 537133056 | bytes 2621440 | tf_op jit(solution)/shard_map/dot_general | solution.py:168
  92.6 0.4 slice_bitcast_fusion
  93.0 0.2 copy.20
  93.2 0.2 copy.19
  93.6 0.9 copy-done.1
  94.5 0.2 copy-done.4
  94.6 1.6 %convert_bitcast_fusion = (bf16[1,512,512]{2,1,0:T(8,128)(2,1)}, bf16[1,512,512]{2,1,0:T(8,128)(2,1)}) fusion(bf16[512,512]{1,0:T(8,128)(2,1)S(1)} %get-tuple-element.10, bf16[1,512,512]{2,1,0:T(8,128)(2,1)S(1)} %copy-done.1, bf16[512,512]{1,0:T(8,128)(2,1)S(1)} %get-tuple-element.9, bf16[1,512,512]{2,1,0:T(8,128)(2,1)S(1)} %copy-done.2, ...), kind=kLoop, calls=%fused_computation.19 | loop fusion | flops 4980736 | bytes 3670016 | tf_op jit(solution)/shard_map/broadcast_in_dim | solution.py:170
  (38 shorter events, 1.4 us)
Async XLA Ops:
  0.6 36.6 %copy-start = (bf16[1024,512]{1,0:T(8,128)(2,1)S(1)}, bf16[1024,512]{1,0:T(8,128)(2,1)}, u32[]{:S(2)}) copy-start(bf16[1024,512]{1,0:T(8,128)(2,1)} %param.10) | copy-start | bytes 3145732
  0.6 1.3 %copy-start.2 = (bf16[1,512,512]{2,1,0:T(8,128)(2,1)S(1)}, bf16[1,512,512]{2,1,0:T(8,128)(2,1)}, u32[]{:S(2)}) copy-start(bf16[1,512,512]{2,1,0:T(8,128)(2,1)} %param.7) | copy-start | bytes 1572868
  3.1 15.5 %copy-start.5 = (bf16[128,512]{1,0:T(8,128)(2,1)S(1)}, bf16[128,512]{1,0:T(8,128)(2,1)}, u32[]{:S(2)}) copy-start(bf16[128,512]{1,0:T(8,128)(2,1)} %param.11) | copy-start | bytes 393220
  3.1 18.6 %copy-start.7 = (s32[96]{0:T(128)S(1)}, s32[96]{0:T(128)}, u32[]{:S(2)}) copy-start(s32[96]{0:T(128)} %param.9) | copy-start | bytes 1156
  3.1 41.4 %all-to-all-start = ((bf16[96,11,4,128]{3,2,1,0:T(4,128)(2,1)}), bf16[96,11,4,128]{3,2,1,0:T(4,128)(2,1)S(1)}, u32[]{:S(2)}, u32[]{:S(2)}) async-start(bf16[96,11,4,128]{3,2,1,0:T(4,128)(2,1)} %bitcast.8), calls=%async_computation | async-start | bytes 2162688 | tf_op jit(solution)/shard_map/all_to_all | solution.py:67
  18.6 4.0 %collective-permute-start = (bf16[128,512]{1,0:T(8,128)(2,1)S(1)}, bf16[128,512]{1,0:T(8,128)(2,1)S(1)}, u32[]{:S(2)}, u32[]{:S(2)}) collective-permute-start(bf16[128,512]{1,0:T(8,128)(2,1)S(1)} %copy-done.5), channel_id=1, source_target_pairs={{0,1},{1,0},{2,3},{3,2},{4,5},{5,4},{6,7},{7,6},{8,9},{9,8},{10,11... | collective-permute-start | bytes 393224 | tf_op jit(solution)/shard_map/ppermute | solution.py:111
  24.1 22.0 %collective-permute-start.1 = (bf16[256,512]{1,0:T(8,128)(2,1)S(1)}, bf16[256,512]{1,0:T(8,128)(2,1)S(1)}, u32[]{:S(2)}, u32[]{:S(2)}) collective-permute-start(bf16[256,512]{1,0:T(8,128)(2,1)S(1)} %pad_maximum_fusion), channel_id=1, source_target_pairs={{0,2},{1,7},{2,4},{3,1},{4,6},{5,3},{6,0},{7,5},{8,10},{9,15},{10,... | collective-permute-start | bytes 786440 | tf_op jit(solution)/shard_map/ppermute | solution.py:117
  46.1 46.5 %all-to-all-start.1 = ((bf16[96,11,4,128]{3,2,1,0:T(4,128)(2,1)}), bf16[96,11,4,128]{3,2,1,0:T(4,128)(2,1)S(1)}, u32[]{:S(2)}, u32[]{:S(2)}) async-start(bf16[96,11,4,128]{3,2,1,0:T(4,128)(2,1)} %shard_map.86), calls=%async_computation.1 | async-start | bytes 2162688 | tf_op jit(solution)/shard_map/all_to_all | solution.py:67
  63.4 26.4 %copy-start.6 = (bf16[1024,512]{1,0:T(8,128)(2,1)S(1)}, bf16[1024,512]{1,0:T(8,128)(2,1)}, u32[]{:S(2)}) copy-start(bf16[1024,512]{1,0:T(8,128)(2,1)} %get-tuple-element.13) | copy-start | bytes 3145732
  63.5 9.2 %collective-permute-start.2 = (bf16[128,512]{1,0:T(8,128)(2,1)S(1)}, bf16[128,512]{1,0:T(8,128)(2,1)S(1)}, u32[]{:S(2)}, u32[]{:S(2)}) collective-permute-start(bf16[128,512]{1,0:T(8,128)(2,1)S(1)} %slice_select_fusion), channel_id=1, source_target_pairs={{0,2},{1,7},{2,4},{3,1},{4,6},{5,3},{6,0},{7,5},{8,10},{9,15},{10,... | collective-permute-start | bytes 393224 | tf_op jit(solution)/shard_map/ppermute | solution.py:124
  72.7 17.1 %collective-permute-start.3 = (bf16[384,512]{1,0:T(8,128)(2,1)S(1)}, bf16[384,512]{1,0:T(8,128)(2,1)S(1)}, u32[]{:S(2)}, u32[]{:S(2)}) collective-permute-start(bf16[384,512]{1,0:T(8,128)(2,1)S(1)} %constant_dynamic-update-slice_fusion), channel_id=1, source_target_pairs={{0,1},{1,0},{2,3},{3,2},{4,5},{5,4},{6,7},{7,6},{8,9},{9,8},{10,11... | collective-permute-start | bytes 1179656 | tf_op jit(solution)/shard_map/ppermute | solution.py:111
  89.9 1.2 %copy-start.3 = (bf16[4,256,512]{2,1,0:T(8,128)(2,1)S(1)}, bf16[4,256,512]{2,1,0:T(8,128)(2,1)}, u32[]{:S(2)}) copy-start(bf16[4,256,512]{2,1,0:T(8,128)(2,1)} %gather_fusion) | copy-start | bytes 3145732
  93.4 1.0 %copy-start.1 = (bf16[1,512,512]{2,1,0:T(8,128)(2,1)S(1)}, bf16[1,512,512]{2,1,0:T(8,128)(2,1)}, u32[]{:S(2)}) copy-start(bf16[1,512,512]{2,1,0:T(8,128)(2,1)} %param.6) | copy-start | bytes 1572868
  93.4 1.2 %copy-start.4 = (bf16[1,512,512]{2,1,0:T(8,128)(2,1)S(1)}, bf16[1,512,512]{2,1,0:T(8,128)(2,1)}, u32[]{:S(2)}) copy-start(bf16[1,512,512]{2,1,0:T(8,128)(2,1)} %param.8) | copy-start | bytes 1572868

commit v11 on v10

--- a/solution.py
+++ b/solution.py
@@ -122,9 +122,9 @@
     chips = lax.axis_size("fsdp") // CORES
     own_core = by_core(near[: tokens // CORES], near[tokens // CORES :])[0]
     far = lax.ppermute(own_core, "fsdp", core_pairs(chips, (1, chips - 1)))
-    fetched = jnp.concatenate([near, far], axis=0)
-    even, odd = by_core(fetched, swap_cores(fetched))
-    return jnp.concatenate([chip, even[:tokens], even[tokens:], odd[tokens:], odd[:tokens]])
+    before, after = by_core(near, swap_cores(near))
+    far_even, far_odd = by_core(far, swap_cores(far))
+    return jnp.concatenate([chip, before, far_even, far_odd, after])
 
 
 def in_arrival_order(activations):

time: 96.7 us -> 98.4 us (1.018)
  other arithmetic: 3.19 us -> 5.93 us
  waiting for transfers between devices: 11.3 us -> 9.95 us
  matrix products: 1.53 us -> 2.75 us
  local copies, waits for them, and re-layouts: 6.92 us -> 5.82 us
    unnamed x2 -> x5, other arithmetic: 1.38 us -> 3.49 us
    ppermute x2 -> x3, starting transfers between devices: 18.8 us -> 20.2 us  [swap_cores(): lax.ppermute(array, 'fsdp', [(i, i ^ 1) for i in range(lax.axis_size('fsd...]
    dot_general x1, matrix products: 1.53 us -> 2.75 us  [on_device(): lax.dot_general(activations, gathered, contract, preferred_element_type=j...]
    ppermute x1, starting transfers between devices: 5.83 us -> 4.65 us  [all_shards(): far = lax.ppermute(own_core, 'fsdp', core_pairs(chips, (1, chips - 1)))]
    ppermute x2 -> x3, waiting for transfers between devices: 2.21 us -> 1.06 us  [swap_cores(): lax.ppermute(array, 'fsdp', [(i, i ^ 1) for i in range(lax.axis_size('fsd...]
    unnamed x18 -> x14, local copies, waits for them, and re-layouts: 2.13 us -> 1.06 us
  transfers between devices with their start and end apart: 6 -> 7, of which waited for: 4 -> 4; matrix products, arithmetic and copies ran while one was open for 6% -> 10% of each run, Pallas kernels for 2% -> 2%
where the time goes in v11:
time: 98.4 us; the launch traced here: 97.9 us
  starting transfers between devices  70 us (71%)
  waiting for transfers between devices  9.95 us (10%)
  other arithmetic  5.93 us (6%)
  local copies, waits for them, and re-layouts  5.82 us (6%)
  matrix products  2.75 us (3%)
  Pallas kernels  2.6 us (3%)
    all_to_all x2, starting transfers between devices, exchange(): lax.all_to_all(pieces, RANKS, split_axis=0, concat_axis=0, tiled=True)  32.8 us
    ppermute x3, starting transfers between devices, swap_cores(): lax.ppermute(array, 'fsdp', [(i, i ^ 1) for i in range(lax.axis_size('fsd...  20.2 us
    ppermute x1, starting transfers between devices, near_shards(): return (chip, lax.ppermute(chip, 'fsdp', core_pairs(chips, (1, chips - 1))))  12.3 us
    all_to_all x2, waiting for transfers between devices, exchange(): lax.all_to_all(pieces, RANKS, split_axis=0, concat_axis=0, tiled=True)  5.68 us
    ppermute x1, starting transfers between devices, all_shards(): far = lax.ppermute(own_core, 'fsdp', core_pairs(chips, (1, chips - 1)))  4.65 us
    unnamed x5, other arithmetic  3.49 us
    ppermute x1, waiting for transfers between devices, all_shards(): far = lax.ppermute(own_core, 'fsdp', core_pairs(chips, (1, chips - 1)))  3.2 us
    dot_general x1, matrix products, on_device(): lax.dot_general(activations, gathered, contract, preferred_element_type=j...  2.75 us
  transfers between devices with their start and end apart: 7, of which 4 were waited for; matrix products, arithmetic and copies ran while one was open for 10% of the time, Pallas kernels for 2%

profile of v11, /device:TPU:1, one launch (start us, length us, event | category | flops | bytes accessed | tf_op | source)
XLA Modules:
  0.0 97.9 jit_solution(4937539224835244468)
XLA Ops:
  0.7 1.3 %reshape_squeeze.6.first_ref = bf16[128,4,512]{2,1,0:T(4,128)(2,1)S(1)} reshape(bf16[1,512,512]{2,1,0:T(8,128)(2,1)} %param.6) | data formatting | bytes 1048576 | tf_op jit(solution)/shard_map/reshape;squeeze | solution.py:49
  2.1 1.0 %shard_map.85 = bf16[264,4,512]{2,1,0:T(4,128)(2,1)} custom-call(bf16[128,4,512]{2,1,0:T(4,128)(2,1)S(1)} %reshape_squeeze.6.first_ref, bf16[128,4,512]{2,1,0:T(4,128)(2,1)S(1)} %reshape_squeeze.7.second_ref), custom_call_target="tpu_custom_call" | custom-call | tf_op jit(solution)/shard_map/pallas_call | solution.py:37
  3.2 15.5 %all-to-all-start = ((bf16[96,11,4,128]{3,2,1,0:T(4,128)(2,1)}), bf16[96,11,4,128]{3,2,1,0:T(4,128)(2,1)S(1)}, u32[]{:S(2)}, u32[]{:S(2)}) async-start(bf16[96,11,4,128]{3,2,1,0:T(4,128)(2,1)} %bitcast.8), calls=%async_computation | async-start | bytes 2162688 | tf_op jit(solution)/shard_map/all_to_all | solution.py:67
  18.7 3.0 %collective-permute-start = (bf16[128,512]{1,0:T(8,128)(2,1)S(1)}, bf16[128,512]{1,0:T(8,128)(2,1)S(1)}, u32[]{:S(2)}, u32[]{:S(2)}) collective-permute-start(bf16[128,512]{1,0:T(8,128)(2,1)S(1)} %copy-done.5), channel_id=1, source_target_pairs={{0,1},{1,0},{2,3},{3,2},{4,5},{5,4},{6,7},{7,6},{8,9},{9,8},{10,11... | collective-permute-start | bytes 393224 | tf_op jit(solution)/shard_map/ppermute | solution.py:111
  21.8 0.9 collective-permute-done
  22.7 0.7 constant_dynamic-update-slice_fusion.1
  23.4 0.7 constant_dynamic-update-slice_fusion
  24.1 12.3 %collective-permute-start.1 = (bf16[256,512]{1,0:T(8,128)(2,1)S(1)}, bf16[256,512]{1,0:T(8,128)(2,1)S(1)}, u32[]{:S(2)}, u32[]{:S(2)}) collective-permute-start(bf16[256,512]{1,0:T(8,128)(2,1)S(1)} %pad_maximum_fusion), channel_id=1, source_target_pairs={{0,2},{1,7},{2,4},{3,1},{4,6},{5,3},{6,0},{7,5},{8,10},{9,15},{10,... | collective-permute-start | bytes 786440 | tf_op jit(solution)/shard_map/ppermute | solution.py:117
  37.2 1.6 %gather_fusion = bf16[4,256,512]{2,1,0:T(8,128)(2,1)} fusion(bf16[4,256,512]{2,1,0:T(8,128)(2,1)S(1)} %bitcast.57, s32[1024]{0:T(1024)S(1)} %pad_clamp_fusion), kind=kCustom, calls=%fused_computation | custom fusion | bytes 2097168 | tf_op jit(solution)/shard_map/gather | solution.py:135
  38.8 5.7 %all-to-all-done.pieces_ref = bf16[96,11,4,128]{3,2,1,0:T(4,128)(2,1)S(1)} async-done(((bf16[96,11,4,128]{3,2,1,0:T(4,128)(2,1)}), bf16[96,11,4,128]{3,2,1,0:T(4,128)(2,1)S(1)}, u32[]{:S(2)}, u32[]{:S(2)}) %all-to-all-start) | async-done | bytes 1081376 | tf_op jit(solution)/shard_map/all_to_all | solution.py:67
  44.5 1.6 %shard_map.86 = bf16[96,11,4,128]{3,2,1,0:T(4,128)(2,1)} custom-call(s32[96]{0:T(128)S(1)} %fusion.9.partner_ref, bf16[96,11,4,128]{3,2,1,0:T(4,128)(2,1)S(1)} %all-to-all-done.pieces_ref), custom_call_target="tpu_custom_call" | custom-call | bytes 2162688 | tf_op jit(solution)/shard_map/pallas_call | solution.py:81
  46.1 17.3 %all-to-all-start.1 = ((bf16[96,11,4,128]{3,2,1,0:T(4,128)(2,1)}), bf16[96,11,4,128]{3,2,1,0:T(4,128)(2,1)S(1)}, u32[]{:S(2)}, u32[]{:S(2)}) async-start(bf16[96,11,4,128]{3,2,1,0:T(4,128)(2,1)} %shard_map.86), calls=%async_computation.1 | async-start | bytes 2162688 | tf_op jit(solution)/shard_map/all_to_all | solution.py:67
  63.4 4.1 %collective-permute-start.2 = (bf16[256,512]{1,0:T(8,128)(2,1)S(1)}, bf16[256,512]{1,0:T(8,128)(2,1)S(1)}, u32[]{:S(2)}, u32[]{:S(2)}) collective-permute-start(bf16[256,512]{1,0:T(8,128)(2,1)S(1)} %collective-permute-done.1), channel_id=1, source_target_pairs={{0,1},{1,0},{2,3},{3,2},{4,5},{5,4},{6,7},{7,6},{8,9},{9,8},{10,11... | collective-permute-start | bytes 786440 | tf_op jit(solution)/shard_map/ppermute | solution.py:111
  67.6 4.6 %collective-permute-start.3 = (bf16[128,512]{1,0:T(8,128)(2,1)S(1)}, bf16[128,512]{1,0:T(8,128)(2,1)S(1)}, u32[]{:S(2)}, u32[]{:S(2)}) collective-permute-start(bf16[128,512]{1,0:T(8,128)(2,1)S(1)} %slice_select_fusion), channel_id=1, source_target_pairs={{0,2},{1,7},{2,4},{3,1},{4,6},{5,3},{6,0},{7,5},{8,10},{9,15},{10,... | collective-permute-start | bytes 393224 | tf_op jit(solution)/shard_map/ppermute | solution.py:124
  72.2 3.2 %collective-permute-done.3 = bf16[128,512]{1,0:T(8,128)(2,1)S(1)} collective-permute-done((bf16[128,512]{1,0:T(8,128)(2,1)S(1)}, bf16[128,512]{1,0:T(8,128)(2,1)S(1)}, u32[]{:S(2)}, u32[]{:S(2)}) %collective-permute-start.3) | collective-permute-done | bytes 131104 | tf_op jit(solution)/shard_map/ppermute | solution.py:124
  75.4 13.0 %collective-permute-start.4 = (bf16[128,512]{1,0:T(8,128)(2,1)S(1)}, bf16[128,512]{1,0:T(8,128)(2,1)S(1)}, u32[]{:S(2)}, u32[]{:S(2)}) collective-permute-start(bf16[128,512]{1,0:T(8,128)(2,1)S(1)} %collective-permute-done.3), channel_id=1, source_target_pairs={{0,1},{1,0},{2,3},{3,2},{4,5},{5,4},{6,7},{7,6},{8,9},{9,8},{10,11... | collective-permute-start | bytes 393224 | tf_op jit(solution)/shard_map/ppermute | solution.py:111
  88.5 0.8 select_dynamic-update-slice_fusion.1
  89.5 0.7 select_dynamic-update-slice_fusion.3
  90.1 0.7 select_dynamic-update-slice_fusion.2
  90.8 0.8 select_dynamic-update-slice_fusion
  91.6 2.8 %fusion = bf16[1,512,512]{2,1,0:T(8,128)(2,1)} fusion(bf16[1024,512]{1,0:T(8,128)(2,1)S(1)} %bitcast.61, bf16[1024,512]{1,0:T(8,128)(2,1)} %select_dynamic-update-slice_fusion), kind=kOutput, calls=%fused_computation.5 | convolution fusion | flops 537133056 | bytes 2621440 | tf_op jit(solution)/shard_map/dot_general | solution.py:168
  94.3 0.4 slice_bitcast_fusion
  95.3 0.9 copy-done.1
  96.3 1.6 %convert_bitcast_fusion = (bf16[1,512,512]{2,1,0:T(8,128)(2,1)}, bf16[1,512,512]{2,1,0:T(8,128)(2,1)}) fusion(bf16[512,512]{1,0:T(8,128)(2,1)S(1)} %get-tuple-element.10, bf16[1,512,512]{2,1,0:T(8,128)(2,1)S(1)} %copy-done.1, bf16[512,512]{1,0:T(8,128)(2,1)S(1)} %get-tuple-element.9, bf16[1,512,512]{2,1,0:T(8,128)(2,1)S(1)} %copy-done.2, ...), kind=kLoop, calls=%fused_computation.19 | loop fusion | flops 4980736 | bytes 3670016 | tf_op jit(solution)/shard_map/broadcast_in_dim | solution.py:170
  (37 shorter events, 2.0 us)
Async XLA Ops:
  0.6 36.6 %copy-start = (bf16[1024,512]{1,0:T(8,128)(2,1)S(1)}, bf16[1024,512]{1,0:T(8,128)(2,1)}, u32[]{:S(2)}) copy-start(bf16[1024,512]{1,0:T(8,128)(2,1)} %param.10) | copy-start | bytes 3145732
  0.6 1.3 %copy-start.2 = (bf16[1,512,512]{2,1,0:T(8,128)(2,1)S(1)}, bf16[1,512,512]{2,1,0:T(8,128)(2,1)}, u32[]{:S(2)}) copy-start(bf16[1,512,512]{2,1,0:T(8,128)(2,1)} %param.7) | copy-start | bytes 1572868
  3.1 15.5 %copy-start.5 = (bf16[128,512]{1,0:T(8,128)(2,1)S(1)}, bf16[128,512]{1,0:T(8,128)(2,1)}, u32[]{:S(2)}) copy-start(bf16[128,512]{1,0:T(8,128)(2,1)} %param.11) | copy-start | bytes 393220
  3.1 18.6 %copy-start.6 = (s32[96]{0:T(128)S(1)}, s32[96]{0:T(128)}, u32[]{:S(2)}) copy-start(s32[96]{0:T(128)} %param.9) | copy-start | bytes 1156
  3.2 41.4 %all-to-all-start = ((bf16[96,11,4,128]{3,2,1,0:T(4,128)(2,1)}), bf16[96,11,4,128]{3,2,1,0:T(4,128)(2,1)S(1)}, u32[]{:S(2)}, u32[]{:S(2)}) async-start(bf16[96,11,4,128]{3,2,1,0:T(4,128)(2,1)} %bitcast.8), calls=%async_computation | async-start | bytes 2162688 | tf_op jit(solution)/shard_map/all_to_all | solution.py:67
  18.7 4.0 %collective-permute-start = (bf16[128,512]{1,0:T(8,128)(2,1)S(1)}, bf16[128,512]{1,0:T(8,128)(2,1)S(1)}, u32[]{:S(2)}, u32[]{:S(2)}) collective-permute-start(bf16[128,512]{1,0:T(8,128)(2,1)S(1)} %copy-done.5), channel_id=1, source_target_pairs={{0,1},{1,0},{2,3},{3,2},{4,5},{5,4},{6,7},{7,6},{8,9},{9,8},{10,11... | collective-permute-start | bytes 393224 | tf_op jit(solution)/shard_map/ppermute | solution.py:111
  24.1 22.0 %collective-permute-start.1 = (bf16[256,512]{1,0:T(8,128)(2,1)S(1)}, bf16[256,512]{1,0:T(8,128)(2,1)S(1)}, u32[]{:S(2)}, u32[]{:S(2)}) collective-permute-start(bf16[256,512]{1,0:T(8,128)(2,1)S(1)} %pad_maximum_fusion), channel_id=1, source_target_pairs={{0,2},{1,7},{2,4},{3,1},{4,6},{5,3},{6,0},{7,5},{8,10},{9,15},{10,... | collective-permute-start | bytes 786440 | tf_op jit(solution)/shard_map/ppermute | solution.py:117
  46.1 48.2 %all-to-all-start.1 = ((bf16[96,11,4,128]{3,2,1,0:T(4,128)(2,1)}), bf16[96,11,4,128]{3,2,1,0:T(4,128)(2,1)S(1)}, u32[]{:S(2)}, u32[]{:S(2)}) async-start(bf16[96,11,4,128]{3,2,1,0:T(4,128)(2,1)} %shard_map.86), calls=%async_computation.1 | async-start | bytes 2162688 | tf_op jit(solution)/shard_map/all_to_all | solution.py:67
  63.4 25.1 %collective-permute-start.2 = (bf16[256,512]{1,0:T(8,128)(2,1)S(1)}, bf16[256,512]{1,0:T(8,128)(2,1)S(1)}, u32[]{:S(2)}, u32[]{:S(2)}) collective-permute-start(bf16[256,512]{1,0:T(8,128)(2,1)S(1)} %collective-permute-done.1), channel_id=1, source_target_pairs={{0,1},{1,0},{2,3},{3,2},{4,5},{5,4},{6,7},{7,6},{8,9},{9,8},{10,11... | collective-permute-start | bytes 786440 | tf_op jit(solution)/shard_map/ppermute | solution.py:111
  67.6 7.9 %collective-permute-start.3 = (bf16[128,512]{1,0:T(8,128)(2,1)S(1)}, bf16[128,512]{1,0:T(8,128)(2,1)S(1)}, u32[]{:S(2)}, u32[]{:S(2)}) collective-permute-start(bf16[128,512]{1,0:T(8,128)(2,1)S(1)} %slice_select_fusion), channel_id=1, source_target_pairs={{0,2},{1,7},{2,4},{3,1},{4,6},{5,3},{6,0},{7,5},{8,10},{9,15},{10,... | collective-permute-start | bytes 393224 | tf_op jit(solution)/shard_map/ppermute | solution.py:124
  75.4 14.0 %collective-permute-start.4 = (bf16[128,512]{1,0:T(8,128)(2,1)S(1)}, bf16[128,512]{1,0:T(8,128)(2,1)S(1)}, u32[]{:S(2)}, u32[]{:S(2)}) collective-permute-start(bf16[128,512]{1,0:T(8,128)(2,1)S(1)} %collective-permute-done.3), channel_id=1, source_target_pairs={{0,1},{1,0},{2,3},{3,2},{4,5},{5,4},{6,7},{7,6},{8,9},{9,8},{10,11... | collective-permute-start | bytes 393224 | tf_op jit(solution)/shard_map/ppermute | solution.py:111
  88.5 3.1 %copy-start.3 = (bf16[4,256,512]{2,1,0:T(8,128)(2,1)S(1)}, bf16[4,256,512]{2,1,0:T(8,128)(2,1)}, u32[]{:S(2)}) copy-start(bf16[4,256,512]{2,1,0:T(8,128)(2,1)} %gather_fusion) | copy-start | bytes 3145732
  95.1 1.0 %copy-start.1 = (bf16[1,512,512]{2,1,0:T(8,128)(2,1)S(1)}, bf16[1,512,512]{2,1,0:T(8,128)(2,1)}, u32[]{:S(2)}) copy-start(bf16[1,512,512]{2,1,0:T(8,128)(2,1)} %param.6) | copy-start | bytes 1572868
  95.2 1.2 %copy-start.4 = (bf16[1,512,512]{2,1,0:T(8,128)(2,1)S(1)}, bf16[1,512,512]{2,1,0:T(8,128)(2,1)}, u32[]{:S(2)}) copy-start(bf16[1,512,512]{2,1,0:T(8,128)(2,1)} %param.8) | copy-start | bytes 1572868
